TPU v7x, 32 devices: a whole 2x2x4 slice. The times are simulated.
32 devices in a mesh: leaf: 8 (over z, y), help: 4 (over x, core).
Axes of the slice: x: 2, y: 2, z: 4, core: 2. Of those that a mesh axis runs over, the one named last changes fastest.
Arguments:
- points: float32 [64, 32768], P(None, ('leaf', 'help')), may hold values from -3 to 3
- weights: float32 [256, 32768], P(None, ('leaf', 'help')), may hold values from -0.12 to 0.12
- interp: float32 [64, 512, 256], P(('leaf', 'help')), may hold values from -0.25 to 0.25
- transfer: float32 [6, 512, 256], replicated, may hold values from -0.25 to 0.25
- near_count: int32 [8, 8], P('leaf', 'help'), may hold values from 1 to 32, 128 in all within a row
- near_src: int32 [64, 32], P(('leaf', 'help')), may hold values from 0 to 63, as said below
- skel_group: int32 [8, 256], P('leaf'), may hold values from 0 to 4095, as said below
- skel_node: int32 [6, 256], replicated, may hold values from 0 to 511, as said below
- far_nodes: int32 [14, 4], replicated, may hold values from 0 to 7, as said below
Outputs:
- product: float32 [256, 32768], P(None, ('leaf', 'help'))
Inputs may be any that keep to these rules, and one draw needn't show every extreme that they name: `near_src`: slot 0 of leaf i names leaf i itself; every source of a leaf of subtree g is a leaf of subtree g - 1, g or g + 1. Slots at or after the leaf's near_count are not used. `near_count`: the 8 counts of one subtree sum to exactly 128. `skel_group`: each row holds 256 distinct indices into its subtree's points, counted from the subtree's first point. `skel_node`: each row holds 256 distinct indices into its two children's skeleton points, the first child's first. `far_nodes`: rows 0 to 7 are the level-0 nodes, the next 4 rows the level-1 nodes, and so on down to the 2 nodes of the highest listed level; each entry is a node number of that row's level. On level 0, the first entry of node k's row is k - 1 (modulo 8) and no other entry is k, k + 1 or k - 1 (modulo 8); on a higher level of c >= 4 nodes, no entry of node k's row is k, k + 1 or k - 1 (modulo c); on the level of 2 nodes, every entry is the other node.
All inputs are finite; a program needn't handle non-finite values. No bound on the sum of `near_count` on one device may be relied on, other than what follows from the above.
Results may differ from a plain program's by a relative error of at most 0.0003.
Values sent between devices are 32-bit elements; how exact they have to be, the bound alone decides.
No kernel may reach another device: no remote copies, remote signals or barrier semaphores. Data moves between devices by JAX's collectives and lax.ppermute only.
A program may use at most 192 MiB of HBM per device.

v0:
```python
from functools import partial

import jax
import jax.numpy as jnp
from jax import lax
from jax.sharding import PartitionSpec as P

F = 64
R = 256
LEAF = 512
SK = 256
NEAR = 32


HIGH = lax.Precision.HIGHEST


def padded(cells, sides, width):
    for axis, dim in sides:
        count = lax.axis_size(axis)
        ends = count - 1
        head = lax.slice_in_dim(cells, 0, width, axis=dim)
        tail = lax.slice_in_dim(cells, cells.shape[dim] - width, cells.shape[dim], axis=dim)
        cells = jnp.concatenate(
            [
                lax.ppermute(tail, axis, [(i, (i + 1) % count) for i in range(ends)]),
                cells,
                lax.ppermute(head, axis, [((i + 1) % count, i) for i in range(ends)]),
            ],
            axis=dim,
        )
    return cells


def from_behind(array, axis, by):
    length = lax.axis_size(axis)
    pairs = [(i, i + by) for i in range(length) if 0 <= i + by < length]
    return lax.ppermute(array, axis, pairs)


def kernel_block(source, target):
    cross = lax.dot_general(
        source, target, (((0,), (0,)), ((), ())), precision=HIGH, preferred_element_type=jnp.float32
    )
    source_sq = jnp.sum(source * source, axis=0)
    target_sq = jnp.sum(target * target, axis=0)
    dist = source_sq[:, None] + target_sq[None, :] - 2.0 * cross
    return jnp.exp((0.5 * F - dist) * 0.25)


def apply_block(source_pts, source_vals, target_pts):
    return jnp.dot(
        source_vals,
        kernel_block(source_pts, target_pts),
        precision=HIGH,
        preferred_element_type=jnp.float32,
    )


def skeleton_term(source, target):
    return apply_block(source[:F], source[F:], target[:F])


def upper_start(level, groups):
    return sum((groups >> step for step in range(1, level)))


def list_start(level, groups):
    return sum((groups >> step for step in range(level)))


def combine(left, right, picks, matrix):
    both_pts = jnp.concatenate([left[:F], right[:F]], axis=1)
    both_vals = jnp.concatenate([left[F:], right[F:]], axis=1)
    chosen = jnp.take(both_pts, picks, axis=1)
    merged = jnp.dot(both_vals, matrix, precision=HIGH, preferred_element_type=jnp.float32)
    return jnp.concatenate([chosen, merged], axis=0)


def add_scaled(value, factor, source, target):
    return value + factor * skeleton_term(source, target)


def keep_scaled(value, factor, source, target):
    return value


def fold_sources(level, helper, helpers, ids, target, total, piece, start):

    def one(index, acc):
        node = index >> level
        aligned = index % (1 << level) == 0
        assigned = node % helpers == helper
        hits = jnp.sum((ids == node).astype(jnp.float32)) * (aligned & assigned).astype(jnp.float32)
        source = lax.dynamic_index_in_dim(piece, index, 0, keepdims=False)
        return lax.cond(hits > 0.0, add_scaled, keep_scaled, acc, hits, source, target)

    return lax.fori_loop(0, piece.shape[0], one, total)


def shards(
    points, weights, interp, transfer, near_count, near_src, skel_group, skel_node, far_nodes
):
    helpers = lax.axis_size("help")
    groups = lax.axis_size("leaf")
    levels = groups.bit_length() - 1
    helper = lax.axis_index("help")
    group = lax.axis_index("leaf")
    own_leaves = interp.shape[0]
    own_cols = points.shape[1]
    cloud = jnp.concatenate([points, weights], axis=0)
    group_cloud = lax.all_gather(cloud, "help", axis=1, tiled=True)
    group_leaves = group_cloud.shape[1] // LEAF
    beside_all = padded(group_cloud, (("leaf", 1),), group_cloud.shape[1])
    leaf_vals = weights.reshape(R, own_leaves, LEAF)
    own_up = jnp.einsum("rjl,jls->rs", leaf_vals, interp, precision=HIGH)
    group_up = lax.psum(own_up, "help")
    group_pts = group_cloud[:F]
    group_skel = jnp.take(group_pts, skel_group[0], axis=1)
    payload = jnp.concatenate([group_skel, group_up], axis=0)
    empty = jnp.zeros((R, SK), jnp.float32)
    far_parts = []
    tiers = [payload]
    for level in range(1, levels):
        right = from_behind(tiers[-1], "leaf", -(1 << level - 1))
        row = upper_start(level, groups) + (group >> level)
        tiers.append(combine(tiers[-1], right, skel_node[row], transfer[row]))
    for level in range(levels):
        ids = far_nodes[list_start(level, groups) + (group >> level)]
        folder = partial(fold_sources, level, helper, helpers, ids, tiers[level])
        far_parts.append(
            folder(
                empty, lax.all_gather(tiers[level][None], "leaf", axis=0, tiled=True), jnp.int32(0)
            )
        )
    far_sums = lax.psum(tuple(far_parts), "help")
    local = far_sums[levels - 1]
    for level in range(levels - 1, 0, -1):
        row = upper_start(level, groups) + (group >> level)
        pushed = lax.dot_general(
            local,
            transfer[row],
            (((1,), (1,)), ((), ())),
            precision=HIGH,
            preferred_element_type=jnp.float32,
        )
        sent = from_behind(pushed[:, SK:], "leaf", 1 << level - 1)
        parent_side = group % (1 << level) == 0
        local = far_sums[level - 1] + jnp.where(parent_side, pushed[:, :SK], sent)
    far_out = jnp.einsum("rs,jls->rjl", local, interp, precision=HIGH).reshape(R, own_cols)
    base = (group - 1) * group_leaves
    counts = near_count[0]

    def own_tile(slot, total):
        leaf = slot // NEAR
        index = slot % NEAR
        column = (near_src[leaf, index] - base) * LEAF
        source = lax.dynamic_slice_in_dim(beside_all, column, LEAF, 1)
        target = lax.dynamic_slice_in_dim(points, leaf * LEAF, LEAF, 1)

        def add_tile(value):
            current = lax.dynamic_slice_in_dim(value, leaf * LEAF, LEAF, 1)
            return lax.dynamic_update_slice_in_dim(
                value, current + apply_block(source[:F], source[F:], target), leaf * LEAF, 1
            )

        return lax.cond(index < counts[leaf], add_tile, lambda value: value, total)

    near_out = lax.fori_loop(0, own_leaves * NEAR, own_tile, jnp.zeros((R, own_cols), jnp.float32))
    return far_out + near_out


def solution(mesh):
    placed = (
        P(None, ("leaf", "help")),
        P(None, ("leaf", "help")),
        P(("leaf", "help"), None, None),
        P(),
        P("leaf", "help"),
        P(("leaf", "help"), None),
        P("leaf", None),
        P(),
        P(),
    )
    return jax.shard_map(
        shards, mesh=mesh, in_specs=placed, out_specs=P(None, ("leaf", "help")), check_vma=False
    )
```

profile of v0, /device:TPU:3, one launch (start us, length us, event | category | flops | bytes accessed | tf_op | source)
XLA Modules:
  0.0 993.8 jit_solution(16538078931142091382)
XLA Ops:
  17.7 43.6 %all-gather.8.cloned.1.call-done = f32[320,4096]{0,1:T(8,128)} async-done(((f32[320,1024]{0,1:T(8,128)}), f32[320,4096]{0,1:T(8,128)}) %all-gather.8.cloned.1.call-update) | async-done | bytes 5242896 | tf_op jit(solution)/shard_map/all_gather | solution.py:112
  66.7 27.9 %all-reduce.4.cloned.1.call-done = f32[256,256]{1,0:T(8,128)} async-done(((f32[256,256]{1,0:T(8,128)}), f32[256,256]{1,0:T(8,128)}) %all-reduce.4.cloned.1.call-update) | async-done | bytes 262160 | tf_op jit(solution)/shard_map/psum | solution.py:117
  98.5 9.0 collective-permute-done
  118.4 8.5 collective-permute-done.1
  152.2 19.2 %while.73 = (s32[]{:T(128)}, f32[256,256]{1,0:T(8,128)S(1)}, s32[]{:T(128)}, s32[4]{0:T(128)S(1)}, f32[8,320,256]{2,1,0:T(8,128)}, /*index=5*/f32[64,256]{1,0:T(...) while((s32[]{:T(128)}, f32[256,256]{1,0:T(8,128)S(1)}, s32[]{:T(128)}, ...), condition=%wide.region_7.8_spmd, body=%wide.region_1.7_spmd.sunk | while | flops 252182048 | bytes 1578854 | solution.py:98
  171.4 153.9 %all-gather.12.cloned.1.call-done = f32[2560,256]{1,0:T(8,128)} async-done(((f32[320,256]{1,0:T(8,128)}), f32[2560,256]{1,0:T(8,128)}) %all-gather.12.cloned.1.call-update) | async-done | bytes 2621456 | tf_op jit(solution)/shard_map/all_gather | solution.py:133
  326.1 9.9 while.74
  336.0 62.2 %all-gather.14.cloned.1.call-done = f32[2560,256]{1,0:T(8,128)} async-done(((f32[320,256]{1,0:T(8,128)}), f32[2560,256]{1,0:T(8,128)}) %all-gather.14.cloned.1.call-update) | async-done | bytes 2621456 | tf_op jit(solution)/shard_map/all_gather | solution.py:133
  398.2 10.6 %while.75 = (s32[]{:T(128)}, f32[256,256]{1,0:T(8,128)S(1)}, s32[]{:T(128)}, s32[4]{0:T(128)S(1)}, f32[8,320,256]{2,1,0:T(8,128)}, /*index=5*/f32[64,256]{1,0:T(...) while((s32[]{:T(128)}, f32[256,256]{1,0:T(8,128)S(1)}, ...), condition=%wide.region_23.25_spmd, body=%wide.region_17.24_spmd.sunk | while | flops 252182048 | bytes 1577950 | solution.py:98
  409.6 36.4 %all-reduce.6.cloned.1.call-done = (f32[256,256]{1,0:T(8,128)}, f32[256,256]{1,0:T(8,128)}, f32[256,256]{1,0:T(8,128)}) async-done(((f32[256,256]{1,0:T(8,128)}, f32[256,256]{1,0:T(8,128)}, f32[256,256]{1,0:T(8,128)}), (f32[256,256]{1,0:T(8,128)}, f32[256,256]{1,0:T(8,128)}, f32[256,256]{1,0:T(8,128)})) %all-reduce.6.cloned.1.call-update) | async-done | bytes 786448 | tf_op jit(solution)/shard_map/psum | solution.py:136
  471.4 17.9 %pad_maximum_fusion = f32[320,12288]{0,1:T(8,128)} fusion(f32[320,4096]{0,1:T(8,128)} %copy.43, f32[320,4096]{0,1:T(8,128)} %all-gather.8.cloned.1.call-done, f32[320,4096]{0,1:T(8,128)} %copy.42), kind=kLoop, calls=%fused_computation.61 | loop fusion | flops 7864320 | bytes 31457280 | tf_op jit(solution)/shard_map/concatenate | solution.py:24
  489.3 17.5 %copy.44 = f32[320,12288]{1,0:T(8,128)} copy(f32[320,12288]{0,1:T(8,128)} %pad_maximum_fusion) | data formatting | bytes 31457280 | tf_op jit(solution)/shard_map/while | solution.py:169
  507.0 471.8 %while.76 = (s32[]{:T(128)}, f32[256,1024]{1,0:T(8,128)S(1)}, s32[2]{0:T(128)S(1)}, s32[2,32]{1,0:T(2,128)S(1)}, s32[]{:T(128)}, /*index=5*/f32[320,12288]{1,0:T...) while((s32[]{:T(128)}, f32[256,1024]{1,0:T(8,128)S(1)}, ...), condition=%wide.region_30.32_spmd, body=%wide.region_25.31_spmd.sunk | while | flops 1008204800 | bytes 4203066 | solution.py:169
  532.0 6.5 conditional.11
  547.8 6.5 conditional.11
  571.4 6.5 conditional.11
  602.9 6.5 conditional.11
  626.6 6.5 conditional.11
  642.3 6.5 conditional.11
  673.8 6.5 conditional.11
  697.4 6.5 conditional.11
  713.2 6.5 conditional.11
  736.8 6.5 conditional.11
  744.7 6.5 conditional.11
  (521 shorter events, 819.8 us)
Async XLA Ops:
  6.5 107.3 %copy-start = (f32[6,512,256]{2,1,0:T(8,128)S(1)}, f32[6,512,256]{2,1,0:T(8,128)}, u32[]{:S(2)}) copy-start(f32[6,512,256]{2,1,0:T(8,128)} %param.30) | copy-start | bytes 9437188
  6.5 54.7 %all-gather.8.cloned.1.call-start = ((), (), s32[]{:S(2)}) async-start(), calls=%async_computation | async-start | bytes 7864320 | tf_op jit(solution)/shard_map/all_gather | solution.py:112
  11.2 6.4 copy-start.17
  14.2 80.4 %all-reduce.4.cloned.1.call-start = ((), (), s32[]{:S(2)}) async-start(), calls=%async_computation.1 | async-start | bytes 524288 | tf_op jit(solution)/shard_map/psum | solution.py:117
  17.6 134.6 %all-gather.10.cloned.1.call-start = ((), (), s32[]{:S(2)}) async-start(), calls=%async_computation.2 | async-start | bytes 2949120 | tf_op jit(solution)/shard_map/all_gather | solution.py:133
  96.3 229.0 %all-gather.12.cloned.1.call-start = ((), (), s32[]{:S(2)}) async-start(), calls=%async_computation.3 | async-start | bytes 2949120 | tf_op jit(solution)/shard_map/all_gather | solution.py:133
  97.2 10.3 %collective-permute-start = (f32[320,256]{1,0:T(8,128)}, f32[320,256]{1,0:T(8,128)S(1)}, u32[]{:S(2)}, u32[]{:S(2)}) collective-permute-start(f32[320,256]{1,0:T(8,128)} %pad_maximum_fusion.2), channel_id=1, source_target_pairs={{4,0},{8,4},{12,8},{16,12},{20,16},{24,20},{28,24},{5,1},{9,5},{13... | collective-permute-start | bytes 983048 | tf_op jit(solution)/shard_map/ppermute | solution.py:38
  117.0 281.2 %all-gather.14.cloned.1.call-start = ((), (), s32[]{:S(2)}) async-start(), calls=%async_computation.4 | async-start | bytes 2949120 | tf_op jit(solution)/shard_map/all_gather | solution.py:133
  117.1 9.8 collective-permute-start.1
  137.7 12.7 %copy-start.15 = (s32[14,4]{0,1:T(4,128)S(1)}, s32[14,4]{0,1:T(4,128)}, u32[]{:S(2)}) copy-start(s32[14,4]{0,1:T(4,128)} %param.35) | copy-start | bytes 676
  137.7 308.3 %all-reduce.6.cloned.1.call-start = ((), (), s32[]{:S(2)}) async-start(), calls=%async_computation.5 | async-start | bytes 1572864 | tf_op jit(solution)/shard_map/psum | solution.py:136
  144.0 308.9 %collective-permute-start.4 = (f32[320,4096]{1,0:T(8,128)}, f32[320,4096]{1,0:T(8,128)}, u32[]{:S(2)}, u32[]{:S(2)}) collective-permute-start(f32[320,4096]{1,0:T(8,128)} %copy.40), channel_id=1, source_target_pairs={{0,4},{4,8},{8,12},{12,16},{16,20},{20,24},{24,28},{1,5},{5,9},{9,... | collective-permute-start | bytes 15728648 | tf_op jit(solution)/shard_map/ppermute | solution.py:26
  149.1 310.2 %collective-permute-start.5 = (f32[320,4096]{1,0:T(8,128)}, f32[320,4096]{1,0:T(8,128)}, u32[]{:S(2)}, u32[]{:S(2)}) collective-permute-start(f32[320,4096]{1,0:T(8,128)} %copy.40), channel_id=1, source_target_pairs={{4,0},{8,4},{12,8},{16,12},{20,16},{24,20},{28,24},{5,1},{9,5},{13... | collective-permute-start | bytes 15728648 | tf_op jit(solution)/shard_map/ppermute | solution.py:28
  171.4 154.6 %copy-start.2 = (f32[256,256]{1,0:T(8,128)}, f32[256,256]{1,0:T(8,128)S(1)}, u32[]{:S(2)}) copy-start(f32[256,256]{1,0:T(8,128)S(1)} %get-tuple-element.1017) | copy-start | bytes 786436
  326.1 72.1 %copy-start.7 = (f32[64,256]{1,0:T(8,128)S(1)}, f32[64,256]{1,0:T(8,128)}, u32[]{:S(2)}) copy-start(f32[64,256]{1,0:T(8,128)} %copy-done.6) | copy-start | bytes 196612
  449.1 16.5 %collective-permute-start.2 = (f32[256,256]{1,0:T(8,128)}, f32[256,256]{1,0:T(8,128)}, u32[]{:S(2)}, u32[]{:S(2)}) collective-permute-start(f32[256,256]{1,0:T(8,128)} %slice.114), channel_id=1, source_target_pairs={{0,8},{4,12},{8,16},{12,20},{16,24},{20,28},{1,9},{5,13},{9,17},{1... | collective-permute-start | bytes 786440 | tf_op jit(solution)/shard_map/ppermute | solution.py:38
  459.3 6.4 copy-start.14
  468.1 512.0 %collective-permute-start.3 = (f32[256,256]{1,0:T(8,128)S(1)}, f32[256,256]{1,0:T(8,128)S(1)}, u32[]{:S(2)}, u32[]{:S(2)}) collective-permute-start(f32[256,256]{1,0:T(8,128)S(1)} %slice.116), channel_id=1, source_target_pairs={{0,4},{4,8},{8,12},{12,16},{16,20},{20,24},{24,28},{1,5},{5,9},{9,... | collective-permute-start | bytes 786440 | tf_op jit(solution)/shard_map/ppermute | solution.py:38
  489.3 17.7 %copy-start.5 = (f32[64,1024]{1,0:T(8,128)S(1)}, f32[64,1024]{1,0:T(8,128)}, u32[]{:S(2)}) copy-start(f32[64,1024]{1,0:T(8,128)} %param.27) | copy-start | bytes 786436
  489.3 17.7 %copy-start.16 = (s32[2,32]{1,0:T(2,128)S(1)}, s32[2,32]{1,0:T(2,128)}, u32[]{:S(2)}) copy-start(s32[2,32]{1,0:T(2,128)} %param.32) | copy-start | bytes 772
  489.3 17.7 %copy-start.18 = (s32[1,2]{1,0:T(1,128)S(1)}, s32[1,2]{1,0:T(1,128)}, u32[]{:S(2)}) copy-start(s32[1,2]{1,0:T(1,128)} %param.31) | copy-start | bytes 28
  507.0 473.8 %copy-start.12 = (f32[256,256]{1,0:T(8,128)S(1)}, f32[256,256]{1,0:T(8,128)}, u32[]{:S(2)}) copy-start(f32[256,256]{1,0:T(8,128)} %get-tuple-element.1095) | copy-start | bytes 786436
  980.1 3.2 copy-start.4
  980.8 6.1 copy-start.1
  (7 other events, 5.1 us)
Sparse Core Ops, SparseCore 0:
  14.3 46.8 all-gather.7
  63.6 30.9 all-reduce.3
  97.0 55.1 all-gather.9
  154.5 170.8 all-gather.11
  327.6 70.5 all-gather.13
  409.7 36.2 all-reduce.5
where the time goes:
time: 978 us; the launch traced here: 994 us
  waiting for transfers between devices  343 us (35%)
  matrix products  267 us (27%)
  local copies, waits for them, and re-layouts  150 us (15%)
  loops' own time  103 us (11%)
  other arithmetic  100 us (10%)
  starting transfers between devices  16.3 us (2%)
  between operations  13.9 us (1%)
    all_gather x3, waiting for transfers between devices, shards(): lax.all_gather(tiers[level][None], 'leaf', axis=0, tiled=True)  218 us
    dot_general x61, matrix products, kernel_block(): lax.dot_general(source, target, (((0,), (0,)), ((), ())), precision=HIGH,...  129 us
    dot_general x61, matrix products, apply_block(): jnp.dot(source_vals, kernel_block(source_pts, target_pts), precision=HIGH...  127 us
    reduce_sum x61, other arithmetic, kernel_block(): target_sq = jnp.sum(target * target, axis=0)  57.5 us
    another operation x1, loops' own time, shards(): lax.fori_loop(0, own_leaves * NEAR, own_tile, jnp.zeros((R, own_cols), jn...  47.2 us
    all_gather x1, waiting for transfers between devices, shards(): group_cloud = lax.all_gather(cloud, 'help', axis=1, tiled=True)  43.6 us
    dynamic_slice x64, local copies, waits for them, and re-layouts, own_tile(): return lax.cond(index < counts[leaf], add_tile, lambda value: value, total)  42.7 us
    another operation x64, loops' own time, own_tile(): return lax.cond(index < counts[leaf], add_tile, lambda value: value, total)  39.3 us
  transfers between devices with their start and end apart: 12, of which 8 were waited for; matrix products, arithmetic and copies ran while one was open for 50% of the time, Pallas kernels for 0%

commit v1 on v0

v1 whole, which is shorter than its diff:
```python
import math
from functools import partial

import jax
import jax.numpy as jnp
from jax import lax
from jax.experimental import pallas as pl
from jax.experimental.pallas import tpu as pltpu
from jax.sharding import PartitionSpec as P

F = 64
R = 256
LEAF = 512
SK = 256
FL = 4
EXTRA = 8

BF = jnp.bfloat16
F32 = jnp.float32
LOG2E = 1.0 / math.log(2.0)
SCALE = math.sqrt(0.5 * LOG2E)
BIAS = 0.0625 * F * LOG2E
VMEM_LIMIT = 44 * 1024 * 1024


def dot(a, b):
    return jnp.dot(a, b, preferred_element_type=F32)


def dot_t(a, b):
    return lax.dot_general(a, b, (((1,), (1,)), ((), ())), preferred_element_type=F32)


def halves(x):
    hi = x.astype(BF)
    lo = (x - hi.astype(F32)).astype(BF)
    return hi, lo


def dot3(a, b, mul=dot):
    a_hi, a_lo = halves(a)
    b_hi, b_lo = halves(b)
    return mul(a_hi, b_hi) + mul(a_lo, b_hi) + mul(a_hi, b_lo)


def target_side(x):
    hi, lo = halves(x)
    both = hi.astype(F32) + lo.astype(F32)
    off = BIAS - 0.5 * jnp.sum(both * both, axis=0, keepdims=True)
    return jnp.concatenate([hi, lo, hi, lo], axis=0), off


def source_side(x):
    xt = x.T
    hi, lo = halves(xt)
    both = hi.astype(F32) + lo.astype(F32)
    off = BIAS - 0.5 * jnp.sum(both * both, axis=1, keepdims=True)
    return jnp.concatenate([hi, hi, lo, lo], axis=1), off


def near_body(nblk, nchunk, has_acc, mult_ref, *refs):
    targets = refs[:nblk]
    src_ref = refs[nblk]
    w_refs = refs[nblk + 1 : nblk + 1 + nchunk]
    at = nblk + 1 + nchunk
    if has_acc:
        acc_refs = refs[at : at + nblk]
        at += nblk
    outs = refs[at : at + nblk]
    t_scr, tb_scr, s_scr, sb_scr, w_scr, o_scr, list_ref = refs[at + nblk :]
    rows = R // nchunk
    for b in range(nblk):
        side, off = target_side(targets[b][:F, :] * SCALE)
        for leaf in range(2):
            cols = slice(leaf * LEAF, (leaf + 1) * LEAF)
            t_scr[2 * b + leaf] = side[:, cols]
            tb_scr[2 * b + leaf] = jnp.broadcast_to(off[:, cols], (8, LEAF))
            if has_acc:
                o_scr[2 * b + leaf] = acc_refs[b][:, cols]
            else:
                o_scr[2 * b + leaf] = jnp.zeros((R, LEAF), F32)
    for leaf in range(2):
        cols = slice(leaf * LEAF, (leaf + 1) * LEAF)
        side, off = source_side(src_ref[:F, cols] * SCALE)
        s_scr[leaf] = side
        sb_scr[leaf] = jnp.broadcast_to(off, (LEAF, 128))
        for c in range(nchunk):
            hi, lo = halves(w_refs[c][:, cols])
            w_scr[leaf, c * rows : (c + 1) * rows, :] = hi
            w_scr[leaf, R + c * rows : R + (c + 1) * rows, :] = lo

    def collect(n, count):
        @pl.when(mult_ref[n] > 0)
        def _():
            list_ref[count] = n

        return count + (mult_ref[n] > 0).astype(jnp.int32)

    count = lax.fori_loop(0, 4 * nblk, collect, jnp.int32(0))

    def tile(index, carry):
        n = list_ref[index]
        t, j = n // 2, n % 2
        side = t_scr[t]
        off = tb_scr[t][:1, :]
        total = jnp.zeros((R, LEAF), F32)
        for half in range(2):
            part = slice(half * 256, (half + 1) * 256)
            cross = dot(s_scr[j, part, :], side)
            src_off = sb_scr[j, part, :]
            src_off = jnp.concatenate([src_off] * (LEAF // 128), axis=1)
            k_hi, k_lo = halves(jnp.exp2(cross + src_off + off))
            total = total + dot(w_scr[j, :R, part], k_hi)
            total = total + dot(w_scr[j, R:, part], k_hi)
            total = total + dot(w_scr[j, :R, part], k_lo)
        o_scr[t] = o_scr[t] + mult_ref[n].astype(F32) * total
        return carry

    lax.fori_loop(0, count, tile, jnp.int32(0))
    for b in range(nblk):
        for leaf in range(2):
            outs[b][:, leaf * LEAF : (leaf + 1) * LEAF] = o_scr[2 * b + leaf]


def near_call(mult, targets, src, chunks, acc=None):
    nblk, nchunk = len(targets), len(chunks)
    cols = 2 * LEAF
    vmem = pl.BlockSpec(memory_space=pltpu.VMEM)
    n_in = nblk + 1 + nchunk
    aliases = {}
    extra = []
    if acc is not None:
        extra = list(acc)
        aliases = {1 + n_in + b: b for b in range(nblk)}
    tiles = nblk * 2
    return pl.pallas_call(
        partial(near_body, nblk, nchunk, acc is not None),
        out_shape=[jax.ShapeDtypeStruct((R, cols), F32)] * nblk,
        in_specs=[pl.BlockSpec(memory_space=pltpu.SMEM)] + [vmem] * (n_in + len(extra)),
        out_specs=[vmem] * nblk,
        scratch_shapes=[
            pltpu.VMEM((2 * nblk, 4 * F, LEAF), BF),
            pltpu.VMEM((2 * nblk, 8, LEAF), F32),
            pltpu.VMEM((2, LEAF, 4 * F), BF),
            pltpu.VMEM((2, LEAF, 128), F32),
            pltpu.VMEM((2, 2 * R, LEAF), BF),
            pltpu.VMEM((2 * nblk, R, LEAF), F32),
            pltpu.SMEM((4 * nblk,), jnp.int32),
        ],
        input_output_aliases=aliases,
        compiler_params=pltpu.CompilerParams(vmem_limit_bytes=VMEM_LIMIT),
        cost_estimate=pl.CostEstimate(
            flops=tiles * 2 * LEAF * LEAF * (4 * F + 3 * R) // 2,
            bytes_accessed=nblk * R * cols * 8,
            transcendentals=tiles * LEAF * LEAF // 2,
        ),
    )(mult, *targets, src, *chunks, *extra)


def up_body(xs, pos_ref, w_ref, interp_ref, keep_ref, give_ref, scr):
    total = jnp.zeros((R, SK), F32)
    for leaf in range(2):
        total = total + dot3(w_ref[:, leaf * LEAF : (leaf + 1) * LEAF], interp_ref[leaf])
    scr[...] = total
    rows = R // (2 * xs)
    x, core = pos_ref[0], pos_ref[1]
    for dx in range(xs):
        there = 2 * lax.rem(x + dx, xs)
        keep_ref[dx] = scr[pl.ds(pl.multiple_of((there + core) * rows, rows), rows), :]
        give_ref[dx] = scr[pl.ds(pl.multiple_of((there + 1 - core) * rows, rows), rows), :]


def up_call(xs, pos, weights, interp):
    rows = R // (2 * xs)
    vmem = pl.BlockSpec(memory_space=pltpu.VMEM)
    return pl.pallas_call(
        partial(up_body, xs),
        out_shape=[jax.ShapeDtypeStruct((xs, rows, SK), F32)] * 2,
        in_specs=[pl.BlockSpec(memory_space=pltpu.SMEM), vmem, vmem],
        out_specs=[vmem, vmem],
        scratch_shapes=[pltpu.VMEM((R, SK), F32)],
        compiler_params=pltpu.CompilerParams(vmem_limit_bytes=VMEM_LIMIT),
        cost_estimate=pl.CostEstimate(
            flops=6 * R * SK * 2 * LEAF, bytes_accessed=2 << 20, transcendentals=0
        ),
    )(pos, weights, interp)


def skel_body(xs, nblk, base_ref, index_ref, *refs):
    blocks = refs[:nblk]
    sums = refs[nblk:-1]
    out_ref = refs[-1]
    cols = 2 * LEAF
    total = jnp.zeros((2 * F, SK), F32)
    spot = lax.broadcasted_iota(jnp.int32, (cols, SK), 0)
    for b in range(nblk):
        hi, lo = halves(blocks[b][:F, :] * SCALE)
        hot = spot + base_ref[b] == index_ref[...]
        total = total + dot(jnp.concatenate([hi, lo], axis=0), hot.astype(F32).astype(BF))
    out_ref[:F, :] = total[:F] + total[F:]
    value = sums[0][...]
    for ref in sums[1:]:
        value = value + ref[...]
    out_ref[F:, :] = value


def skel_call(xs, bases, index, blocks, sums):
    rows = R // (2 * xs)
    vmem = pl.BlockSpec(memory_space=pltpu.VMEM)
    return pl.pallas_call(
        partial(skel_body, xs, len(blocks)),
        out_shape=jax.ShapeDtypeStruct((F + rows, SK), F32),
        in_specs=[pl.BlockSpec(memory_space=pltpu.SMEM)] + [vmem] * (1 + len(blocks) + len(sums)),
        out_specs=vmem,
        compiler_params=pltpu.CompilerParams(vmem_limit_bytes=VMEM_LIMIT),
        cost_estimate=pl.CostEstimate(
            flops=2 * 2 * F * SK * 2 * LEAF * len(blocks), bytes_accessed=1 << 20, transcendentals=0
        ),
    )(bases, index, *blocks, *sums)


def upper_start(level, groups):
    return sum((groups >> step for step in range(1, level)))


def list_start(level, groups):
    return sum((groups >> step for step in range(level)))


def far_body(groups, rows, steps, pos_ref, far_ref, node_ref, transfer_ref, *refs):
    pieces = refs[: len(steps) + 1]
    out_ref, p_scr, u_scr, f_scr = refs[len(steps) + 1 :]
    levels = groups.bit_length() - 1
    group = pos_ref[2]
    start = [sum(groups >> step for step in range(level)) for level in range(levels)]
    held = [0]
    p_scr[0] = pieces[0][:F, :]
    u_scr[0] = pieces[0][F:, :]
    for piece, step in zip(pieces[1:], steps):
        for at, mask in enumerate(held):
            p_scr[mask ^ step] = piece[at, :F, :]
            u_scr[mask ^ step] = piece[at, F:, :]
        held = held + [mask ^ step for mask in held]
    spot = lax.broadcasted_iota(jnp.int32, (2 * SK, SK), 0)
    for level in range(1, levels):
        bit = (group >> (level - 1)) & 1
        for m in range(groups >> level):
            row = upper_start(level, groups) + (m ^ (group >> level))
            left = start[level - 1] + 2 * m + bit
            right = start[level - 1] + 2 * m + 1 - bit
            hot = (spot == node_ref[row]).astype(F32).astype(BF)
            pts = jnp.concatenate([p_scr[left], p_scr[right]], axis=1)
            hi, lo = halves(pts)
            both = dot(jnp.concatenate([hi, lo], axis=0), hot)
            p_scr[start[level] + m] = both[:F] + both[F:]
            vals = jnp.concatenate([u_scr[left], u_scr[right]], axis=1)
            u_scr[start[level] + m] = dot3(vals, transfer_ref[row])
    for level in range(levels):
        node = group >> level
        side, off = target_side(p_scr[start[level]])
        f_scr[level] = jnp.zeros((rows, SK), F32)

        def one(m, carry, level=level, node=node, side=side, off=off):
            hits = jnp.int32(0)
            for slot in range(FL):
                entry = far_ref[list_start(level, groups) + node, slot]
                hits = hits + (entry == (m ^ node)).astype(jnp.int32)

            @pl.when(hits > 0)
            def _():
                src, src_off = source_side(p_scr[start[level] + m])
                block = jnp.exp2(dot(src, side) + src_off + off)
                term = dot3(u_scr[start[level] + m], block)
                f_scr[level] = f_scr[level] + hits.astype(F32) * term

            return carry

        lax.fori_loop(0, groups >> level, one, jnp.int32(0))
    local = f_scr[levels - 1]
    for level in range(levels - 1, 0, -1):
        row = upper_start(level, groups) + (group >> level)
        bit = (group >> (level - 1)) & 1
        matrix = transfer_ref[row, pl.ds(pl.multiple_of(bit * SK, SK), SK), :]
        local = f_scr[level - 1] + dot3(local, matrix, dot_t)
    out_ref[...] = local


def far_call(groups, pos, far_nodes, skel_node, transfer, pieces, steps):
    rows = pieces[0].shape[0] - F
    vmem = pl.BlockSpec(memory_space=pltpu.VMEM)
    smem = pl.BlockSpec(memory_space=pltpu.SMEM)
    nodes = 2 * groups
    return pl.pallas_call(
        partial(far_body, groups, rows, steps),
        out_shape=jax.ShapeDtypeStruct((rows, SK), F32),
        in_specs=[smem, smem, vmem, vmem] + [vmem] * len(pieces),
        out_specs=vmem,
        scratch_shapes=[
            pltpu.VMEM((nodes, F, SK), F32),
            pltpu.VMEM((nodes, rows, SK), F32),
            pltpu.VMEM((groups.bit_length(), rows, SK), F32),
        ],
        compiler_params=pltpu.CompilerParams(vmem_limit_bytes=VMEM_LIMIT),
        cost_estimate=pl.CostEstimate(
            flops=20 * 2 * 256 * SK * SK * 4, bytes_accessed=4 << 20, transcendentals=20 * SK * SK
        ),
    )(pos, far_nodes, skel_node[:, None, :], transfer, *pieces)


def final_body(xs, nsum, pos_ref, interp_ref, *refs):
    same = refs[:xs]
    mate = refs[xs]
    sums = refs[xs + 1 : xs + 1 + nsum]
    out_ref, v_scr = refs[xs + 1 + nsum :]
    rows = R // (2 * xs)
    x, core = pos_ref[0], pos_ref[1]
    for dx in range(xs):
        there = 2 * lax.rem(x + dx, xs)
        v_scr[pl.ds(pl.multiple_of((there + core) * rows, rows), rows), :] = same[dx][...]
        v_scr[pl.ds(pl.multiple_of((there + 1 - core) * rows, rows), rows), :] = mate[dx]
    value = v_scr[...]
    for leaf in range(2):
        cols = slice(leaf * LEAF, (leaf + 1) * LEAF)
        total = dot3(value, interp_ref[leaf], dot_t)
        for ref in sums:
            total = total + ref[:, cols]
        out_ref[:, cols] = total


def final_call(xs, pos, interp, same, mate, sums):
    vmem = pl.BlockSpec(memory_space=pltpu.VMEM)
    return pl.pallas_call(
        partial(final_body, xs, len(sums)),
        out_shape=jax.ShapeDtypeStruct((R, 2 * LEAF), F32),
        in_specs=[pl.BlockSpec(memory_space=pltpu.SMEM)] + [vmem] * (1 + xs + 1 + len(sums)),
        out_specs=vmem,
        scratch_shapes=[pltpu.VMEM((R, SK), F32)],
        compiler_params=pltpu.CompilerParams(vmem_limit_bytes=VMEM_LIMIT),
        cost_estimate=pl.CostEstimate(
            flops=6 * R * SK * 2 * LEAF, bytes_accessed=5 << 20, transcendentals=0
        ),
    )(pos, interp, *same, mate, *sums)


def help_pairs(xs, dx, dc):
    return [
        (2 * ((x + dx) % xs) + (core ^ dc), 2 * x + core) for x in range(xs) for core in range(2)
    ]


def shards(
    points, weights, interp, transfer, near_count, near_src, skel_group, skel_node, far_nodes
):
    helpers = lax.axis_size("help")
    groups = lax.axis_size("leaf")
    xs = helpers // 2
    helper = lax.axis_index("help")
    group = lax.axis_index("leaf")
    x, core = helper // 2, helper % 2
    leaves = 2 * helpers
    pos = jnp.stack([x, core, group]).astype(jnp.int32)
    nchunk = 2

    def from_help(value, dx, dc):
        return lax.ppermute(value, "help", help_pairs(xs, dx, dc))

    beside = [(i, i ^ 1) for i in range(groups)]
    across = [(i, i + 2) for i in range(0, groups - 2, 2)]
    across += [(i, i - 2) for i in range(3, groups, 2)]

    slots = near_src.shape[1]
    relative = near_src - (group - 1) * leaves
    used = lax.broadcasted_iota(jnp.int32, near_src.shape, 1) < near_count[0][:, None]
    names = lax.broadcasted_iota(jnp.int32, (2, slots, 3 * leaves), 2)
    times = jnp.sum(((relative[:, :, None] == names) & used[:, :, None]).astype(F32), axis=1)
    times = times.reshape(2, 3, leaves)
    even = group % 2 == 0
    before, own, after = times[:, 0], times[:, 1], times[:, 2]
    times = jnp.stack([own, jnp.where(even, after, before), jnp.where(even, before, after)], axis=1)
    flat = times.reshape(1, 6 * leaves)
    flat = jnp.pad(flat, ((0, EXTRA - 1), (0, points.shape[1] - 6 * leaves)))
    packed = jnp.concatenate([points, flat], axis=0)

    rows = R // nchunk
    w_own = [weights[c * rows : (c + 1) * rows] for c in range(nchunk)]
    pts_y = lax.ppermute(points, "leaf", beside)
    w_y = [lax.ppermute(chunk, "leaf", beside) for chunk in w_own]
    pts_z = lax.ppermute(pts_y, "leaf", across)
    w_z = [lax.ppermute(chunk, "leaf", across) for chunk in w_y]

    order = [(dx, dc) for dx in range(xs) for dc in range(2)]
    blocks = [packed if o == (0, 0) else from_help(packed, *o) for o in order]
    keep, give = up_call(xs, pos, weights, interp)
    half = keep + from_help(give, 0, 1)
    sums = [half[0]] + [
        lax.ppermute(half[dx], "help", help_pairs(xs, -dx, 0)) for dx in range(1, xs)
    ]

    mult = jnp.stack([block[F, : 6 * leaves].reshape(2, 3, helpers, 2) for block in blocks])
    mult = lax.dynamic_index_in_dim(mult, helper, 3, keepdims=False).astype(jnp.int32)
    mult = mult.transpose(2, 0, 1, 3).reshape(3, len(order) * 4)

    bases = jnp.stack([(2 * ((x + dx) % xs) + (core ^ dc)) for dx, dc in order]) * (2 * LEAF)
    payload = skel_call(xs, bases.astype(jnp.int32), skel_group, blocks, sums)

    steps = [1 << k for k in range(groups.bit_length() - 1)]
    steps = steps[:1] + steps[:0:-1]
    pieces = [payload]
    held = payload[None]
    for step in steps:
        got = lax.ppermute(held, "leaf", [(i, i ^ step) for i in range(groups)])
        pieces.append(got)
        held = jnp.concatenate([held, got], axis=0)

    near = near_call(mult[0], blocks, points, w_own)
    near = near_call(mult[1], blocks, pts_y, w_y, near)

    v_own = far_call(groups, pos, far_nodes, skel_node, transfer, pieces, steps)
    v_same = [v_own] + [from_help(v_own, dx, 0) for dx in range(1, xs)]
    v_mate = from_help(jnp.stack(v_same), 0, 1)

    away = near_call(mult[2][8:], blocks[2:], pts_z, w_z, near[2:])
    home = near_call(mult[2][:8], blocks[:2], pts_z, w_z, near[:2])
    parts = [home[0], from_help(home[1], 0, 1)]
    for dx in range(1, xs):
        keep_dx, give_dx = away[2 * dx - 2], away[2 * dx - 1]
        part = keep_dx + from_help(give_dx, 0, 1)
        parts.append(lax.ppermute(part, "help", help_pairs(xs, -dx, 0)))
    return final_call(xs, pos, interp, v_same, v_mate, parts)


def solution(mesh):
    placed = (
        P(None, ("leaf", "help")),
        P(None, ("leaf", "help")),
        P(("leaf", "help"), None, None),
        P(),
        P("leaf", "help"),
        P(("leaf", "help"), None),
        P("leaf", None),
        P(),
        P(),
    )
    return jax.shard_map(
        shards, mesh=mesh, in_specs=placed, out_specs=P(None, ("leaf", "help")), check_vma=False
    )
```

time: 978 us -> 155 us (0.16)
  the two profiles are of different devices: /device:TPU:3 before, /device:TPU:9 now
where the time goes in v1:
time: 155 us; the launch traced here: 154 us
  Pallas kernels  53.7 us (35%)
  waiting for transfers between devices  47.1 us (30%)
  starting transfers between devices  24 us (15%)
  local copies, waits for them, and re-layouts  20.4 us (13%)
  other arithmetic  8.09 us (5%)
    pallas_call x4, Pallas kernels, near_call(): pl.pallas_call(partial(near_body, nblk, nchunk, acc is not None), out_sha...  42.2 us
    unnamed x59, local copies, waits for them, and re-layouts  18 us
    ppermute x8, waiting for transfers between devices, from_help(): return lax.ppermute(value, 'help', help_pairs(xs, dx, dc))  17.7 us
    ppermute x3, waiting for transfers between devices, shards(): got = lax.ppermute(held, 'leaf', [(i, i ^ step) for i in range(groups)])  14.9 us
    ppermute x2, waiting for transfers between devices, shards(): w_y = [lax.ppermute(chunk, 'leaf', beside) for chunk in w_own]  11.4 us
    ppermute x8, starting transfers between devices, from_help(): return lax.ppermute(value, 'help', help_pairs(xs, dx, dc))  11 us
    ppermute x2, starting transfers between devices, shards(): w_z = [lax.ppermute(chunk, 'leaf', across) for chunk in w_y]  6.38 us
    pallas_call x1, Pallas kernels, far_call(): pl.pallas_call(partial(far_body, groups, rows, steps), out_shape=jax.Shap...  6.36 us
  transfers between devices with their start and end apart: 19, of which 8 were waited for; matrix products, arithmetic and copies ran while one was open for 4% of the time, Pallas kernels for 28%

profile of v1, /device:TPU:9, one launch (start us, length us, event | category | flops | bytes accessed | tf_op | source)
XLA Modules:
  0.0 153.6 jit_solution(16072993769077384240)
XLA Ops:
  4.7 1.2 collective-permute-start.1
  6.4 1.2 collective-permute-start.10
  7.7 1.2 copy-done
  14.5 1.2 collective-permute-start.14
  16.5 3.2 %collective-permute-start.11 = (f32[64,1024]{1,0:T(8,128)}, f32[64,1024]{1,0:T(8,128)}, u32[]{:S(2)}, u32[]{:S(2)}) collective-permute-start(f32[64,1024]{1,0:T(8,128)} %collective-permute-done.10.refs_4_), channel_id=1, source_target_pairs={{0,8},{8,16},{16,24},{12,4},{20,12},{28,20},{1,9},{9,17},{17,25},{... | collective-permute-start | bytes 786440 | tf_op jit(solution)/shard_map/ppermute | solution.py:388
  22.7 3.4 %collective-permute-done.12.refs_5_ = f32[128,1024]{1,0:T(8,128)} collective-permute-done((f32[128,1024]{1,0:T(8,128)S(1)}, f32[128,1024]{1,0:T(8,128)}, u32[]{:S(2)}, u32[]{:S(2)}) %collective-permute-start.12) | collective-permute-done | bytes 524320 | tf_op jit(solution)/shard_map/ppermute | solution.py:387
  26.1 3.2 %collective-permute-start.13 = (f32[128,1024]{1,0:T(8,128)}, f32[128,1024]{1,0:T(8,128)S(1)}, u32[]{:S(2)}, u32[]{:S(2)}) collective-permute-start(f32[128,1024]{1,0:T(8,128)} %collective-permute-done.12.refs_5_), channel_id=1, source_target_pairs={{0,8},{8,16},{16,24},{12,4},{20,12},{28,20},{1,9},{9,17},{17,25},{... | collective-permute-start | bytes 1572872 | tf_op jit(solution)/shard_map/ppermute | solution.py:389
  29.3 8.0 %collective-permute-done.14.refs_6_ = f32[128,1024]{1,0:T(8,128)} collective-permute-done((f32[128,1024]{1,0:T(8,128)S(1)}, f32[128,1024]{1,0:T(8,128)}, u32[]{:S(2)}, u32[]{:S(2)}) %collective-permute-start.14) | collective-permute-done | bytes 524320 | tf_op jit(solution)/shard_map/ppermute | solution.py:387
  37.3 3.2 %collective-permute-start.15 = (f32[128,1024]{1,0:T(8,128)}, f32[128,1024]{1,0:T(8,128)S(1)}, u32[]{:S(2)}, u32[]{:S(2)}) collective-permute-start(f32[128,1024]{1,0:T(8,128)} %collective-permute-done.14.refs_6_), channel_id=1, source_target_pairs={{0,8},{8,16},{16,24},{12,4},{20,12},{28,20},{1,9},{9,17},{17,25},{... | collective-permute-start | bytes 1572872 | tf_op jit(solution)/shard_map/ppermute | solution.py:389
  46.5 13.8 %shard_map.94 = (f32[256,1024]{1,0:T(8,128)S(1)}, f32[256,1024]{1,0:T(8,128)}, f32[256,1024]{1,0:T(8,128)S(1)}, f32[256,1024]{1,0:T(8,128)}) custom-call(s32[16]{0:T(128)S(1)} %squeeze.21.mult_ref, f32[72,1024]{1,0:T(8,128)S(1)} %select_maximum_fusion.refs_0_, f32[72,1024]{1,0:T(8,128)S(1)} %copy-done.4, f32[72,1024]{1,0:T(8,128)S(1)} %copy-done.9, ...), custom_call_target="tpu_custom_call" | custom-call | flops 2147483648 | bytes 8388608 | tf_op jit(solution)/shard_map/pallas_call | solution.py:136
  63.5 16.1 %shard_map.95 = (f32[256,1024]{1,0:T(8,128)S(1)}, f32[256,1024]{1,0:T(8,128)}, f32[256,1024]{1,0:T(8,128)S(1)}, f32[256,1024]{1,0:T(8,128)}) custom-call(s32[16]{0:T(128)S(1)} %squeeze.20.mult_ref, f32[72,1024]{1,0:T(8,128)S(1)} %select_maximum_fusion.refs_0_, ...), custom_call_target="tpu_custom_call", output_to_operand_aliasing={{0}: (8, {}), {1}: (9, {}), {2}: (10, {}), {3}: (11, {})} | custom-call | flops 2147483648 | bytes 8388608 | tf_op jit(solution)/shard_map/pallas_call | solution.py:136
  79.7 7.6 %shard_map.97 = (f32[256,1024]{1,0:T(8,128)S(1)}, f32[256,1024]{1,0:T(8,128)}) custom-call(s32[8]{0:T(128)S(1)} %slice.71.mult_ref, f32[72,1024]{1,0:T(8,128)S(1)} %copy-done.11, f32[72,1024]{1,0:T(8,128)S(1)} %copy-done.14, f32[64,1024]{1,0:T(8,128)} %collective-permute-done.11.refs_2_, ...), custom_call_target="tpu_custom_call", output_to_operand_aliasing={{0}: (6, {}), {1}: (7, {})} | custom-call | flops 1073741824 | bytes 4194304 | tf_op jit(solution)/shard_map/pallas_call | solution.py:136
  87.5 3.0 %collective-permute-done.4.refs_5_ = f32[64,256]{1,0:T(8,128)S(1)} collective-permute-done((f32[64,256]{1,0:T(8,128)S(1)}, f32[64,256]{1,0:T(8,128)S(1)}, u32[]{:S(2)}, u32[]{:S(2)}) %collective-permute-start.4) | collective-permute-done | bytes 65568 | tf_op jit(solution)/shard_map/ppermute | solution.py:396
  91.7 3.8 %collective-permute-done.5.refs_1_ = f32[1,128,256]{2,1,0:T(8,128)S(1)} collective-permute-done((f32[1,128,256]{2,1,0:T(8,128)S(1)}, f32[1,128,256]{2,1,0:T(8,128)S(1)}, u32[]{:S(2)}, u32[]{:S(2)}) %collective-permute-start.5) | collective-permute-done | bytes 131104 | tf_op jit(solution)/shard_map/ppermute | solution.py:411
  96.4 11.1 %collective-permute-done.6.refs_2_ = f32[2,128,256]{2,1,0:T(8,128)} collective-permute-done((f32[2,128,256]{2,1,0:T(8,128)}, f32[2,128,256]{2,1,0:T(8,128)}, u32[]{:S(2)}, u32[]{:S(2)}) %collective-permute-start.6) | collective-permute-done | bytes 262176 | tf_op jit(solution)/shard_map/ppermute | solution.py:411
  107.5 1.9 %pad_maximum_fusion = f32[4,128,256]{2,1,0:T(8,128)} fusion(f32[2,128,256]{2,1,0:T(8,128)} %collective-permute-done.6.refs_2_, f32[1,128,256]{2,1,0:T(8,128)} %copy-done.21, f32[1,128,256]{2,1,0:T(8,128)} %bitcast.21), kind=kLoop, calls=%fused_computation | loop fusion | flops 262144 | bytes 1048576 | tf_op jit(solution)/shard_map/concatenate | solution.py:413
  110.9 4.7 %shard_map.96 = (f32[256,1024]{1,0:T(8,128)S(1)}, f32[256,1024]{1,0:T(8,128)}) custom-call(s32[8]{0:T(128)S(1)} %slice.65.mult_ref, f32[72,1024]{1,0:T(8,128)S(1)} %select_maximum_fusion.refs_0_, f32[72,1024]{1,0:T(8,128)S(1)} %copy-done.7, f32[64,1024]{1,0:T(8,128)} %collective-permute-done.11.refs_2_, ...), custom_call_target="tpu_custom_call", output_to_operand_aliasing={{0}: (6, {}), {1}: (7, {})} | custom-call | flops 1073741824 | bytes 4194304 | tf_op jit(solution)/shard_map/pallas_call | solution.py:136
  115.6 5.6 %collective-permute-start.16 = (f32[256,1024]{1,0:T(8,128)}, f32[256,1024]{1,0:T(8,128)}, u32[]{:S(2)}, u32[]{:S(2)}) collective-permute-start(f32[256,1024]{1,0:T(8,128)} %get-tuple-element.28), channel_id=1, source_target_pairs={{1,0},{0,1},{3,2},{2,3},{5,4},{4,5},{7,6},{6,7},{9,8},{8,9},{11,10... | collective-permute-start | bytes 3145736 | tf_op jit(solution)/shard_map/ppermute | solution.py:365
  121.3 1.4 add.56
  122.9 2.0 %copy-done.25 = f32[6,512,256]{2,1,0:T(8,128)S(1)} copy-done((f32[6,512,256]{2,1,0:T(8,128)S(1)}, f32[6,512,256]{2,1,0:T(8,128)}, u32[]{:S(2)}) %copy-start.25) | copy-done | bytes 3145752
  124.8 6.4 %shard_map.93.refs_0_ = f32[64,256]{1,0:T(8,128)S(1)} custom-call(s32[3]{0:T(128)S(1)} %pad_add_fusion.pos_ref, s32[14,4]{1,0:T(8,128)S(1)} %copy.68.far_ref, s32[6,1,256]{2,1,0:T(1,128)S(1)} %broadcast_in_dim.8.node_ref, f32[6,512,256]{2,1,0:T(8,128)S(1)} %copy-done.25, f32[128,256]{1,0:T(8,128)S(1)} %copy-done.16, f32[1,128,256]{2,1,0:T(8,128)S(1)} %copy-done.22, ...), custom_call_target="tpu_custom_call" | custom-call | flops 2684354560 | bytes 4194304 | tf_op jit(solution)/shard_map/pallas_call | solution.py:293
  131.2 1.5 collective-permute-start.8
  132.7 16.1 %collective-permute-done.8.refs_1_ = f32[64,256]{1,0:T(8,128)S(1)} collective-permute-done((f32[64,256]{1,0:T(8,128)S(1)}, f32[64,256]{1,0:T(8,128)S(1)}, u32[]{:S(2)}, u32[]{:S(2)}) %collective-permute-start.8) | collective-permute-done | bytes 65568 | tf_op jit(solution)/shard_map/ppermute | solution.py:365
  150.7 2.8 %shard_map.98 = f32[256,1024]{1,0:T(8,128)} custom-call(s32[3]{0:T(128)S(1)} %pad_add_fusion.pos_ref, f32[2,512,256]{2,1,0:T(8,128)S(1)} %copy-done.2, f32[64,256]{1,0:T(8,128)S(1)} %shard_map.93.refs_0_, f32[64,256]{1,0:T(8,128)S(1)} %collective-permute-done.8.refs_1_, f32[2,64,256]{2,1,0:T(8,128)S(1)} %collective-permute-done.9.refs_2_, ...), custom_call_target="tpu_custom_call" | custom-call | flops 402653184 | bytes 5242880 | tf_op jit(solution)/shard_map/pallas_call | solution.py:332
  (120 shorter events, 29.5 us)
Async XLA Ops:
  3.9 12.6 %collective-permute-start = (f32[72,1024]{1,0:T(8,128)S(1)}, f32[72,1024]{1,0:T(8,128)S(1)}, u32[]{:S(2)}, u32[]{:S(2)}) collective-permute-start(f32[72,1024]{1,0:T(8,128)S(1)} %select_maximum_fusion.refs_0_), channel_id=1, source_target_pairs={{1,0},{0,1},{3,2},{2,3},{5,4},{4,5},{7,6},{6,7},{9,8},{8,9},{11,10... | collective-permute-start | bytes 884744 | tf_op jit(solution)/shard_map/ppermute | solution.py:365
  4.7 15.9 %collective-permute-start.1 = (f32[72,1024]{1,0:T(8,128)S(1)}, f32[72,1024]{1,0:T(8,128)S(1)}, u32[]{:S(2)}, u32[]{:S(2)}) collective-permute-start(f32[72,1024]{1,0:T(8,128)S(1)} %select_maximum_fusion.refs_0_), channel_id=1, source_target_pairs={{2,0},{3,1},{0,2},{1,3},{6,4},{7,5},{4,6},{5,7},{10,8},{11,9},{8,1... | collective-permute-start | bytes 884744 | tf_op jit(solution)/shard_map/ppermute | solution.py:365
  5.9 15.6 %collective-permute-start.2 = (f32[72,1024]{1,0:T(8,128)S(1)}, f32[72,1024]{1,0:T(8,128)S(1)}, u32[]{:S(2)}, u32[]{:S(2)}) collective-permute-start(f32[72,1024]{1,0:T(8,128)S(1)} %select_maximum_fusion.refs_0_), channel_id=1, source_target_pairs={{3,0},{2,1},{1,2},{0,3},{7,4},{6,5},{5,6},{4,7},{11,8},{10,9},{9,1... | collective-permute-start | bytes 884744 | tf_op jit(solution)/shard_map/ppermute | solution.py:365
  6.4 8.1 %collective-permute-start.10 = (f32[64,1024]{1,0:T(8,128)}, f32[64,1024]{1,0:T(8,128)}, u32[]{:S(2)}, u32[]{:S(2)}) collective-permute-start(f32[64,1024]{1,0:T(8,128)} %refs_4_.1), channel_id=1, source_target_pairs={{0,4},{4,0},{8,12},{12,8},{16,20},{20,16},{24,28},{28,24},{1,5},{5... | collective-permute-start | bytes 786440 | tf_op jit(solution)/shard_map/ppermute | solution.py:386
  11.3 1.5 collective-permute-start.3
  12.8 13.3 %collective-permute-start.12 = (f32[128,1024]{1,0:T(8,128)S(1)}, f32[128,1024]{1,0:T(8,128)}, u32[]{:S(2)}, u32[]{:S(2)}) collective-permute-start(f32[128,1024]{1,0:T(8,128)S(1)} %get-tuple-element.38.refs_5_), channel_id=1, source_target_pairs={{0,4},{4,0},{8,12},{12,8},{16,20},{20,16},{24,28},{28,24},{1,5},{5... | collective-permute-start | bytes 1572872 | tf_op jit(solution)/shard_map/ppermute | solution.py:387
  14.5 22.8 %collective-permute-start.14 = (f32[128,1024]{1,0:T(8,128)S(1)}, f32[128,1024]{1,0:T(8,128)}, u32[]{:S(2)}, u32[]{:S(2)}) collective-permute-start(f32[128,1024]{1,0:T(8,128)S(1)} %get-tuple-element.37.refs_6_), channel_id=1, source_target_pairs={{0,4},{4,0},{8,12},{12,8},{16,20},{20,16},{24,28},{28,24},{1,5},{5... | collective-permute-start | bytes 1572872 | tf_op jit(solution)/shard_map/ppermute | solution.py:387
  16.5 63.1 %collective-permute-start.11 = (f32[64,1024]{1,0:T(8,128)}, f32[64,1024]{1,0:T(8,128)}, u32[]{:S(2)}, u32[]{:S(2)}) collective-permute-start(f32[64,1024]{1,0:T(8,128)} %collective-permute-done.10.refs_4_), channel_id=1, source_target_pairs={{0,8},{8,16},{16,24},{12,4},{20,12},{28,20},{1,9},{9,17},{17,25},{... | collective-permute-start | bytes 786440 | tf_op jit(solution)/shard_map/ppermute | solution.py:388
  26.1 53.6 %collective-permute-start.13 = (f32[128,1024]{1,0:T(8,128)}, f32[128,1024]{1,0:T(8,128)S(1)}, u32[]{:S(2)}, u32[]{:S(2)}) collective-permute-start(f32[128,1024]{1,0:T(8,128)} %collective-permute-done.12.refs_5_), channel_id=1, source_target_pairs={{0,8},{8,16},{16,24},{12,4},{20,12},{28,20},{1,9},{9,17},{17,25},{... | collective-permute-start | bytes 1572872 | tf_op jit(solution)/shard_map/ppermute | solution.py:389
  37.3 42.4 %collective-permute-start.15 = (f32[128,1024]{1,0:T(8,128)}, f32[128,1024]{1,0:T(8,128)S(1)}, u32[]{:S(2)}, u32[]{:S(2)}) collective-permute-start(f32[128,1024]{1,0:T(8,128)} %collective-permute-done.14.refs_6_), channel_id=1, source_target_pairs={{0,8},{8,16},{16,24},{12,4},{20,12},{28,20},{1,9},{9,17},{17,25},{... | collective-permute-start | bytes 1572872 | tf_op jit(solution)/shard_map/ppermute | solution.py:389
  63.5 16.2 %copy-start.11 = (f32[72,1024]{1,0:T(8,128)S(1)}, f32[72,1024]{1,0:T(8,128)}, u32[]{:S(2)}) copy-start(f32[72,1024]{1,0:T(8,128)} %copy-done.8) | copy-start | bytes 884740
  79.6 10.9 %copy-start.24 = (s32[1,256]{1,0:T(1,128)S(1)}, s32[1,256]{1,0:T(1,128)}, u32[]{:S(2)}) copy-start(s32[1,256]{1,0:T(1,128)} %index_ref.1) | copy-start | bytes 3076
  87.3 34.0 %collective-permute-start.17 = (f32[256,1024]{1,0:T(8,128)}, f32[256,1024]{1,0:T(8,128)}, u32[]{:S(2)}, u32[]{:S(2)}) collective-permute-start(f32[256,1024]{1,0:T(8,128)} %get-tuple-element.32), channel_id=1, source_target_pairs={{1,0},{0,1},{3,2},{2,3},{5,4},{4,5},{7,6},{6,7},{9,8},{8,9},{11,10... | collective-permute-start | bytes 3145736 | tf_op jit(solution)/shard_map/ppermute | solution.py:365
  87.3 3.2 %collective-permute-start.4 = (f32[64,256]{1,0:T(8,128)S(1)}, f32[64,256]{1,0:T(8,128)S(1)}, u32[]{:S(2)}, u32[]{:S(2)}) collective-permute-start(f32[64,256]{1,0:T(8,128)S(1)} %get-tuple-element.39), channel_id=1, source_target_pairs={{2,0},{3,1},{0,2},{1,3},{6,4},{7,5},{4,6},{5,7},{10,8},{11,9},{8,1... | collective-permute-start | bytes 196616 | tf_op jit(solution)/shard_map/ppermute | solution.py:396
  91.6 3.9 %collective-permute-start.5 = (f32[1,128,256]{2,1,0:T(8,128)S(1)}, f32[1,128,256]{2,1,0:T(8,128)S(1)}, u32[]{:S(2)}, u32[]{:S(2)}) collective-permute-start(f32[1,128,256]{2,1,0:T(8,128)S(1)} %bitcast.19), channel_id=1, source_target_pairs={{0,4},{4,0},{8,12},{12,8},{16,20},{20,16},{24,28},{28,24},{1,5},{5... | collective-permute-start | bytes 393224 | tf_op jit(solution)/shard_map/ppermute | solution.py:411
  96.3 11.3 %collective-permute-start.6 = (f32[2,128,256]{2,1,0:T(8,128)}, f32[2,128,256]{2,1,0:T(8,128)}, u32[]{:S(2)}, u32[]{:S(2)}) collective-permute-start(f32[2,128,256]{2,1,0:T(8,128)} %pad_maximum_fusion.1), channel_id=1, source_target_pairs={{0,16},{4,20},{8,24},{12,28},{16,0},{20,4},{24,8},{28,12},{1,17},{... | collective-permute-start | bytes 786440 | tf_op jit(solution)/shard_map/ppermute | solution.py:411
  109.4 13.4 %collective-permute-start.7 = (f32[4,128,256]{2,1,0:T(8,128)}, f32[4,128,256]{2,1,0:T(8,128)}, u32[]{:S(2)}, u32[]{:S(2)}) collective-permute-start(f32[4,128,256]{2,1,0:T(8,128)} %pad_maximum_fusion), channel_id=1, source_target_pairs={{0,8},{4,12},{8,0},{12,4},{16,24},{20,28},{24,16},{28,20},{1,9},{5... | collective-permute-start | bytes 1572872 | tf_op jit(solution)/shard_map/ppermute | solution.py:411
  110.9 11.8 %copy-start.28 = (s32[14,4]{0,1:T(4,128)S(1)}, s32[14,4]{0,1:T(4,128)}, u32[]{:S(2)}) copy-start(s32[14,4]{0,1:T(4,128)} %param.17) | copy-start | bytes 676
  110.9 11.9 %copy-start.27 = (s32[6,256]{1,0:T(8,128)S(1)}, s32[6,256]{1,0:T(8,128)}, u32[]{:S(2)}) copy-start(s32[6,256]{1,0:T(8,128)} %param.16) | copy-start | bytes 18436
  115.6 35.1 %collective-permute-start.16 = (f32[256,1024]{1,0:T(8,128)}, f32[256,1024]{1,0:T(8,128)}, u32[]{:S(2)}, u32[]{:S(2)}) collective-permute-start(f32[256,1024]{1,0:T(8,128)} %get-tuple-element.28), channel_id=1, source_target_pairs={{1,0},{0,1},{3,2},{2,3},{5,4},{4,5},{7,6},{6,7},{9,8},{8,9},{11,10... | collective-permute-start | bytes 3145736 | tf_op jit(solution)/shard_map/ppermute | solution.py:365
  122.6 28.1 %collective-permute-start.18 = (f32[256,1024]{1,0:T(8,128)S(1)}, f32[256,1024]{1,0:T(8,128)S(1)}, u32[]{:S(2)}, u32[]{:S(2)}) collective-permute-start(f32[256,1024]{1,0:T(8,128)S(1)} %add.56), channel_id=1, source_target_pairs={{2,0},{3,1},{0,2},{1,3},{6,4},{7,5},{4,6},{5,7},{10,8},{11,9},{8,1... | collective-permute-start | bytes 3145736 | tf_op jit(solution)/shard_map/ppermute | solution.py:428
  122.8 27.9 %copy-start.2 = (f32[2,512,256]{2,1,0:T(8,128)S(1)}, f32[2,512,256]{2,1,0:T(8,128)}, u32[]{:S(2)}) copy-start(f32[2,512,256]{2,1,0:T(8,128)} %interp_ref.3) | copy-start | bytes 3145732
  131.2 17.6 %collective-permute-start.8 = (f32[64,256]{1,0:T(8,128)S(1)}, f32[64,256]{1,0:T(8,128)S(1)}, u32[]{:S(2)}, u32[]{:S(2)}) collective-permute-start(f32[64,256]{1,0:T(8,128)S(1)} %shard_map.93.refs_0_), channel_id=1, source_target_pairs={{2,0},{3,1},{0,2},{1,3},{6,4},{7,5},{4,6},{5,7},{10,8},{11,9},{8,1... | collective-permute-start | bytes 196616 | tf_op jit(solution)/shard_map/ppermute | solution.py:365
  148.8 1.9 %collective-permute-start.9 = (f32[2,64,256]{2,1,0:T(8,128)S(1)}, f32[2,64,256]{2,1,0:T(8,128)S(1)}, u32[]{:S(2)}, u32[]{:S(2)}) collective-permute-start(f32[2,64,256]{2,1,0:T(8,128)S(1)} %pad_maximum_fusion.2), channel_id=1, source_target_pairs={{1,0},{0,1},{3,2},{2,3},{5,4},{4,5},{7,6},{6,7},{9,8},{8,9},{11,10... | collective-permute-start | bytes 393224 | tf_op jit(solution)/shard_map/ppermute | solution.py:365
  (24 other events, 55.5 us)

commit v2 on v1

v2 whole, which is shorter than its diff:
```python
import math
from functools import partial

import jax
import jax.numpy as jnp
from jax import lax
from jax.experimental import pallas as pl
from jax.experimental.pallas import tpu as pltpu
from jax.sharding import PartitionSpec as P

F = 64
R = 256
LEAF = 512
SK = 256
FL = 4
EXTRA = 8

BF = jnp.bfloat16
F32 = jnp.float32
LOG2E = 1.0 / math.log(2.0)
SCALE = math.sqrt(0.5 * LOG2E)
BIAS = 0.0625 * F * LOG2E
VMEM_LIMIT = 24 * 1024 * 1024


def dot(a, b):
    return jnp.dot(a, b, preferred_element_type=F32)


def dot_t(a, b):
    return lax.dot_general(a, b, (((1,), (1,)), ((), ())), preferred_element_type=F32)


def halves(x):
    hi = x.astype(BF)
    lo = (x - hi.astype(F32)).astype(BF)
    return hi, lo


def dot3(a, b, mul=dot):
    a_hi, a_lo = halves(a)
    b_hi, b_lo = halves(b)
    return mul(a_hi, b_hi) + mul(a_lo, b_hi) + mul(a_hi, b_lo)


def target_side(x):
    hi, lo = halves(x)
    both = hi.astype(F32) + lo.astype(F32)
    off = BIAS - 0.5 * jnp.sum(both * both, axis=0, keepdims=True)
    return jnp.concatenate([hi, lo, hi, lo], axis=0), off


def source_side(x):
    xt = x.T
    hi, lo = halves(xt)
    both = hi.astype(F32) + lo.astype(F32)
    off = BIAS - 0.5 * jnp.sum(both * both, axis=1, keepdims=True)
    return jnp.concatenate([hi, hi, lo, lo], axis=1), off


def near_body(nblk, nset, nchunk, rows, acc_row, mult_ref, *refs):
    tiles_of = 4 * nset * nblk
    t_refs = refs[: 2 * nblk]
    at = 2 * nblk
    s_refs = refs[at : at + nset * (2 + nchunk)]
    at += nset * (2 + nchunk)
    acc_refs = refs[at : at + nblk] if acc_row is not None else ()
    outs = refs[-9 - nblk : -9]
    t_scr, tb_scr, s_scr, sb_scr, w_scr, o_scr, kh_scr, kl_scr, list_ref = refs[-9:]
    each = rows // nchunk
    for b in range(nblk):
        for leaf in range(2):
            cols = slice(leaf * LEAF, (leaf + 1) * LEAF)
            t_scr[2 * b + leaf] = t_refs[2 * b][leaf]
            tb_scr[2 * b + leaf] = t_refs[2 * b + 1][leaf]
            if acc_refs:
                o_scr[2 * b + leaf] = acc_refs[b][acc_row : acc_row + rows, cols]
            else:
                o_scr[2 * b + leaf] = jnp.zeros((rows, LEAF), F32)
    for k in range(nset):
        side_ref, off_ref = s_refs[k * (2 + nchunk) : k * (2 + nchunk) + 2]
        chunks = s_refs[k * (2 + nchunk) + 2 : (k + 1) * (2 + nchunk)]
        for leaf in range(2):
            cols = slice(leaf * LEAF, (leaf + 1) * LEAF)
            j = 2 * k + leaf
            s_scr[j] = side_ref[leaf]
            sb_scr[j] = off_ref[leaf]
            for c in range(nchunk):
                hi, lo = halves(chunks[c][:, cols])
                w_scr[j, c * each : (c + 1) * each, :] = hi
                w_scr[j, rows + c * each : rows + (c + 1) * each, :] = lo

    def collect(n, count):
        @pl.when(mult_ref[n] > 0)
        def _():
            list_ref[count] = n

        return count + (mult_ref[n] > 0).astype(jnp.int32)

    list_ref[0] = 0
    count = lax.fori_loop(0, tiles_of, collect, jnp.int32(0))

    def block(index, slot):
        n = list_ref[jnp.minimum(index, jnp.maximum(count - 1, 0))]
        t, j = n // (2 * nset), n % (2 * nset)
        side = t_scr[t]
        off = tb_scr[t][:1, :]
        for half in range(2):
            part = slice(half * 256, (half + 1) * 256)
            cross = dot(s_scr[j, part, :], side)
            src_off = sb_scr[j, part, :]
            src_off = jnp.concatenate([src_off] * (LEAF // 128), axis=1)
            k_hi, k_lo = halves(jnp.exp2(cross + src_off + off))
            kh_scr[slot, part, :] = k_hi
            kl_scr[slot, part, :] = k_lo

    def apply(index, slot):
        n = list_ref[index]
        t, j = n // (2 * nset), n % (2 * nset)
        factor = mult_ref[n].astype(F32)
        for half in range(2):
            cols = slice(half * 256, (half + 1) * 256)
            both = dot(w_scr[j], kh_scr[slot, :, cols])
            low = dot(w_scr[j, :rows, :], kl_scr[slot, :, cols])
            o_scr[t, :, cols] = o_scr[t, :, cols] + factor * (both[:rows] + both[rows:] + low)

    @pl.when(count > 0)
    def _():
        block(0, 0)

    def pair(index, carry):
        block(2 * index + 1, 1)
        apply(2 * index, 0)

        @pl.when(2 * index + 1 < count)
        def _():
            block(2 * index + 2, 0)
            apply(2 * index + 1, 1)

        return carry

    lax.fori_loop(0, (count + 1) // 2, pair, jnp.int32(0))
    for b in range(nblk):
        for leaf in range(2):
            outs[b][:, leaf * LEAF : (leaf + 1) * LEAF] = o_scr[2 * b + leaf]


def near_call(name, mult, targets, sources, rows, acc=None, acc_row=None, after=()):
    nblk, nset, nchunk = len(targets), len(sources), len(sources[0]) - 2
    cols = 2 * LEAF
    vmem = pl.BlockSpec(memory_space=pltpu.VMEM)
    operands = [a for t in targets for a in t] + [a for s in sources for a in s]
    operands += list(acc) if acc is not None else []
    return pl.pallas_call(
        partial(near_body, nblk, nset, nchunk, rows, acc_row),
        name=name,
        out_shape=[jax.ShapeDtypeStruct((rows, cols), F32)] * nblk,
        in_specs=[pl.BlockSpec(memory_space=pltpu.SMEM)]
        + [vmem] * len(operands)
        + [pl.BlockSpec(memory_space=pl.ANY)] * len(after),
        out_specs=[vmem] * nblk,
        scratch_shapes=[
            pltpu.VMEM((2 * nblk, 4 * F, LEAF), BF),
            pltpu.VMEM((2 * nblk, 8, LEAF), F32),
            pltpu.VMEM((2 * nset, LEAF, 4 * F), BF),
            pltpu.VMEM((2 * nset, LEAF, 128), F32),
            pltpu.VMEM((2 * nset, 2 * rows, LEAF), BF),
            pltpu.VMEM((2 * nblk, rows, LEAF), F32),
            pltpu.VMEM((2, LEAF, LEAF), BF),
            pltpu.VMEM((2, LEAF, LEAF), BF),
            pltpu.SMEM((4 * nset * nblk,), jnp.int32),
        ],
        compiler_params=pltpu.CompilerParams(vmem_limit_bytes=VMEM_LIMIT),
    )(mult, *operands, *after)


def source_body(pts_ref, side_ref, off_ref):
    for leaf in range(2):
        cols = slice(leaf * LEAF, (leaf + 1) * LEAF)
        side, off = source_side(pts_ref[:, cols] * SCALE)
        side_ref[leaf] = side
        off_ref[leaf] = jnp.broadcast_to(off, (LEAF, 128))


def source_call(pts):
    vmem = pl.BlockSpec(memory_space=pltpu.VMEM)
    return pl.pallas_call(
        source_body,
        name="source_side",
        out_shape=[
            jax.ShapeDtypeStruct((2, LEAF, 4 * F), BF),
            jax.ShapeDtypeStruct((2, LEAF, 128), F32),
        ],
        in_specs=[vmem],
        out_specs=[vmem, vmem],
        compiler_params=pltpu.CompilerParams(vmem_limit_bytes=VMEM_LIMIT),
    )(pts)


def up_body(xs, pos_ref, w_ref, interp_ref, keep_ref, give_ref, scr):
    total = jnp.zeros((R, SK), F32)
    for leaf in range(2):
        total = total + dot3(w_ref[:, leaf * LEAF : (leaf + 1) * LEAF], interp_ref[leaf])
    scr[...] = total
    rows = R // (2 * xs)
    x, core = pos_ref[0], pos_ref[1]
    for dx in range(xs):
        there = 2 * lax.rem(x + dx, xs)
        keep_ref[dx] = scr[pl.ds(pl.multiple_of((there + core) * rows, rows), rows), :]
        give_ref[dx] = scr[pl.ds(pl.multiple_of((there + 1 - core) * rows, rows), rows), :]


def up_call(xs, pos, weights, interp):
    rows = R // (2 * xs)
    vmem = pl.BlockSpec(memory_space=pltpu.VMEM)
    return pl.pallas_call(
        partial(up_body, xs),
        name="leaf_up",
        out_shape=[jax.ShapeDtypeStruct((xs, rows, SK), F32)] * 2,
        in_specs=[pl.BlockSpec(memory_space=pltpu.SMEM), vmem, vmem],
        out_specs=[vmem, vmem],
        scratch_shapes=[pltpu.VMEM((R, SK), F32)],
        compiler_params=pltpu.CompilerParams(vmem_limit_bytes=VMEM_LIMIT),
    )(pos, weights, interp)


def skel_body(xs, nsum, base_ref, index_ref, same_ref, mate_ref, *refs):
    nblk = 2 * xs
    sums = refs[:nsum]
    out_ref = refs[nsum]
    sides = refs[nsum + 1 :]
    cols = 2 * LEAF
    total = jnp.zeros((2 * F, SK), F32)
    spot = lax.broadcasted_iota(jnp.int32, (cols, SK), 0)
    for b in range(nblk):
        pts = (same_ref, mate_ref)[b % 2][b // 2, :F, :] * SCALE
        side, off = target_side(pts)
        for leaf in range(2):
            part = slice(leaf * LEAF, (leaf + 1) * LEAF)
            sides[2 * b][leaf] = side[:, part]
            sides[2 * b + 1][leaf] = jnp.broadcast_to(off[:, part], (8, LEAF))
        hot = spot + base_ref[b] == index_ref[...]
        total = total + dot(side[: 2 * F], hot.astype(F32).astype(BF))
    out_ref[:F, :] = total[:F] + total[F:]
    value = sums[0][...]
    for ref in sums[1:]:
        value = value + ref[...]
    out_ref[F:, :] = value


def skel_call(xs, bases, index, same, mate, sums):
    rows = R // (2 * xs)
    nblk = 2 * xs
    vmem = pl.BlockSpec(memory_space=pltpu.VMEM)
    side = [
        jax.ShapeDtypeStruct((2, 4 * F, LEAF), BF),
        jax.ShapeDtypeStruct((2, 8, LEAF), F32),
    ]
    out = pl.pallas_call(
        partial(skel_body, xs, len(sums)),
        name="skeleton",
        out_shape=[jax.ShapeDtypeStruct((F + rows, SK), F32)] + side * nblk,
        in_specs=[pl.BlockSpec(memory_space=pltpu.SMEM)] + [vmem] * (3 + len(sums)),
        out_specs=[vmem] * (1 + 2 * nblk),
        compiler_params=pltpu.CompilerParams(vmem_limit_bytes=VMEM_LIMIT),
    )(bases, index, same, mate, *sums)
    return out[0], [(out[1 + 2 * b], out[2 + 2 * b]) for b in range(nblk)]


def upper_start(level, groups):
    return sum((groups >> step for step in range(1, level)))


def list_start(level, groups):
    return sum((groups >> step for step in range(level)))


def far_body(groups, rows, steps, pos_ref, far_ref, node_ref, transfer_ref, *refs):
    pieces = refs[: len(steps) + 1]
    out_ref, p_scr, u_scr, f_scr = refs[-4:]
    levels = groups.bit_length() - 1
    group = pos_ref[2]
    start = [sum(groups >> step for step in range(level)) for level in range(levels)]
    held = [0]
    p_scr[0] = pieces[0][:F, :]
    u_scr[0] = pieces[0][F:, :]
    for piece, step in zip(pieces[1:], steps):
        for at, mask in enumerate(held):
            p_scr[mask ^ step] = piece[at, :F, :]
            u_scr[mask ^ step] = piece[at, F:, :]
        held = held + [mask ^ step for mask in held]
    spot = lax.broadcasted_iota(jnp.int32, (2 * SK, SK), 0)
    for level in range(1, levels):
        bit = (group >> (level - 1)) & 1
        for m in range(groups >> level):
            row = upper_start(level, groups) + (m ^ (group >> level))
            left = start[level - 1] + 2 * m + bit
            right = start[level - 1] + 2 * m + 1 - bit
            hot = (spot == node_ref[row]).astype(F32).astype(BF)
            pts = jnp.concatenate([p_scr[left], p_scr[right]], axis=1)
            hi, lo = halves(pts)
            both = dot(jnp.concatenate([hi, lo], axis=0), hot)
            p_scr[start[level] + m] = both[:F] + both[F:]
            vals = jnp.concatenate([u_scr[left], u_scr[right]], axis=1)
            u_scr[start[level] + m] = dot3(vals, transfer_ref[row])
    for level in range(levels):
        node = group >> level
        side, off = target_side(p_scr[start[level]])
        f_scr[level] = jnp.zeros((rows, SK), F32)

        def one(m, carry, level=level, node=node, side=side, off=off):
            hits = jnp.int32(0)
            for slot in range(FL):
                entry = far_ref[list_start(level, groups) + node, slot]
                hits = hits + (entry == (m ^ node)).astype(jnp.int32)

            @pl.when(hits > 0)
            def _():
                src, src_off = source_side(p_scr[start[level] + m])
                block = jnp.exp2(dot(src, side) + src_off + off)
                term = dot3(u_scr[start[level] + m], block)
                f_scr[level] = f_scr[level] + hits.astype(F32) * term

            return carry

        lax.fori_loop(0, groups >> level, one, jnp.int32(0))
    local = f_scr[levels - 1]
    for level in range(levels - 1, 0, -1):
        row = upper_start(level, groups) + (group >> level)
        bit = (group >> (level - 1)) & 1
        matrix = transfer_ref[row, pl.ds(pl.multiple_of(bit * SK, SK), SK), :]
        local = f_scr[level - 1] + dot3(local, matrix, dot_t)
    out_ref[...] = local


def far_call(groups, pos, far_nodes, skel_node, transfer, pieces, steps, after=()):
    rows = pieces[0].shape[0] - F
    vmem = pl.BlockSpec(memory_space=pltpu.VMEM)
    smem = pl.BlockSpec(memory_space=pltpu.SMEM)
    nodes = 2 * groups
    return pl.pallas_call(
        partial(far_body, groups, rows, steps),
        name="far",
        out_shape=jax.ShapeDtypeStruct((rows, SK), F32),
        in_specs=[smem, smem, vmem, vmem]
        + [vmem] * len(pieces)
        + [pl.BlockSpec(memory_space=pl.ANY)] * len(after),
        out_specs=vmem,
        scratch_shapes=[
            pltpu.VMEM((nodes, F, SK), F32),
            pltpu.VMEM((nodes, rows, SK), F32),
            pltpu.VMEM((groups.bit_length(), rows, SK), F32),
        ],
        compiler_params=pltpu.CompilerParams(vmem_limit_bytes=VMEM_LIMIT),
    )(pos, far_nodes, skel_node[:, None, :], transfer, *pieces, *after)


def final_body(xs, pos_ref, interp_ref, home_ref, mate_ref, *refs):
    same = refs[:xs]
    v_mate = refs[xs]
    parts = refs[xs + 1 : -2]
    out_ref, v_scr = refs[-2:]
    rows = R // (2 * xs)
    x, core = pos_ref[0], pos_ref[1]
    for dx in range(xs):
        there = 2 * lax.rem(x + dx, xs)
        v_scr[pl.ds(pl.multiple_of((there + core) * rows, rows), rows), :] = same[dx][...]
        v_scr[pl.ds(pl.multiple_of((there + 1 - core) * rows, rows), rows), :] = v_mate[dx]
    value = v_scr[...]
    for leaf in range(2):
        cols = slice(leaf * LEAF, (leaf + 1) * LEAF)
        total = dot3(value, interp_ref[leaf], dot_t)
        out_ref[:, cols] = total + home_ref[:, cols] + mate_ref[:, cols]
    for n, ref in enumerate(parts):
        part = slice(n % 2 * (R // 2), (n % 2 + 1) * (R // 2))
        out_ref[part, :] = out_ref[part, :] + ref[...]


def final_call(xs, pos, interp, home, mate, same, v_mate, parts):
    vmem = pl.BlockSpec(memory_space=pltpu.VMEM)
    return pl.pallas_call(
        partial(final_body, xs),
        name="join",
        out_shape=jax.ShapeDtypeStruct((R, 2 * LEAF), F32),
        in_specs=[pl.BlockSpec(memory_space=pltpu.SMEM)] + [vmem] * (3 + xs + 1 + len(parts)),
        out_specs=vmem,
        scratch_shapes=[pltpu.VMEM((R, SK), F32)],
        compiler_params=pltpu.CompilerParams(vmem_limit_bytes=VMEM_LIMIT),
    )(pos, interp, home, mate, *same, v_mate, *parts)


def help_pairs(xs, dx, dc):
    return [
        (2 * ((x + dx) % xs) + (core ^ dc), 2 * x + core) for x in range(xs) for core in range(2)
    ]


def shards(
    points, weights, interp, transfer, near_count, near_src, skel_group, skel_node, far_nodes
):
    helpers = lax.axis_size("help")
    groups = lax.axis_size("leaf")
    xs = helpers // 2
    helper = lax.axis_index("help")
    group = lax.axis_index("leaf")
    x, core = helper // 2, helper % 2
    leaves = 2 * helpers
    pos = jnp.stack([x, core, group]).astype(jnp.int32)
    nchunk = 2

    def from_help(value, dx, dc):
        return lax.ppermute(value, "help", help_pairs(xs, dx, dc))

    beside = [(i, i ^ 1) for i in range(groups)]
    across = [(i, i + 2) for i in range(0, groups - 2, 2)]
    across += [(i, i - 2) for i in range(3, groups, 2)]

    slots = near_src.shape[1]
    relative = near_src - (group - 1) * leaves
    used = lax.broadcasted_iota(jnp.int32, near_src.shape, 1) < near_count[0][:, None]
    names = lax.broadcasted_iota(jnp.int32, (2, slots, 3 * leaves), 2)
    times = jnp.sum(((relative[:, :, None] == names) & used[:, :, None]).astype(F32), axis=1)
    times = times.reshape(2, 3, leaves)
    even = group % 2 == 0
    before, own, after = times[:, 0], times[:, 1], times[:, 2]
    times = jnp.stack([own, jnp.where(even, after, before), jnp.where(even, before, after)], axis=1)
    flat = times.reshape(1, 6 * leaves)
    flat = jnp.pad(flat, ((0, EXTRA - 1), (0, points.shape[1] - 6 * leaves)))
    packed = jnp.concatenate([points, flat], axis=0)

    rows = R // nchunk
    w_own = [weights[c * rows : (c + 1) * rows] for c in range(nchunk)]
    pts_y = lax.ppermute(points, "leaf", beside)
    w_y = [lax.ppermute(chunk, "leaf", beside) for chunk in w_own]

    order = [(dx, dc) for dx in range(xs) for dc in range(2)]
    packed, w_own = lax.optimization_barrier((packed, w_own))
    same = jnp.stack([packed] + [from_help(packed, dx, 0) for dx in range(1, xs)])
    mate = from_help(same, 0, 1)
    keep, give = up_call(xs, pos, weights, interp)
    half = keep + from_help(give, 0, 1)
    sums = [half[0]] + [
        lax.ppermute(half[dx], "help", help_pairs(xs, -dx, 0)) for dx in range(1, xs)
    ]

    mult = jnp.stack([same[:, F, : 6 * leaves], mate[:, F, : 6 * leaves]], axis=1)
    mult = mult.reshape(helpers, 2, 3, helpers, 2)
    mult = lax.dynamic_index_in_dim(mult, helper, 3, keepdims=False).astype(jnp.int32)

    def mult_of(blocks, sets):
        return mult[blocks][:, :, sets].reshape(-1)

    bases = jnp.stack([(2 * ((x + dx) % xs) + (core ^ dc)) for dx, dc in order]) * (2 * LEAF)
    payload, targets = skel_call(xs, bases.astype(jnp.int32), skel_group, same, mate, sums)
    home, away = slice(0, 2), slice(2, None)
    own_src = (*source_call(points), *w_own)
    y_src = (*source_call(pts_y), *w_y)

    pts_z = lax.ppermute(pts_y, "leaf", across)
    z_side = source_call(pts_z)

    n0a = near_call("near_own_away", mult_of(away, slice(0, 1)), targets[away], [own_src], R)
    w_y[0], n0a = lax.optimization_barrier((w_y[0], n0a))
    w_z = [lax.ppermute(w_y[0], "leaf", across)]
    n0h = near_call(
        "near_own_home", mult_of(home, slice(0, 1)), targets[home], [own_src], R, after=n0a[:1]
    )
    w_y[1], n0h = lax.optimization_barrier((w_y[1], n0h))
    w_z.append(lax.ppermute(w_y[1], "leaf", across))

    steps = [1 << k for k in range(groups.bit_length() - 1)][::-1]
    pieces = [payload]
    held = payload[None]
    for step in steps:
        got = lax.ppermute(held, "leaf", [(i, i ^ step) for i in range(groups)])
        pieces.append(got)
        held = jnp.concatenate([held, got], axis=0)

    n1a = near_call(
        "near_pair_away", mult_of(away, slice(1, 2)), targets[away], [y_src], R, n0a, 0,
        after=n0h[:1],
    )
    n1h = near_call(
        "near_pair_home", mult_of(home, slice(1, 2)), targets[home], [y_src], R, n0h, 0,
        after=n1a[:1],
    )
    m2a = mult_of(away, slice(2, 3))
    last = n1h[:1]
    parts = []
    for c in range(nchunk):
        blocks = near_call(
            "near_next_away", m2a, targets[away], [(*z_side, w_z[c])], rows, n1a, c * rows,
            after=last,
        )
        part = [
            blocks[2 * dx - 2] + from_help(blocks[2 * dx - 1], 0, 1) for dx in range(1, xs)
        ]
        parts.append(
            [lax.ppermute(part[dx - 1], "help", help_pairs(xs, -dx, 0)) for dx in range(1, xs)]
        )
        last = part[:1]
        if c == 0:
            v_own = far_call(
                groups, pos, far_nodes, skel_node, transfer, pieces, steps, after=last
            )
            last = [v_own]
            v_same = [v_own] + [from_help(v_own, dx, 0) for dx in range(1, xs)]
            v_mate = from_help(jnp.stack(v_same), 0, 1)
    n2h = near_call(
        "near_next_home", mult_of(home, slice(2, 3)), targets[home], [(*z_side, *w_z)], R, n1h, 0,
        after=last,
    )
    flat_parts = [parts[c][dx] for dx in range(xs - 1) for c in range(nchunk)]
    return final_call(
        xs, pos, interp, n2h[0], from_help(n2h[1], 0, 1), v_same, v_mate, flat_parts
    )


def solution(mesh):
    placed = (
        P(None, ("leaf", "help")),
        P(None, ("leaf", "help")),
        P(("leaf", "help"), None, None),
        P(),
        P("leaf", "help"),
        P(("leaf", "help"), None),
        P("leaf", None),
        P(),
        P(),
    )
    return jax.shard_map(
        shards, mesh=mesh, in_specs=placed, out_specs=P(None, ("leaf", "help")), check_vma=False
    )
```

time: 155 us -> 181 us (1.17)
  the two profiles are of different devices: /device:TPU:9 before, /device:TPU:25 now
where the time goes in v2:
time: 181 us; the launch traced here: 178 us
  waiting for transfers between devices  57.2 us (32%)
  Pallas kernels  48 us (27%)
  local copies, waits for them, and re-layouts  32.5 us (18%)
  starting transfers between devices  29.4 us (16%)
  other arithmetic  10.4 us (6%)
    ppermute x8, waiting for transfers between devices, from_help(): return lax.ppermute(value, 'help', help_pairs(xs, dx, dc))  33.5 us
    pallas_call x7, Pallas kernels, near_call(): pl.pallas_call(partial(near_body, nblk, nset, nchunk, rows, acc_row), nam...  32.6 us
    unnamed x114, local copies, waits for them, and re-layouts  26.6 us
    ppermute x3, waiting for transfers between devices, shards(): got = lax.ppermute(held, 'leaf', [(i, i ^ step) for i in range(groups)])  16.5 us
    ppermute x8, starting transfers between devices, from_help(): return lax.ppermute(value, 'help', help_pairs(xs, dx, dc))  15.7 us
    ppermute x1, waiting for transfers between devices, shards(): pts_y = lax.ppermute(points, 'leaf', beside)  7.16 us
    pallas_call x1, Pallas kernels, far_call(): pl.pallas_call(partial(far_body, groups, rows, steps), name='far', out_sh...  6.51 us
    ppermute x3, starting transfers between devices, shards(): got = lax.ppermute(held, 'leaf', [(i, i ^ step) for i in range(groups)])  4.29 us
  transfers between devices with their start and end apart: 20, of which 7 were waited for; matrix products, arithmetic and copies ran while one was open for 5% of the time, Pallas kernels for 20%

profile of v2, /device:TPU:25, one launch (start us, length us, event | category | flops | bytes accessed | tf_op | source)
XLA Modules:
  0.0 178.2 jit_solution(14189218386729052903)
XLA Ops:
  5.4 6.8 %collective-permute-done = f32[72,1024]{1,0:T(8,128)} collective-permute-done((f32[72,1024]{1,0:T(8,128)S(1)}, f32[72,1024]{1,0:T(8,128)}, u32[]{:S(2)}, u32[]{:S(2)}) %collective-permute-start) | collective-permute-done | bytes 294944 | tf_op jit(solution)/shard_map/ppermute | solution.py:412
  12.2 1.8 %pad_maximum_fusion.same_ref = f32[2,72,1024]{2,1,0:T(8,128)} fusion(f32[1,72,1024]{2,1,0:T(8,128)} %bitcast.5, f32[1,72,1024]{2,1,0:T(8,128)S(1)} %bitcast.36), kind=kLoop, calls=%fused_computation.1 | loop fusion | flops 147456 | bytes 1179648 | tf_op jit(solution)/shard_map/stack | solution.py:438
  14.0 1.5 collective-permute-start.1
  19.6 1.5 source_side.4
  26.7 2.0 %skeleton.1 = (f32[128,256]{1,0:T(8,128)S(1)}, bf16[2,256,512]{2,1,0:T(8,128)(2,1)S(1)}, f32[2,8,512]{2,1,0:T(8,128)S(1)}, bf16[2,256,512]{2,1,0:T(8,128)(2,1)S(...) custom-call(s32[4]{0:T(128)S(1)} %add_multiply_fusion.base_ref, ...), custom_call_target="tpu_custom_call" | custom-call | tf_op jit(solution)/shard_map/skeleton/pallas_call | solution.py:259
  30.8 2.3 %near_own_away.1 = (f32[256,1024]{1,0:T(8,128)S(1)}, f32[256,1024]{1,0:T(8,128)S(1)}) custom-call(s32[8]{0:T(128)S(1)} %reshape.55.mult_ref, bf16[2,256,512]{2,1,0:T(8,128)(2,1)S(1)} %get-tuple-element.54.refs_0_, f32[2,8,512]{2,1,0:T(8,128)S(1)} %get-tuple-element.55.refs_1_, bf16[2,256,512]{2,1,0:T(8,128)(2,1)S(1)} %get-tuple-element.56.refs_2_, ...), custom_call_target="tpu_custom_call" | custom-call | tf_op jit(solution)/shard_map/near_own_away/pallas_call | solution.py:154
  35.5 4.3 %collective-permute-start.10 = (f32[1,128,256]{2,1,0:T(8,128)S(1)}, f32[1,128,256]{2,1,0:T(8,128)S(1)}, u32[]{:S(2)}, u32[]{:S(2)}) collective-permute-start(f32[1,128,256]{2,1,0:T(8,128)S(1)} %bitcast.31), channel_id=1, source_target_pairs={{0,16},{4,20},{8,24},{12,28},{16,0},{20,4},{24,8},{28,12},{1,17},{... | collective-permute-start | bytes 393224 | tf_op jit(solution)/shard_map/ppermute | solution.py:475
  39.8 7.2 %collective-permute-done.4.pts_ref = f32[64,1024]{1,0:T(8,128)} collective-permute-done((f32[64,1024]{1,0:T(8,128)}, f32[64,1024]{1,0:T(8,128)}, u32[]{:S(2)}, u32[]{:S(2)}) %collective-permute-start.4) | collective-permute-done | bytes 262176 | tf_op jit(solution)/shard_map/ppermute | solution.py:433
  48.2 5.8 %collective-permute-done.10.refs_1_ = f32[1,128,256]{2,1,0:T(8,128)S(1)} collective-permute-done((f32[1,128,256]{2,1,0:T(8,128)S(1)}, f32[1,128,256]{2,1,0:T(8,128)S(1)}, u32[]{:S(2)}, u32[]{:S(2)}) %collective-permute-start.10) | collective-permute-done | bytes 131104 | tf_op jit(solution)/shard_map/ppermute | solution.py:475
  54.7 1.5 source_side.5
  64.7 5.4 %near_own_home.1 = (f32[256,1024]{1,0:T(8,128)S(1)}, f32[256,1024]{1,0:T(8,128)S(1)}) custom-call(s32[8]{0:T(128)S(1)} %reshape.56.mult_ref, bf16[2,256,512]{2,1,0:T(8,128)(2,1)S(1)} %get-tuple-element.48.refs_0_, f32[2,8,512]{2,1,0:T(8,128)S(1)} %get-tuple-element.49.refs_1_, bf16[2,256,512]{2,1,0:T(8,128)(2,1)S(1)} %get-tuple-element.50.refs_2_, ...), custom_call_target="tpu_custom_call" | custom-call | tf_op jit(solution)/shard_map/near_own_home/pallas_call | solution.py:154
  79.1 3.2 %near_pair_away.1 = (f32[256,1024]{1,0:T(8,128)S(1)}, f32[256,1024]{1,0:T(8,128)S(1)}) custom-call(s32[8]{0:T(128)S(1)} %reshape.58.mult_ref, bf16[2,256,512]{2,1,0:T(8,128)(2,1)S(1)} %get-tuple-element.54.refs_0_, f32[2,8,512]{2,1,0:T(8,128)S(1)} %get-tuple-element.55.refs_1_, bf16[2,256,512]{2,1,0:T(8,128)(2,1)S(1)} %get-tuple-element.56.refs_2_, ...), custom_call_target="tpu_custom_call" | custom-call | tf_op jit(solution)/shard_map/near_pair_away/pallas_call | solution.py:154
  82.4 5.8 %near_pair_home.1 = (f32[256,1024]{1,0:T(8,128)S(1)}, f32[256,1024]{1,0:T(8,128)S(1)}) custom-call(s32[8]{0:T(128)S(1)} %reshape.57.mult_ref, bf16[2,256,512]{2,1,0:T(8,128)(2,1)S(1)} %get-tuple-element.48.refs_0_, f32[2,8,512]{2,1,0:T(8,128)S(1)} %get-tuple-element.49.refs_1_, bf16[2,256,512]{2,1,0:T(8,128)(2,1)S(1)} %get-tuple-element.50.refs_2_, ...), custom_call_target="tpu_custom_call" | custom-call | tf_op jit(solution)/shard_map/near_pair_home/pallas_call | solution.py:154
  88.3 5.9 %near_next_away.2 = (f32[128,1024]{1,0:T(8,128)S(1)}, f32[128,1024]{1,0:T(8,128)}) custom-call(s32[8]{0:T(128)S(1)} %reshape.59.mult_ref, bf16[2,256,512]{2,1,0:T(8,128)(2,1)S(1)} %get-tuple-element.54.refs_0_, f32[2,8,512]{2,1,0:T(8,128)S(1)} %get-tuple-element.55.refs_1_, bf16[2,256,512]{2,1,0:T(8,128)(2,1)S(1)} %get-tuple-element.56.refs_2_, ...), custom_call_target="tpu_custom_call" | custom-call | tf_op jit(solution)/shard_map/near_next_away/pallas_call | solution.py:154
  94.1 10.3 %collective-permute-start.13 = (f32[128,1024]{1,0:T(8,128)}, f32[128,1024]{1,0:T(8,128)}, u32[]{:S(2)}, u32[]{:S(2)}) collective-permute-start(f32[128,1024]{1,0:T(8,128)} %get-tuple-element.80), channel_id=1, source_target_pairs={{1,0},{0,1},{3,2},{2,3},{5,4},{4,5},{7,6},{6,7},{9,8},{8,9},{11,10... | collective-permute-start | bytes 1572872 | tf_op jit(solution)/shard_map/ppermute | solution.py:412
  104.5 1.8 %pad_maximum_fusion.1 = f32[4,128,256]{2,1,0:T(8,128)} fusion(f32[2,128,256]{2,1,0:T(8,128)} %collective-permute-done.11.refs_2_, f32[1,128,256]{2,1,0:T(8,128)S(1)} %collective-permute-done.10.refs_1_, f32[1,128,256]{2,1,0:T(8,128)S(1)} %bitcast.33), kind=kLoop, calls=%fused_computation.3 | loop fusion | flops 262144 | bytes 1048576 | tf_op jit(solution)/shard_map/concatenate | solution.py:477
  109.2 10.8 %collective-permute-done.12.refs_3_ = f32[4,128,256]{2,1,0:T(8,128)} collective-permute-done((f32[4,128,256]{2,1,0:T(8,128)}, f32[4,128,256]{2,1,0:T(8,128)}, u32[]{:S(2)}, u32[]{:S(2)}) %collective-permute-start.12) | collective-permute-done | bytes 524320 | tf_op jit(solution)/shard_map/ppermute | solution.py:475
  120.0 1.9 %copy-done.21 = f32[6,512,256]{2,1,0:T(8,128)S(1)} copy-done((f32[6,512,256]{2,1,0:T(8,128)S(1)}, f32[6,512,256]{2,1,0:T(8,128)}, u32[]{:S(2)}) %copy-start.21) | copy-done | bytes 3145752
  121.8 6.5 %far.1.refs_9_.refs_0_ = f32[64,256]{1,0:T(8,128)S(1)} custom-call(s32[3]{0:T(128)S(1)} %pad_add_fusion.pos_ref, s32[14,4]{1,0:T(8,128)S(1)} %copy.41.far_ref, s32[6,1,256]{2,1,0:T(1,128)S(1)} %broadcast_in_dim.8.node_ref, f32[6,512,256]{2,1,0:T(8,128)S(1)} %copy-done.21, f32[128,256]{1,0:T(8,128)S(1)} %get-tuple-element.78.refs_0_, ...), custom_call_target="tpu_custom_call" | custom-call | tf_op jit(solution)/shard_map/far/pallas_call | solution.py:341
  128.4 5.4 %near_next_away.3 = (f32[128,1024]{1,0:T(8,128)S(1)}, f32[128,1024]{1,0:T(8,128)}) custom-call(s32[8]{0:T(128)S(1)} %reshape.59.mult_ref, bf16[2,256,512]{2,1,0:T(8,128)(2,1)S(1)} %get-tuple-element.54.refs_0_, f32[2,8,512]{2,1,0:T(8,128)S(1)} %get-tuple-element.55.refs_1_, bf16[2,256,512]{2,1,0:T(8,128)(2,1)S(1)} %get-tuple-element.56.refs_2_, ...), custom_call_target="tpu_custom_call" | custom-call | tf_op jit(solution)/shard_map/near_next_away/pallas_call | solution.py:154
  135.9 1.6 collective-permute-done.14
  143.1 4.6 %near_next_home.1 = (f32[256,1024]{1,0:T(8,128)S(1)}, f32[256,1024]{1,0:T(8,128)S(1)}) custom-call(s32[8]{0:T(128)S(1)} %reshape.54.mult_ref, bf16[2,256,512]{2,1,0:T(8,128)(2,1)S(1)} %get-tuple-element.48.refs_0_, f32[2,8,512]{2,1,0:T(8,128)S(1)} %copy-done.45, bf16[2,256,512]{2,1,0:T(8,128)(2,1)S(1)} %get-tuple-element.50.refs_2_, ...), custom_call_target="tpu_custom_call" | custom-call | tf_op jit(solution)/shard_map/near_next_home/pallas_call | solution.py:154
  149.4 24.2 %collective-permute-done.16.refs_1_ = f32[64,256]{1,0:T(8,128)S(1)} collective-permute-done((f32[64,256]{1,0:T(8,128)S(1)}, f32[64,256]{1,0:T(8,128)S(1)}, u32[]{:S(2)}, u32[]{:S(2)}) %collective-permute-start.16) | collective-permute-done | bytes 65568 | tf_op jit(solution)/shard_map/ppermute | solution.py:412
  175.9 2.2 %join.1 = f32[256,1024]{1,0:T(8,128)} custom-call(s32[3]{0:T(128)S(1)} %pad_add_fusion.pos_ref, f32[2,512,256]{2,1,0:T(8,128)S(1)} %copy-done.18, f32[256,1024]{1,0:T(8,128)S(1)} %get-tuple-element.83.home_ref, f32[256,1024]{1,0:T(8,128)S(1)} %collective-permute-done.15.mate_ref, f32[64,256]{1,0:T(8,128)S(1)} %far.1.refs_9_.refs_0_, ...), custom_call_target="tpu_custom_call" | custom-call | tf_op jit(solution)/shard_map/join/pallas_call | solution.py:381
  (183 shorter events, 53.4 us)
Async XLA Ops:
  4.1 8.0 %collective-permute-start = (f32[72,1024]{1,0:T(8,128)S(1)}, f32[72,1024]{1,0:T(8,128)}, u32[]{:S(2)}, u32[]{:S(2)}) collective-permute-start(f32[72,1024]{1,0:T(8,128)S(1)} %select_maximum_fusion), channel_id=1, source_target_pairs={{2,0},{3,1},{0,2},{1,3},{6,4},{7,5},{4,6},{5,7},{10,8},{11,9},{8,1... | collective-permute-start | bytes 884744 | tf_op jit(solution)/shard_map/ppermute | solution.py:412
  14.0 10.8 %collective-permute-start.1 = (f32[2,72,1024]{2,1,0:T(8,128)}, f32[2,72,1024]{2,1,0:T(8,128)}, u32[]{:S(2)}, u32[]{:S(2)}) collective-permute-start(f32[2,72,1024]{2,1,0:T(8,128)} %pad_maximum_fusion.same_ref), channel_id=1, source_target_pairs={{1,0},{0,1},{3,2},{2,3},{5,4},{4,5},{7,6},{6,7},{9,8},{8,9},{11,10... | collective-permute-start | bytes 1769480 | tf_op jit(solution)/shard_map/ppermute | solution.py:412
  16.8 6.0 %collective-permute-start.2 = (f32[2,64,256]{2,1,0:T(8,128)S(1)}, f32[2,64,256]{2,1,0:T(8,128)S(1)}, u32[]{:S(2)}, u32[]{:S(2)}) collective-permute-start(f32[2,64,256]{2,1,0:T(8,128)S(1)} %get-tuple-element.47), channel_id=1, source_target_pairs={{1,0},{0,1},{3,2},{2,3},{5,4},{4,5},{7,6},{6,7},{9,8},{8,9},{11,10... | collective-permute-start | bytes 393224 | tf_op jit(solution)/shard_map/ppermute | solution.py:412
  16.9 17.3 %collective-permute-start.6 = (f32[128,1024]{1,0:T(8,128)S(1)}, f32[128,1024]{1,0:T(8,128)}, u32[]{:S(2)}, u32[]{:S(2)}) collective-permute-start(f32[128,1024]{1,0:T(8,128)S(1)} %get-tuple-element.60.refs_6_), channel_id=1, source_target_pairs={{0,4},{4,0},{8,12},{12,8},{16,20},{20,16},{24,28},{28,24},{1,5},{5... | collective-permute-start | bytes 1572872 | tf_op jit(solution)/shard_map/ppermute | solution.py:434
  18.2 54.0 %collective-permute-start.8 = (f32[128,1024]{1,0:T(8,128)S(1)}, f32[128,1024]{1,0:T(8,128)}, u32[]{:S(2)}, u32[]{:S(2)}) collective-permute-start(f32[128,1024]{1,0:T(8,128)S(1)} %get-tuple-element.61.refs_7_), channel_id=1, source_target_pairs={{0,4},{4,0},{8,12},{12,8},{16,20},{20,16},{24,28},{28,24},{1,5},{5... | collective-permute-start | bytes 1572872 | tf_op jit(solution)/shard_map/ppermute | solution.py:434
  18.4 28.6 %collective-permute-start.4 = (f32[64,1024]{1,0:T(8,128)}, f32[64,1024]{1,0:T(8,128)}, u32[]{:S(2)}, u32[]{:S(2)}) collective-permute-start(f32[64,1024]{1,0:T(8,128)} %pts_ref.1), channel_id=1, source_target_pairs={{0,4},{4,0},{8,12},{12,8},{16,20},{20,16},{24,28},{28,24},{1,5},{5... | collective-permute-start | bytes 786440 | tf_op jit(solution)/shard_map/ppermute | solution.py:433
  22.9 3.8 %collective-permute-start.3 = (f32[64,256]{1,0:T(8,128)S(1)}, f32[64,256]{1,0:T(8,128)S(1)}, u32[]{:S(2)}, u32[]{:S(2)}) collective-permute-start(f32[64,256]{1,0:T(8,128)S(1)} %get-tuple-element.87), channel_id=1, source_target_pairs={{2,0},{3,1},{0,2},{1,3},{6,4},{7,5},{4,6},{5,7},{10,8},{11,9},{8,1... | collective-permute-start | bytes 196616 | tf_op jit(solution)/shard_map/ppermute | solution.py:443
  28.7 53.6 %copy-start.44 = (f32[2,8,512]{2,1,0:T(8,128)}, f32[2,8,512]{2,1,0:T(8,128)S(1)}, u32[]{:S(2)}) copy-start(f32[2,8,512]{2,1,0:T(8,128)S(1)} %get-tuple-element.49.refs_1_) | copy-start | bytes 98308
  28.7 53.6 %copy-start.46 = (f32[2,8,512]{2,1,0:T(8,128)}, f32[2,8,512]{2,1,0:T(8,128)S(1)}, u32[]{:S(2)}) copy-start(f32[2,8,512]{2,1,0:T(8,128)S(1)} %get-tuple-element.51.refs_3_) | copy-start | bytes 98308
  34.2 37.9 %copy-start.53 = (s32[2,2,1,2]{0,3,2,1:T(2,128)S(1)}, s32[2,2,1,2]{0,3,2,1:T(2,128)}, u32[]{:S(2)}) copy-start(s32[2,2,1,2]{0,3,2,1:T(2,128)} %get-tuple-element.90) | copy-start | bytes 100
  34.2 39.0 %copy-start.52 = (s32[2,2,1,2]{0,3,2,1:T(2,128)S(1)}, s32[2,2,1,2]{0,3,2,1:T(2,128)}, u32[]{:S(2)}) copy-start(s32[2,2,1,2]{0,3,2,1:T(2,128)} %get-tuple-element.89) | copy-start | bytes 100
  34.2 54.0 %collective-permute-start.7 = (f32[128,1024]{1,0:T(8,128)}, f32[128,1024]{1,0:T(8,128)}, u32[]{:S(2)}, u32[]{:S(2)}) collective-permute-start(f32[128,1024]{1,0:T(8,128)} %collective-permute-done.6.refs_6_), channel_id=1, source_target_pairs={{0,8},{8,16},{16,24},{12,4},{20,12},{28,20},{1,9},{9,17},{17,25},{... | collective-permute-start | bytes 1572872 | tf_op jit(solution)/shard_map/ppermute | solution.py:464
  35.5 18.5 %collective-permute-start.10 = (f32[1,128,256]{2,1,0:T(8,128)S(1)}, f32[1,128,256]{2,1,0:T(8,128)S(1)}, u32[]{:S(2)}, u32[]{:S(2)}) collective-permute-start(f32[1,128,256]{2,1,0:T(8,128)S(1)} %bitcast.31), channel_id=1, source_target_pairs={{0,16},{4,20},{8,24},{12,28},{16,0},{20,4},{24,8},{28,12},{1,17},{... | collective-permute-start | bytes 393224 | tf_op jit(solution)/shard_map/ppermute | solution.py:475
  46.9 10.9 %collective-permute-start.5 = (f32[64,1024]{1,0:T(8,128)}, f32[64,1024]{1,0:T(8,128)S(1)}, u32[]{:S(2)}, u32[]{:S(2)}) collective-permute-start(f32[64,1024]{1,0:T(8,128)} %collective-permute-done.4.pts_ref), channel_id=1, source_target_pairs={{0,8},{8,16},{16,24},{12,4},{20,12},{28,20},{1,9},{9,17},{17,25},{... | collective-permute-start | bytes 786440 | tf_op jit(solution)/shard_map/ppermute | solution.py:459
  54.7 49.8 %collective-permute-start.11 = (f32[2,128,256]{2,1,0:T(8,128)}, f32[2,128,256]{2,1,0:T(8,128)}, u32[]{:S(2)}, u32[]{:S(2)}) collective-permute-start(f32[2,128,256]{2,1,0:T(8,128)} %pad_maximum_fusion.2), channel_id=1, source_target_pairs={{0,8},{4,12},{8,0},{12,4},{16,24},{20,28},{24,16},{28,20},{1,9},{5... | collective-permute-start | bytes 786440 | tf_op jit(solution)/shard_map/ppermute | solution.py:475
  94.1 13.6 %collective-permute-start.13 = (f32[128,1024]{1,0:T(8,128)}, f32[128,1024]{1,0:T(8,128)}, u32[]{:S(2)}, u32[]{:S(2)}) collective-permute-start(f32[128,1024]{1,0:T(8,128)} %get-tuple-element.80), channel_id=1, source_target_pairs={{1,0},{0,1},{3,2},{2,3},{5,4},{4,5},{7,6},{6,7},{9,8},{8,9},{11,10... | collective-permute-start | bytes 1572872 | tf_op jit(solution)/shard_map/ppermute | solution.py:412
  106.3 13.7 %collective-permute-start.12 = (f32[4,128,256]{2,1,0:T(8,128)}, f32[4,128,256]{2,1,0:T(8,128)}, u32[]{:S(2)}, u32[]{:S(2)}) collective-permute-start(f32[4,128,256]{2,1,0:T(8,128)} %pad_maximum_fusion.1), channel_id=1, source_target_pairs={{0,4},{4,0},{8,12},{12,8},{16,20},{20,16},{24,28},{28,24},{1,5},{5... | collective-permute-start | bytes 1572872 | tf_op jit(solution)/shard_map/ppermute | solution.py:475
  106.3 22.1 %collective-permute-start.9 = (f32[128,1024]{1,0:T(8,128)}, f32[128,1024]{1,0:T(8,128)}, u32[]{:S(2)}, u32[]{:S(2)}) collective-permute-start(f32[128,1024]{1,0:T(8,128)} %collective-permute-done.8.refs_7_), channel_id=1, source_target_pairs={{0,8},{8,16},{16,24},{12,4},{20,12},{28,20},{1,9},{9,17},{17,25},{... | collective-permute-start | bytes 1572872 | tf_op jit(solution)/shard_map/ppermute | solution.py:469
  134.7 2.8 %collective-permute-start.14 = (f32[128,1024]{1,0:T(8,128)}, f32[128,1024]{1,0:T(8,128)S(1)}, u32[]{:S(2)}, u32[]{:S(2)}) collective-permute-start(f32[128,1024]{1,0:T(8,128)} %get-tuple-element.82), channel_id=1, source_target_pairs={{1,0},{0,1},{3,2},{2,3},{5,4},{4,5},{7,6},{6,7},{9,8},{8,9},{11,10... | collective-permute-start | bytes 1572872 | tf_op jit(solution)/shard_map/ppermute | solution.py:412
  147.7 28.2 %collective-permute-start.15 = (f32[256,1024]{1,0:T(8,128)S(1)}, f32[256,1024]{1,0:T(8,128)S(1)}, u32[]{:S(2)}, u32[]{:S(2)}) collective-permute-start(f32[256,1024]{1,0:T(8,128)S(1)} %get-tuple-element.84), channel_id=1, source_target_pairs={{1,0},{0,1},{3,2},{2,3},{5,4},{4,5},{7,6},{6,7},{9,8},{8,9},{11,10... | collective-permute-start | bytes 3145736 | tf_op jit(solution)/shard_map/ppermute | solution.py:412
  147.8 28.1 %collective-permute-start.18 = (f32[128,1024]{1,0:T(8,128)S(1)}, f32[128,1024]{1,0:T(8,128)S(1)}, u32[]{:S(2)}, u32[]{:S(2)}) collective-permute-start(f32[128,1024]{1,0:T(8,128)S(1)} %copy-done.35), channel_id=1, source_target_pairs={{2,0},{3,1},{0,2},{1,3},{6,4},{7,5},{4,6},{5,7},{10,8},{11,9},{8,1... | collective-permute-start | bytes 1572872 | tf_op jit(solution)/shard_map/ppermute | solution.py:499
  147.9 28.0 %collective-permute-start.19 = (f32[128,1024]{1,0:T(8,128)S(1)}, f32[128,1024]{1,0:T(8,128)S(1)}, u32[]{:S(2)}, u32[]{:S(2)}) collective-permute-start(f32[128,1024]{1,0:T(8,128)S(1)} %add.60.refs_10_), channel_id=1, source_target_pairs={{2,0},{3,1},{0,2},{1,3},{6,4},{7,5},{4,6},{5,7},{10,8},{11,9},{8,1... | collective-permute-start | bytes 1572872 | tf_op jit(solution)/shard_map/ppermute | solution.py:499
  149.3 24.2 %collective-permute-start.16 = (f32[64,256]{1,0:T(8,128)S(1)}, f32[64,256]{1,0:T(8,128)S(1)}, u32[]{:S(2)}, u32[]{:S(2)}) collective-permute-start(f32[64,256]{1,0:T(8,128)S(1)} %far.1.refs_9_.refs_0_), channel_id=1, source_target_pairs={{2,0},{3,1},{0,2},{1,3},{6,4},{7,5},{4,6},{5,7},{10,8},{11,9},{8,1... | collective-permute-start | bytes 196616 | tf_op jit(solution)/shard_map/ppermute | solution.py:412
  173.6 2.3 %collective-permute-start.17 = (f32[2,64,256]{2,1,0:T(8,128)S(1)}, f32[2,64,256]{2,1,0:T(8,128)S(1)}, u32[]{:S(2)}, u32[]{:S(2)}) collective-permute-start(f32[2,64,256]{2,1,0:T(8,128)S(1)} %pad_maximum_fusion.3), channel_id=1, source_target_pairs={{1,0},{0,1},{3,2},{2,3},{5,4},{4,5},{7,6},{6,7},{9,8},{8,9},{11,10... | collective-permute-start | bytes 393224 | tf_op jit(solution)/shard_map/ppermute | solution.py:412
  (52 other events, 412.0 us)

commit v3 on v2

v3 whole, which is shorter than its diff:
```python
import math
from functools import partial

import jax
import jax.numpy as jnp
from jax import lax
from jax.experimental import pallas as pl
from jax.experimental.pallas import tpu as pltpu
from jax.sharding import PartitionSpec as P

F = 64
R = 256
LEAF = 512
SK = 256
FL = 4
EXTRA = 8

BF = jnp.bfloat16
F32 = jnp.float32
LOG2E = 1.0 / math.log(2.0)
SCALE = math.sqrt(0.5 * LOG2E)
BIAS = 0.0625 * F * LOG2E
VMEM_LIMIT = 24 * 1024 * 1024


def dot(a, b):
    return jnp.dot(a, b, preferred_element_type=F32)


def dot_t(a, b):
    return lax.dot_general(a, b, (((1,), (1,)), ((), ())), preferred_element_type=F32)


def halves(x):
    hi = x.astype(BF)
    lo = (x - hi.astype(F32)).astype(BF)
    return hi, lo


def dot3(a, b, mul=dot):
    a_hi, a_lo = halves(a)
    b_hi, b_lo = halves(b)
    return mul(a_hi, b_hi) + mul(a_lo, b_hi) + mul(a_hi, b_lo)


def target_side(x):
    hi, lo = halves(x)
    both = hi.astype(F32) + lo.astype(F32)
    off = BIAS - 0.5 * jnp.sum(both * both, axis=0, keepdims=True)
    return jnp.concatenate([hi, lo, hi, lo], axis=0), off


def source_side(x):
    xt = x.T
    hi, lo = halves(xt)
    both = hi.astype(F32) + lo.astype(F32)
    off = BIAS - 0.5 * jnp.sum(both * both, axis=1, keepdims=True)
    return jnp.concatenate([hi, hi, lo, lo], axis=1), off


def near_body(nblk, kinds, nchunk, rows, acc_row, first, pos_ref, times_ref, *refs):
    nset = len(kinds)
    t_refs = refs[: 2 * nblk]
    at = 2 * nblk
    s_refs = refs[at : at + nset * (1 + nchunk)]
    at += nset * (1 + nchunk)
    acc_refs = refs[at : at + nblk] if acc_row is not None else ()
    outs = refs[-8 - nblk : -8]
    t_scr, tb_scr, s_scr, sb_scr, w_scr, o_scr, k_scr, list_ref = refs[-8:]
    each = rows // nchunk
    for b in range(nblk):
        for leaf in range(2):
            cols = slice(leaf * LEAF, (leaf + 1) * LEAF)
            t_scr[2 * b + leaf] = t_refs[2 * b][leaf]
            tb_scr[2 * b + leaf] = t_refs[2 * b + 1][leaf]
            if acc_refs:
                o_scr[2 * b + leaf] = acc_refs[b][acc_row : acc_row + rows, cols]
            else:
                o_scr[2 * b + leaf] = jnp.zeros((rows, LEAF), F32)
    for k in range(nset):
        pts_ref = s_refs[k * (1 + nchunk)]
        chunks = s_refs[k * (1 + nchunk) + 1 : (k + 1) * (1 + nchunk)]
        for leaf in range(2):
            cols = slice(leaf * LEAF, (leaf + 1) * LEAF)
            j = 2 * k + leaf
            side, off = source_side(pts_ref[:F, cols] * SCALE)
            s_scr[j] = side
            sb_scr[j] = jnp.broadcast_to(off, (LEAF, 128))
            for c in range(nchunk):
                hi, lo = halves(chunks[c][:, cols])
                w_scr[j, c * each : (c + 1) * each, :] = hi
                w_scr[j, rows + c * each : rows + (c + 1) * each, :] = lo

    x, core, group, leaves = pos_ref[0], pos_ref[1], pos_ref[2], pos_ref[3]
    odd = group % 2
    column = []
    for kind in kinds:
        relative = {"own": 1, "pair": 2 - 2 * odd, "next": 2 * odd}[kind]
        column.append(relative * leaves + 2 * (2 * x + core))

    count = jnp.int32(0)
    list_ref[0] = 0
    for t in range(2 * nblk):
        for j in range(2 * nset):
            times = times_ref[(2 * first + t) * 128 + column[j // 2] + j % 2]

            @pl.when(times > 0)
            def _(count=count, t=t, j=j, times=times):
                list_ref[count] = (times * 64 + t) * 8 + j

            count = count + (times > 0).astype(jnp.int32)

    def entry(index):
        code = list_ref[index]
        return (code >> 3) & 63, code & 7, (code >> 9).astype(F32)

    def block(index, slot):
        t, j, _ = entry(jnp.minimum(index, jnp.maximum(count - 1, 0)))
        side = t_scr[t]
        off = tb_scr[t][:1, :]
        for half in range(2):
            part = slice(half * 256, (half + 1) * 256)
            cross = dot(s_scr[j, part, :], side)
            src_off = sb_scr[j, part, :]
            src_off = jnp.concatenate([src_off] * (LEAF // 128), axis=1)
            k_hi, k_lo = halves(jnp.exp2(cross + src_off + off))
            k_scr[slot, part, :] = k_hi
            k_scr[slot, LEAF + half * 256 : LEAF + (half + 1) * 256, :] = k_lo

    def apply(index, slot):
        t, j, factor = entry(index)
        for half in range(2):
            cols = slice(half * 256, (half + 1) * 256)
            both = dot(w_scr[j], k_scr[slot, :LEAF, cols])
            low = dot(w_scr[j, :rows, :], k_scr[slot, LEAF:, cols])
            o_scr[t, :, cols] = o_scr[t, :, cols] + factor * (both[:rows] + both[rows:] + low)

    @pl.when(count > 0)
    def _():
        block(0, 0)

    def pair(index, carry):
        block(2 * index + 1, 1)
        apply(2 * index, 0)

        @pl.when(2 * index + 1 < count)
        def _():
            block(2 * index + 2, 0)
            apply(2 * index + 1, 1)

        return carry

    lax.fori_loop(0, (count + 1) // 2, pair, jnp.int32(0))
    for b in range(nblk):
        for leaf in range(2):
            outs[b][:, leaf * LEAF : (leaf + 1) * LEAF] = o_scr[2 * b + leaf]


def near_call(name, where, targets, first, sources, rows, acc=None, acc_row=None, after=()):
    nblk, nchunk = len(targets), len(next(iter(sources.values()))) - 1
    nset = len(sources)
    cols = 2 * LEAF
    vmem = pl.BlockSpec(memory_space=pltpu.VMEM)
    smem = pl.BlockSpec(memory_space=pltpu.SMEM)
    operands = [a for t in targets for a in t] + [a for s in sources.values() for a in s]
    operands += list(acc) if acc is not None else []
    return pl.pallas_call(
        partial(near_body, nblk, tuple(sources), nchunk, rows, acc_row, first),
        name=name,
        out_shape=[jax.ShapeDtypeStruct((rows, cols), F32)] * nblk,
        in_specs=[smem, smem]
        + [vmem] * len(operands)
        + [pl.BlockSpec(memory_space=pl.ANY)] * len(after),
        out_specs=[vmem] * nblk,
        scratch_shapes=[
            pltpu.VMEM((2 * nblk, 4 * F, LEAF), BF),
            pltpu.VMEM((2 * nblk, 8, LEAF), F32),
            pltpu.VMEM((2 * nset, LEAF, 4 * F), BF),
            pltpu.VMEM((2 * nset, LEAF, 128), F32),
            pltpu.VMEM((2 * nset, 2 * rows, LEAF), BF),
            pltpu.VMEM((2 * nblk, rows, LEAF), F32),
            pltpu.VMEM((2, 2 * LEAF, LEAF), BF),
            pltpu.SMEM((4 * nset * nblk,), jnp.int32),
        ],
        compiler_params=pltpu.CompilerParams(vmem_limit_bytes=VMEM_LIMIT),
    )(*where, *operands, *after)


def share_rows(xs):
    return R // (2 * xs) * SK // (2 * LEAF)


def leaf_body(xs, pos_ref, count_ref, src_ref, pts_ref, w_ref, interp_ref, *refs):
    msgs, scr = refs[:-1], refs[-1]
    total = jnp.zeros((R, SK), F32)
    for leaf in range(2):
        total = total + dot3(w_ref[:, leaf * LEAF : (leaf + 1) * LEAF], interp_ref[leaf])
    scr[...] = total
    x, core, group, leaves = pos_ref[0], pos_ref[1], pos_ref[2], pos_ref[3]
    slots = src_ref.shape[0]
    name = lax.broadcasted_iota(jnp.int32, (slots, 128), 1) + (group - 1) * leaves
    slot = lax.broadcasted_iota(jnp.int32, (slots, 128), 0)
    times = []
    for leaf in range(2):
        hit = (src_ref[:, leaf : leaf + 1] == name) & (slot < count_ref[0, leaf])
        times.append(jnp.sum(hit.astype(F32), axis=0, keepdims=True))
    times = jnp.concatenate(times + [jnp.zeros((EXTRA - 2, 128), F32)], axis=0)
    rows = R // (2 * xs)
    tall = share_rows(xs)
    for n, msg in enumerate(msgs):
        helper = 2 * lax.rem(x + n // 2, xs) + (core if n % 2 == 0 else 1 - core)
        msg[:F, :] = pts_ref[...]
        msg[F : F + EXTRA, :] = jnp.zeros((EXTRA, 2 * LEAF), F32)
        msg[F : F + EXTRA, :128] = times
        for i in range(rows // tall):
            at = pl.multiple_of(helper * rows + i * tall, tall)
            msg[F + EXTRA :, i * SK : (i + 1) * SK] = scr[pl.ds(at, tall), :]


def leaf_call(xs, pos, near_count, near_src, points, weights, interp):
    vmem = pl.BlockSpec(memory_space=pltpu.VMEM)
    smem = pl.BlockSpec(memory_space=pltpu.SMEM)
    height = F + EXTRA + share_rows(xs)
    return pl.pallas_call(
        partial(leaf_body, xs),
        name="leaf_up",
        out_shape=[jax.ShapeDtypeStruct((height, 2 * LEAF), F32)] * (2 * xs),
        in_specs=[smem, smem, vmem, vmem, vmem, vmem],
        out_specs=[vmem] * (2 * xs),
        scratch_shapes=[pltpu.VMEM((R, SK), F32)],
        compiler_params=pltpu.CompilerParams(vmem_limit_bytes=VMEM_LIMIT),
    )(pos, near_count, near_src.T, points, weights, interp)


def skel_body(xs, pos_ref, index_ref, *refs):
    nblk = 2 * xs
    msgs = refs[:nblk]
    out_ref = refs[nblk]
    sides = refs[nblk + 1 :]
    rows = R // nblk
    tall = share_rows(xs)
    total = jnp.zeros((2 * F, SK), F32)
    value = jnp.zeros((tall, 2 * LEAF), F32)
    spot = lax.broadcasted_iota(jnp.int32, (2 * LEAF, SK), 0)
    x, core = pos_ref[0], pos_ref[1]
    for b in range(nblk):
        helper = 2 * lax.rem(x + b // 2, xs) + (core if b % 2 == 0 else 1 - core)
        side, off = target_side(msgs[b][:F, :] * SCALE)
        for leaf in range(2):
            part = slice(leaf * LEAF, (leaf + 1) * LEAF)
            sides[2 * b][leaf] = side[:, part]
            sides[2 * b + 1][leaf] = jnp.broadcast_to(off[:, part], (8, LEAF))
        hot = spot + helper * (2 * LEAF) == index_ref[...]
        total = total + dot(side[: 2 * F], hot.astype(F32).astype(BF))
        value = value + msgs[b][F + EXTRA :, :]
    out_ref[:F, :] = total[:F] + total[F:]
    for i in range(rows // tall):
        out_ref[F + i * tall : F + (i + 1) * tall, :] = value[:, i * SK : (i + 1) * SK]


def skel_call(xs, pos, index, msgs):
    rows = R // (2 * xs)
    nblk = 2 * xs
    vmem = pl.BlockSpec(memory_space=pltpu.VMEM)
    side = [
        jax.ShapeDtypeStruct((2, 4 * F, LEAF), BF),
        jax.ShapeDtypeStruct((2, 8, LEAF), F32),
    ]
    out = pl.pallas_call(
        partial(skel_body, xs),
        name="skeleton",
        out_shape=[jax.ShapeDtypeStruct((F + rows, SK), F32)] + side * nblk,
        in_specs=[pl.BlockSpec(memory_space=pltpu.SMEM)] + [vmem] * (1 + nblk),
        out_specs=[vmem] * (1 + 2 * nblk),
        compiler_params=pltpu.CompilerParams(vmem_limit_bytes=VMEM_LIMIT),
    )(pos, index, *msgs)
    return out[0], [(out[1 + 2 * b], out[2 + 2 * b]) for b in range(nblk)]


def upper_start(level, groups):
    return sum((groups >> step for step in range(1, level)))


def list_start(level, groups):
    return sum((groups >> step for step in range(level)))


def far_body(groups, rows, pos_ref, far_ref, node_ref, transfer_ref, *refs):
    pieces, beside = refs[: groups // 2], refs[groups // 2]
    out_ref, p_scr, u_scr, f_scr = refs[-4:]
    levels = groups.bit_length() - 1
    group = pos_ref[2]
    start = [sum(groups >> step for step in range(level)) for level in range(levels)]
    for n, piece in enumerate(pieces):
        p_scr[2 * n] = piece[:F, :]
        u_scr[2 * n] = piece[F:, :]
        p_scr[2 * n + 1] = beside[n, :F, :]
        u_scr[2 * n + 1] = beside[n, F:, :]
    spot = lax.broadcasted_iota(jnp.int32, (2 * SK, SK), 0)
    for level in range(1, levels):
        bit = (group >> (level - 1)) & 1
        for m in range(groups >> level):
            row = upper_start(level, groups) + (m ^ (group >> level))
            left = start[level - 1] + 2 * m + bit
            right = start[level - 1] + 2 * m + 1 - bit
            hot = (spot == node_ref[row]).astype(F32).astype(BF)
            pts = jnp.concatenate([p_scr[left], p_scr[right]], axis=1)
            hi, lo = halves(pts)
            both = dot(jnp.concatenate([hi, lo], axis=0), hot)
            p_scr[start[level] + m] = both[:F] + both[F:]
            vals = jnp.concatenate([u_scr[left], u_scr[right]], axis=1)
            u_scr[start[level] + m] = dot3(vals, transfer_ref[row])
    for level in range(levels):
        node = group >> level
        side, off = target_side(p_scr[start[level]])
        f_scr[level] = jnp.zeros((rows, SK), F32)

        def one(m, carry, level=level, node=node, side=side, off=off):
            hits = jnp.int32(0)
            for slot in range(FL):
                entry = far_ref[list_start(level, groups) + node, slot]
                hits = hits + (entry == (m ^ node)).astype(jnp.int32)

            @pl.when(hits > 0)
            def _():
                src, src_off = source_side(p_scr[start[level] + m])
                block = jnp.exp2(dot(src, side) + src_off + off)
                term = dot3(u_scr[start[level] + m], block)
                f_scr[level] = f_scr[level] + hits.astype(F32) * term

            return carry

        lax.fori_loop(0, groups >> level, one, jnp.int32(0))
    local = f_scr[levels - 1]
    for level in range(levels - 1, 0, -1):
        row = upper_start(level, groups) + (group >> level)
        bit = (group >> (level - 1)) & 1
        matrix = transfer_ref[row, pl.ds(pl.multiple_of(bit * SK, SK), SK), :]
        local = f_scr[level - 1] + dot3(local, matrix, dot_t)
    out_ref[...] = local


def far_call(groups, pos, far_nodes, skel_node, transfer, pieces, beside, after):
    rows = pieces[0].shape[0] - F
    vmem = pl.BlockSpec(memory_space=pltpu.VMEM)
    smem = pl.BlockSpec(memory_space=pltpu.SMEM)
    nodes = 2 * groups
    return pl.pallas_call(
        partial(far_body, groups, rows),
        name="far",
        out_shape=jax.ShapeDtypeStruct((rows, SK), F32),
        in_specs=[smem, smem, vmem, vmem]
        + [vmem] * (len(pieces) + 1)
        + [pl.BlockSpec(memory_space=pl.ANY)] * len(after),
        out_specs=vmem,
        scratch_shapes=[
            pltpu.VMEM((nodes, F, SK), F32),
            pltpu.VMEM((nodes, rows, SK), F32),
            pltpu.VMEM((groups.bit_length(), rows, SK), F32),
        ],
        compiler_params=pltpu.CompilerParams(vmem_limit_bytes=VMEM_LIMIT),
    )(pos, far_nodes, skel_node[:, None, :], transfer, *pieces, beside, *after)


def final_body(xs, pos_ref, interp_ref, home_ref, mate_ref, *refs):
    values = refs[: 2 * xs]
    out_ref, v_scr = refs[-2:]
    rows = R // (2 * xs)
    x, core = pos_ref[0], pos_ref[1]
    for n, ref in enumerate(values):
        helper = 2 * lax.rem(x + n // 2, xs) + (core if n % 2 == 0 else 1 - core)
        v_scr[pl.ds(pl.multiple_of(helper * rows, rows), rows), :] = ref[...]
    value = v_scr[...]
    for leaf in range(2):
        cols = slice(leaf * LEAF, (leaf + 1) * LEAF)
        total = dot3(value, interp_ref[leaf], dot_t)
        out_ref[:, cols] = total + home_ref[:, cols] + mate_ref[:, cols]


def add_body(value_ref, *refs):
    out_ref = refs[-1]
    rows = R // 2
    count = (len(refs) - 1) // 2
    for c in range(2):
        part = slice(c * rows, (c + 1) * rows)
        total = value_ref[part, :]
        for ref in refs[c * count : (c + 1) * count]:
            total = total + ref[...]
        out_ref[part, :] = total


def add_call(value, parts):
    vmem = pl.BlockSpec(memory_space=pltpu.VMEM)
    operands = [value] + parts[0] + parts[1]
    return pl.pallas_call(
        add_body,
        name="add_parts",
        out_shape=jax.ShapeDtypeStruct(value.shape, F32),
        in_specs=[vmem] * len(operands),
        out_specs=vmem,
        compiler_params=pltpu.CompilerParams(vmem_limit_bytes=VMEM_LIMIT),
    )(*operands)


def final_call(xs, pos, interp, home, mate, values):
    vmem = pl.BlockSpec(memory_space=pltpu.VMEM)
    return pl.pallas_call(
        partial(final_body, xs),
        name="join",
        out_shape=jax.ShapeDtypeStruct((R, 2 * LEAF), F32),
        in_specs=[pl.BlockSpec(memory_space=pltpu.SMEM)] + [vmem] * (3 + 2 * xs),
        out_specs=vmem,
        scratch_shapes=[pltpu.VMEM((R, SK), F32)],
        compiler_params=pltpu.CompilerParams(vmem_limit_bytes=VMEM_LIMIT),
    )(pos, interp, home, mate, *values)


def help_pairs(xs, dx, dc):
    return [
        (2 * ((x + dx) % xs) + (core ^ dc), 2 * x + core) for x in range(xs) for core in range(2)
    ]


def shards(
    points, weights, interp, transfer, near_count, near_src, skel_group, skel_node, far_nodes
):
    helpers = lax.axis_size("help")
    groups = lax.axis_size("leaf")
    xs = helpers // 2
    helper = lax.axis_index("help")
    group = lax.axis_index("leaf")
    x, core = helper // 2, helper % 2
    leaves = 2 * helpers
    pos = jnp.stack([x, core, group, jnp.int32(leaves)]).astype(jnp.int32)
    rows = R // 2

    def from_help(value, dx, dc):
        return lax.ppermute(value, "help", help_pairs(xs, dx, dc))

    def to_help(value, dx):
        return lax.ppermute(value, "help", help_pairs(xs, -dx, 0))

    def together(*values):
        return lax.optimization_barrier(values)

    beside = [(i, i ^ 1) for i in range(groups)]
    across = [(i, i + 2) for i in range(0, groups - 2, 2)]
    across += [(i, i - 2) for i in range(3, groups, 2)]
    order = [(dx, dc) for dx in range(xs) for dc in range(2)]

    pts_y = lax.ppermute(points, "leaf", beside)
    msgs = leaf_call(xs, pos, near_count, near_src, points, weights, interp)
    w_own = [weights[:rows], weights[rows:]]
    got = [lax.ppermute(msgs[n], "help", help_pairs(xs, -dx, dc)) for n, (dx, dc) in enumerate(order) if n]
    w_y = [lax.ppermute(chunk, "leaf", beside) for chunk in w_own]

    pts_y, got = together(pts_y, got)
    pts_z = lax.ppermute(pts_y, "leaf", across)
    blocks = [msgs[0]] + [got[order.index((-dx % xs, dc)) - 1] for dx, dc in order[1:]]
    times = jnp.stack([block[F : F + 2, :128] for block in blocks]).astype(jnp.int32).reshape(-1)
    where = (pos, times)
    payload, targets = skel_call(xs, pos, skel_group, blocks)
    home, away = slice(0, 2), slice(2, None)

    pieces = [payload]
    for mask in range(2, groups, 2):
        pieces.append(lax.ppermute(payload, "leaf", [(i, i ^ mask) for i in range(groups)]))
    n0 = near_call("near_own", where, targets, 0, {"own": (points, *w_own)}, R)
    w_z = [lax.ppermute(w_y[0], "leaf", across)]
    w_y = list(together(*w_y))
    w_z.append(lax.ppermute(w_y[1], "leaf", across))
    pieces, w_y = together(pieces, w_y)
    side = lax.ppermute(jnp.stack(pieces), "leaf", beside)

    n1 = near_call("near_pair", where, targets, 0, {"pair": (pts_y, *w_y)}, R, n0, 0)
    sums = []
    for c in range(2):
        source = {"next": (pts_z, w_z[c])}
        part = near_call(
            "near_next_away", where, targets[away], 2, source, rows, n1[away], c * rows
        )
        kept, given = part[::2], part[1::2]
        sums.append((kept, [from_help(value, 0, 1) for value in given]))
    parts = []
    for c in range(2):
        kept, mates = sums[c]
        if c == 0:
            mates, side, w_z = together(mates, side, w_z)
        both = [k + m for k, m in zip(kept, mates)]
        parts.append([to_help(value, dx + 1) for dx, value in enumerate(both)])
    v_own = far_call(groups, pos, far_nodes, skel_node, transfer, pieces, side, both[:1])
    values = [v_own] + [from_help(v_own, dx, dc) for dx, dc in order[1:]]
    source = {"next": (pts_z, *w_z)}
    n2 = near_call("near_next_home", where, targets[home], 0, source, R, n1[home], 0, [v_own])
    mine = add_call(n2[0], parts)
    return final_call(xs, pos, interp, mine, from_help(n2[1], 0, 1), values)


def solution(mesh):
    placed = (
        P(None, ("leaf", "help")),
        P(None, ("leaf", "help")),
        P(("leaf", "help"), None, None),
        P(),
        P("leaf", "help"),
        P(("leaf", "help"), None),
        P("leaf", None),
        P(),
        P(),
    )
    return jax.shard_map(
        shards, mesh=mesh, in_specs=placed, out_specs=P(None, ("leaf", "help")), check_vma=False
    )
```

time: 181 us -> 140 us (0.77)
  the two profiles are of different devices: /device:TPU:25 before, /device:TPU:15 now
where the time goes in v3:
time: 140 us; the launch traced here: 139 us
  waiting for transfers between devices  51.6 us (37%)
  Pallas kernels  45.8 us (33%)
  starting transfers between devices  21.9 us (16%)
  local copies, waits for them, and re-layouts  16 us (11%)
  other arithmetic  3.51 us (3%)
    pallas_call x5, Pallas kernels, near_call(): pl.pallas_call(partial(near_body, nblk, tuple(sources), nchunk, rows, acc...  34.6 us
    ppermute x2, waiting for transfers between devices, to_help(): return lax.ppermute(value, 'help', help_pairs(xs, -dx, 0))  20.8 us
    ppermute x3, waiting for transfers between devices, shards(): lax.ppermute(msgs[n], 'help', help_pairs(xs, -dx, dc))  16.6 us
    unnamed x64, local copies, waits for them, and re-layouts  14.7 us
    ppermute x1, waiting for transfers between devices, shards(): pts_z = lax.ppermute(pts_y, 'leaf', across)  9.8 us
    pallas_call x1, Pallas kernels, far_call(): pl.pallas_call(partial(far_body, groups, rows), name='far', out_shape=jax...  6.48 us
    ppermute x6, waiting for transfers between devices, from_help(): return lax.ppermute(value, 'help', help_pairs(xs, dx, dc))  4.41 us
    ppermute x3, starting transfers between devices, shards(): lax.ppermute(msgs[n], 'help', help_pairs(xs, -dx, dc))  3.29 us
  transfers between devices with their start and end apart: 21, of which 8 were waited for; matrix products, arithmetic and copies ran while one was open for 4% of the time, Pallas kernels for 23%

profile of v3, /device:TPU:15, one launch (start us, length us, event | category | flops | bytes accessed | tf_op | source)
XLA Modules:
  0.0 139.1 jit_solution(8530236706216328838)
XLA Ops:
  9.2 1.6 %collective-permute-start.1 = (f32[88,1024]{1,0:T(8,128)S(1)}, f32[88,1024]{1,0:T(8,128)S(1)}, u32[]{:S(2)}, u32[]{:S(2)}) collective-permute-start(f32[88,1024]{1,0:T(8,128)S(1)} %get-tuple-element.49), channel_id=1, source_target_pairs={{1,0},{0,1},{3,2},{2,3},{5,4},{4,5},{7,6},{6,7},{9,8},{8,9},{11,10... | collective-permute-start | bytes 1081352 | tf_op jit(solution)/shard_map/ppermute | solution.py:454
  11.0 1.4 %collective-permute-start.3 = (f32[88,1024]{1,0:T(8,128)S(1)}, f32[88,1024]{1,0:T(8,128)S(1)}, u32[]{:S(2)}, u32[]{:S(2)}) collective-permute-start(f32[88,1024]{1,0:T(8,128)S(1)} %get-tuple-element.51), channel_id=1, source_target_pairs={{3,0},{2,1},{1,2},{0,3},{7,4},{6,5},{5,6},{4,7},{11,8},{10,9},{9,1... | collective-permute-start | bytes 1081352 | tf_op jit(solution)/shard_map/ppermute | solution.py:454
  12.5 8.3 %collective-permute-done.2.refs_2_ = f32[88,1024]{1,0:T(8,128)S(1)} collective-permute-done((f32[88,1024]{1,0:T(8,128)S(1)}, f32[88,1024]{1,0:T(8,128)S(1)}, u32[]{:S(2)}, u32[]{:S(2)}) %collective-permute-start.2) | collective-permute-done | bytes 360480 | tf_op jit(solution)/shard_map/ppermute | solution.py:454
  20.7 8.3 %collective-permute-done.3.refs_3_ = f32[88,1024]{1,0:T(8,128)S(1)} collective-permute-done((f32[88,1024]{1,0:T(8,128)S(1)}, f32[88,1024]{1,0:T(8,128)S(1)}, u32[]{:S(2)}, u32[]{:S(2)}) %collective-permute-start.3) | collective-permute-done | bytes 360480 | tf_op jit(solution)/shard_map/ppermute | solution.py:454
  30.6 2.3 %collective-permute-start.8 = (f32[128,256]{1,0:T(8,128)S(1)}, f32[128,256]{1,0:T(8,128)S(1)}, u32[]{:S(2)}, u32[]{:S(2)}) collective-permute-start(f32[128,256]{1,0:T(8,128)S(1)} %get-tuple-element.76.refs_0_), channel_id=1, source_target_pairs={{0,16},{4,20},{8,24},{12,28},{16,0},{20,4},{24,8},{28,12},{1,17},{... | collective-permute-start | bytes 393224 | tf_op jit(solution)/shard_map/ppermute | solution.py:467
  33.9 3.2 %collective-permute-start.13 = (f32[128,1024]{1,0:T(8,128)}, f32[128,1024]{1,0:T(8,128)S(1)}, u32[]{:S(2)}, u32[]{:S(2)}) collective-permute-start(f32[128,1024]{1,0:T(8,128)} %collective-permute-done.10.refs_10_), channel_id=1, source_target_pairs={{0,8},{8,16},{16,24},{12,4},{20,12},{28,20},{1,9},{9,17},{17,25},{... | collective-permute-start | bytes 1572872 | tf_op jit(solution)/shard_map/ppermute | solution.py:471
  37.1 1.9 %collective-permute-start.6 = (f32[128,1024]{1,0:T(8,128)}, f32[128,1024]{1,0:T(8,128)S(1)}, u32[]{:S(2)}, u32[]{:S(2)}) collective-permute-start(f32[128,1024]{1,0:T(8,128)} %copy-done.10), channel_id=1, source_target_pairs={{0,8},{8,16},{16,24},{12,4},{20,12},{28,20},{1,9},{9,17},{17,25},{... | collective-permute-start | bytes 1572872 | tf_op jit(solution)/shard_map/ppermute | solution.py:469
  39.0 1.9 %collective-permute-start.4 = (f32[64,1024]{1,0:T(8,128)}, f32[64,1024]{1,0:T(8,128)S(1)}, u32[]{:S(2)}, u32[]{:S(2)}) collective-permute-start(f32[64,1024]{1,0:T(8,128)} %copy-done.25), channel_id=1, source_target_pairs={{0,8},{8,16},{16,24},{12,4},{20,12},{28,20},{1,9},{9,17},{17,25},{... | collective-permute-start | bytes 786440 | tf_op jit(solution)/shard_map/ppermute | solution.py:458
  41.0 8.5 %near_own.1 = (f32[256,1024]{1,0:T(8,128)S(1)}, f32[256,1024]{1,0:T(8,128)S(1)}, f32[256,1024]{1,0:T(8,128)S(1)}, f32[256,1024]{1,0:T(8,128)S(1)}) custom-call(s32[4]{0:T(128)S(1)} %pad_add_fusion.pos_ref, s32[1024]{0:T(1024)S(1)} %bitcast.21, bf16[2,256,512]{2,1,0:T(8,128)(2,1)S(1)} %get-tuple-element.55.refs_0_, ...), custom_call_target="tpu_custom_call" | custom-call | tf_op jit(solution)/shard_map/near_own/pallas_call | solution.py:167
  50.4 2.8 %collective-permute-start.12 = (f32[4,128,256]{2,1,0:T(8,128)}, f32[4,128,256]{2,1,0:T(8,128)}, u32[]{:S(2)}, u32[]{:S(2)}) collective-permute-start(f32[4,128,256]{2,1,0:T(8,128)} %pad_maximum_fusion), channel_id=1, source_target_pairs={{0,4},{4,0},{8,12},{12,8},{16,20},{20,16},{24,28},{28,24},{1,5},{5... | collective-permute-start | bytes 1572872 | tf_op jit(solution)/shard_map/ppermute | solution.py:473
  53.2 9.0 %near_pair.1 = (f32[256,1024]{1,0:T(8,128)S(1)}, f32[256,1024]{1,0:T(8,128)S(1)}, f32[256,1024]{1,0:T(8,128)S(1)}, f32[256,1024]{1,0:T(8,128)S(1)}) custom-call(s32[4]{0:T(128)S(1)} %pad_add_fusion.pos_ref, s32[1024]{0:T(1024)S(1)} %bitcast.22, bf16[2,256,512]{2,1,0:T(8,128)(2,1)S(1)} %get-tuple-element.55.refs_0_, ...), custom_call_target="tpu_custom_call" | custom-call | tf_op jit(solution)/shard_map/near_pair/pallas_call | solution.py:167
  63.5 9.8 %collective-permute-done.4.refs_4_ = f32[64,1024]{1,0:T(8,128)S(1)} collective-permute-done((f32[64,1024]{1,0:T(8,128)}, f32[64,1024]{1,0:T(8,128)S(1)}, u32[]{:S(2)}, u32[]{:S(2)}) %collective-permute-start.4) | collective-permute-done | bytes 262176 | tf_op jit(solution)/shard_map/ppermute | solution.py:458
  73.3 5.9 %near_next_away.2 = (f32[128,1024]{1,0:T(8,128)S(1)}, f32[128,1024]{1,0:T(8,128)}) custom-call(s32[4]{0:T(128)S(1)} %pad_add_fusion.pos_ref, s32[1024]{0:T(1024)S(1)} %bitcast.23, bf16[2,256,512]{2,1,0:T(8,128)(2,1)S(1)} %get-tuple-element.60.refs_4_.refs_0_, f32[2,8,512]{2,1,0:T(8,128)S(1)} %get-tuple-element.61.refs_5_.refs_1_, ...), custom_call_target="tpu_custom_call" | custom-call | tf_op jit(solution)/shard_map/near_next_away/pallas_call | solution.py:167
  80.3 6.1 %near_next_away.3 = (f32[128,1024]{1,0:T(8,128)S(1)}, f32[128,1024]{1,0:T(8,128)}) custom-call(s32[4]{0:T(128)S(1)} %pad_add_fusion.pos_ref, s32[1024]{0:T(1024)S(1)} %bitcast.24, bf16[2,256,512]{2,1,0:T(8,128)(2,1)S(1)} %get-tuple-element.60.refs_4_.refs_0_, f32[2,8,512]{2,1,0:T(8,128)S(1)} %get-tuple-element.61.refs_5_.refs_1_, ...), custom_call_target="tpu_custom_call" | custom-call | tf_op jit(solution)/shard_map/near_next_away/pallas_call | solution.py:167
  90.1 1.3 add.12.refs_5_
  91.5 1.9 %copy-done.3 = f32[6,512,256]{2,1,0:T(8,128)S(1)} copy-done((f32[6,512,256]{2,1,0:T(8,128)S(1)}, f32[6,512,256]{2,1,0:T(8,128)}, u32[]{:S(2)}) %copy-start.3) | copy-done | bytes 3145752
  96.1 6.5 %far.1.refs_9_.refs_0_ = f32[64,256]{1,0:T(8,128)S(1)} custom-call(s32[4]{0:T(128)S(1)} %pad_add_fusion.pos_ref, s32[14,4]{1,0:T(8,128)S(1)} %copy.11.far_ref, s32[6,1,256]{2,1,0:T(1,128)S(1)} %broadcast_in_dim.3.node_ref, f32[6,512,256]{2,1,0:T(8,128)S(1)} %copy-done.3, f32[128,256]{1,0:T(8,128)S(1)} %get-tuple-element.76.refs_0_, ...), custom_call_target="tpu_custom_call" | custom-call | tf_op jit(solution)/shard_map/far/pallas_call | solution.py:348
  102.6 5.1 %near_next_home.1 = (f32[256,1024]{1,0:T(8,128)S(1)}, f32[256,1024]{1,0:T(8,128)S(1)}) custom-call(s32[4]{0:T(128)S(1)} %pad_add_fusion.pos_ref, s32[1024]{0:T(1024)S(1)} %bitcast.25, bf16[2,256,512]{2,1,0:T(8,128)(2,1)S(1)} %get-tuple-element.55.refs_0_, f32[2,8,512]{2,1,0:T(8,128)S(1)} %copy-done.22, bf16[2,256,512]{2,1,0:T(8,128)(2,1)S(1)} %get-tuple-element.57.refs_2_, ...), custom_call_target="tpu_custom_call" | custom-call | tf_op jit(solution)/shard_map/near_next_home/pallas_call | solution.py:167
  109.2 1.5 %collective-permute-start.16 = (f32[128,1024]{1,0:T(8,128)S(1)}, f32[128,1024]{1,0:T(8,128)S(1)}, u32[]{:S(2)}, u32[]{:S(2)}) collective-permute-start(f32[128,1024]{1,0:T(8,128)S(1)} %add.12.refs_5_), channel_id=1, source_target_pairs={{2,0},{3,1},{0,2},{1,3},{6,4},{7,5},{4,6},{5,7},{10,8},{11,9},{8,1... | collective-permute-start | bytes 1572872 | tf_op jit(solution)/shard_map/ppermute | solution.py:441
  111.5 10.9 %collective-permute-done.15.refs_0_ = f32[128,1024]{1,0:T(8,128)S(1)} collective-permute-done((f32[128,1024]{1,0:T(8,128)S(1)}, f32[128,1024]{1,0:T(8,128)S(1)}, u32[]{:S(2)}, u32[]{:S(2)}) %collective-permute-start.15) | collective-permute-done | bytes 524320 | tf_op jit(solution)/shard_map/ppermute | solution.py:441
  122.5 1.4 collective-permute-start.20
  123.8 9.9 %collective-permute-done.16.refs_1_ = f32[128,1024]{1,0:T(8,128)S(1)} collective-permute-done((f32[128,1024]{1,0:T(8,128)S(1)}, f32[128,1024]{1,0:T(8,128)S(1)}, u32[]{:S(2)}, u32[]{:S(2)}) %collective-permute-start.16) | collective-permute-done | bytes 524320 | tf_op jit(solution)/shard_map/ppermute | solution.py:441
  135.1 1.8 %collective-permute-done.20.refs_3_ = f32[64,256]{1,0:T(8,128)S(1)} collective-permute-done((f32[64,256]{1,0:T(8,128)S(1)}, f32[64,256]{1,0:T(8,128)S(1)}, u32[]{:S(2)}, u32[]{:S(2)}) %collective-permute-start.20) | collective-permute-done | bytes 65568 | tf_op jit(solution)/shard_map/ppermute | solution.py:438
  136.9 2.2 %join.1 = f32[256,1024]{1,0:T(8,128)} custom-call(s32[4]{0:T(128)S(1)} %pad_add_fusion.pos_ref, f32[2,512,256]{2,1,0:T(8,128)S(1)} %copy-done.1, f32[256,1024]{1,0:T(8,128)S(1)} %add_parts.1.home_ref, f32[256,1024]{1,0:T(8,128)S(1)} %collective-permute-done.17.mate_ref, f32[64,256]{1,0:T(8,128)S(1)} %far.1.refs_9_.refs_0_, ...), custom_call_target="tpu_custom_call" | custom-call | tf_op jit(solution)/shard_map/join/pallas_call | solution.py:407
  (102 shorter events, 25.4 us)
Async XLA Ops:
  0.0 29.0 %copy-start.27 = (s32[1,256]{1,0:T(1,128)S(1)}, s32[1,256]{1,0:T(1,128)}, u32[]{:S(2)}) copy-start(s32[1,256]{1,0:T(1,128)} %index_ref.1) | copy-start | bytes 3076
  0.0 11.0 %collective-permute-start = (f32[64,1024]{1,0:T(8,128)}, f32[64,1024]{1,0:T(8,128)S(1)}, u32[]{:S(2)}, u32[]{:S(2)}) collective-permute-start(f32[64,1024]{1,0:T(8,128)} %refs_8_.1), channel_id=1, source_target_pairs={{0,4},{4,0},{8,12},{12,8},{16,20},{20,16},{24,28},{28,24},{1,5},{5... | collective-permute-start | bytes 786440 | tf_op jit(solution)/shard_map/ppermute | solution.py:451
  1.5 31.5 %collective-permute-start.5 = (f32[128,1024]{1,0:T(8,128)S(1)}, f32[128,1024]{1,0:T(8,128)S(1)}, u32[]{:S(2)}, u32[]{:S(2)}) collective-permute-start(f32[128,1024]{1,0:T(8,128)S(1)} %get-tuple-element.92.refs_9_), channel_id=1, source_target_pairs={{0,4},{4,0},{8,12},{12,8},{16,20},{20,16},{24,28},{28,24},{1,5},{5... | collective-permute-start | bytes 1572872 | tf_op jit(solution)/shard_map/ppermute | solution.py:455
  2.8 31.1 %collective-permute-start.10 = (f32[128,1024]{1,0:T(8,128)S(1)}, f32[128,1024]{1,0:T(8,128)}, u32[]{:S(2)}, u32[]{:S(2)}) collective-permute-start(f32[128,1024]{1,0:T(8,128)S(1)} %get-tuple-element.91.refs_10_), channel_id=1, source_target_pairs={{0,4},{4,0},{8,12},{12,8},{16,20},{20,16},{24,28},{28,24},{1,5},{5... | collective-permute-start | bytes 1572872 | tf_op jit(solution)/shard_map/ppermute | solution.py:455
  8.0 33.0 %copy-start.5 = (f32[64,1024]{1,0:T(8,128)S(1)}, f32[64,1024]{1,0:T(8,128)}, u32[]{:S(2)}) copy-start(f32[64,1024]{1,0:T(8,128)} %refs_8_.1) | copy-start | bytes 786436
  9.2 3.3 %collective-permute-start.1 = (f32[88,1024]{1,0:T(8,128)S(1)}, f32[88,1024]{1,0:T(8,128)S(1)}, u32[]{:S(2)}, u32[]{:S(2)}) collective-permute-start(f32[88,1024]{1,0:T(8,128)S(1)} %get-tuple-element.49), channel_id=1, source_target_pairs={{1,0},{0,1},{3,2},{2,3},{5,4},{4,5},{7,6},{6,7},{9,8},{8,9},{11,10... | collective-permute-start | bytes 1081352 | tf_op jit(solution)/shard_map/ppermute | solution.py:454
  10.7 10.0 %collective-permute-start.2 = (f32[88,1024]{1,0:T(8,128)S(1)}, f32[88,1024]{1,0:T(8,128)S(1)}, u32[]{:S(2)}, u32[]{:S(2)}) collective-permute-start(f32[88,1024]{1,0:T(8,128)S(1)} %get-tuple-element.50), channel_id=1, source_target_pairs={{2,0},{3,1},{0,2},{1,3},{6,4},{7,5},{4,6},{5,7},{10,8},{11,9},{8,1... | collective-permute-start | bytes 1081352 | tf_op jit(solution)/shard_map/ppermute | solution.py:454
  11.0 18.0 %collective-permute-start.3 = (f32[88,1024]{1,0:T(8,128)S(1)}, f32[88,1024]{1,0:T(8,128)S(1)}, u32[]{:S(2)}, u32[]{:S(2)}) collective-permute-start(f32[88,1024]{1,0:T(8,128)S(1)} %get-tuple-element.51), channel_id=1, source_target_pairs={{3,0},{2,1},{1,2},{0,3},{7,4},{6,5},{5,6},{4,7},{11,8},{10,9},{9,1... | collective-permute-start | bytes 1081352 | tf_op jit(solution)/shard_map/ppermute | solution.py:454
  30.3 8.7 %collective-permute-start.7 = (f32[128,256]{1,0:T(8,128)S(1)}, f32[128,256]{1,0:T(8,128)S(1)}, u32[]{:S(2)}, u32[]{:S(2)}) collective-permute-start(f32[128,256]{1,0:T(8,128)S(1)} %get-tuple-element.76.refs_0_), channel_id=1, source_target_pairs={{0,8},{4,12},{8,0},{12,4},{16,24},{20,28},{24,16},{28,20},{1,9},{5... | collective-permute-start | bytes 393224 | tf_op jit(solution)/shard_map/ppermute | solution.py:467
  30.6 18.9 %collective-permute-start.8 = (f32[128,256]{1,0:T(8,128)S(1)}, f32[128,256]{1,0:T(8,128)S(1)}, u32[]{:S(2)}, u32[]{:S(2)}) collective-permute-start(f32[128,256]{1,0:T(8,128)S(1)} %get-tuple-element.76.refs_0_), channel_id=1, source_target_pairs={{0,16},{4,20},{8,24},{12,28},{16,0},{20,4},{24,8},{28,12},{1,17},{... | collective-permute-start | bytes 393224 | tf_op jit(solution)/shard_map/ppermute | solution.py:467
  32.9 16.6 %collective-permute-start.9 = (f32[128,256]{1,0:T(8,128)S(1)}, f32[128,256]{1,0:T(8,128)S(1)}, u32[]{:S(2)}, u32[]{:S(2)}) collective-permute-start(f32[128,256]{1,0:T(8,128)S(1)} %get-tuple-element.76.refs_0_), channel_id=1, source_target_pairs={{0,24},{4,28},{8,16},{12,20},{16,8},{20,12},{24,0},{28,4},{1,25},{... | collective-permute-start | bytes 393224 | tf_op jit(solution)/shard_map/ppermute | solution.py:467
  33.9 46.4 %collective-permute-start.13 = (f32[128,1024]{1,0:T(8,128)}, f32[128,1024]{1,0:T(8,128)S(1)}, u32[]{:S(2)}, u32[]{:S(2)}) collective-permute-start(f32[128,1024]{1,0:T(8,128)} %collective-permute-done.10.refs_10_), channel_id=1, source_target_pairs={{0,8},{8,16},{16,24},{12,4},{20,12},{28,20},{1,9},{9,17},{17,25},{... | collective-permute-start | bytes 1572872 | tf_op jit(solution)/shard_map/ppermute | solution.py:471
  37.1 36.2 %collective-permute-start.6 = (f32[128,1024]{1,0:T(8,128)}, f32[128,1024]{1,0:T(8,128)S(1)}, u32[]{:S(2)}, u32[]{:S(2)}) collective-permute-start(f32[128,1024]{1,0:T(8,128)} %copy-done.10), channel_id=1, source_target_pairs={{0,8},{8,16},{16,24},{12,4},{20,12},{28,20},{1,9},{9,17},{17,25},{... | collective-permute-start | bytes 1572872 | tf_op jit(solution)/shard_map/ppermute | solution.py:469
  39.0 34.2 %collective-permute-start.4 = (f32[64,1024]{1,0:T(8,128)}, f32[64,1024]{1,0:T(8,128)S(1)}, u32[]{:S(2)}, u32[]{:S(2)}) collective-permute-start(f32[64,1024]{1,0:T(8,128)} %copy-done.25), channel_id=1, source_target_pairs={{0,8},{8,16},{16,24},{12,4},{20,12},{28,20},{1,9},{9,17},{17,25},{... | collective-permute-start | bytes 786440 | tf_op jit(solution)/shard_map/ppermute | solution.py:458
  50.4 37.6 %collective-permute-start.12 = (f32[4,128,256]{2,1,0:T(8,128)}, f32[4,128,256]{2,1,0:T(8,128)}, u32[]{:S(2)}, u32[]{:S(2)}) collective-permute-start(f32[4,128,256]{2,1,0:T(8,128)} %pad_maximum_fusion), channel_id=1, source_target_pairs={{0,4},{4,0},{8,12},{12,8},{16,20},{20,16},{24,28},{28,24},{1,5},{5... | collective-permute-start | bytes 1572872 | tf_op jit(solution)/shard_map/ppermute | solution.py:473
  80.0 8.0 %collective-permute-start.11 = (f32[128,1024]{1,0:T(8,128)}, f32[128,1024]{1,0:T(8,128)}, u32[]{:S(2)}, u32[]{:S(2)}) collective-permute-start(f32[128,1024]{1,0:T(8,128)} %get-tuple-element.75), channel_id=1, source_target_pairs={{1,0},{0,1},{3,2},{2,3},{5,4},{4,5},{7,6},{6,7},{9,8},{8,9},{11,10... | collective-permute-start | bytes 1572872 | tf_op jit(solution)/shard_map/ppermute | solution.py:438
  87.2 2.1 %collective-permute-start.14 = (f32[128,1024]{1,0:T(8,128)}, f32[128,1024]{1,0:T(8,128)S(1)}, u32[]{:S(2)}, u32[]{:S(2)}) collective-permute-start(f32[128,1024]{1,0:T(8,128)} %get-tuple-element.86), channel_id=1, source_target_pairs={{1,0},{0,1},{3,2},{2,3},{5,4},{4,5},{7,6},{6,7},{9,8},{8,9},{11,10... | collective-permute-start | bytes 1572872 | tf_op jit(solution)/shard_map/ppermute | solution.py:438
  107.7 29.2 %copy-start.1 = (f32[2,512,256]{2,1,0:T(8,128)S(1)}, f32[2,512,256]{2,1,0:T(8,128)}, u32[]{:S(2)}) copy-start(f32[2,512,256]{2,1,0:T(8,128)} %interp_ref.3) | copy-start | bytes 3145732
  107.7 29.2 %collective-permute-start.17 = (f32[256,1024]{1,0:T(8,128)S(1)}, f32[256,1024]{1,0:T(8,128)S(1)}, u32[]{:S(2)}, u32[]{:S(2)}) collective-permute-start(f32[256,1024]{1,0:T(8,128)S(1)} %get-tuple-element.90), channel_id=1, source_target_pairs={{1,0},{0,1},{3,2},{2,3},{5,4},{4,5},{7,6},{6,7},{9,8},{8,9},{11,10... | collective-permute-start | bytes 3145736 | tf_op jit(solution)/shard_map/ppermute | solution.py:438
  109.2 13.3 %collective-permute-start.15 = (f32[128,1024]{1,0:T(8,128)S(1)}, f32[128,1024]{1,0:T(8,128)S(1)}, u32[]{:S(2)}, u32[]{:S(2)}) collective-permute-start(f32[128,1024]{1,0:T(8,128)S(1)} %add.13), channel_id=1, source_target_pairs={{2,0},{3,1},{0,2},{1,3},{6,4},{7,5},{4,6},{5,7},{10,8},{11,9},{8,1... | collective-permute-start | bytes 1572872 | tf_op jit(solution)/shard_map/ppermute | solution.py:441
  109.2 24.5 %collective-permute-start.16 = (f32[128,1024]{1,0:T(8,128)S(1)}, f32[128,1024]{1,0:T(8,128)S(1)}, u32[]{:S(2)}, u32[]{:S(2)}) collective-permute-start(f32[128,1024]{1,0:T(8,128)S(1)} %add.12.refs_5_), channel_id=1, source_target_pairs={{2,0},{3,1},{0,2},{1,3},{6,4},{7,5},{4,6},{5,7},{10,8},{11,9},{8,1... | collective-permute-start | bytes 1572872 | tf_op jit(solution)/shard_map/ppermute | solution.py:441
  110.7 23.1 %collective-permute-start.18 = (f32[64,256]{1,0:T(8,128)S(1)}, f32[64,256]{1,0:T(8,128)S(1)}, u32[]{:S(2)}, u32[]{:S(2)}) collective-permute-start(f32[64,256]{1,0:T(8,128)S(1)} %far.1.refs_9_.refs_0_), channel_id=1, source_target_pairs={{1,0},{0,1},{3,2},{2,3},{5,4},{4,5},{7,6},{6,7},{9,8},{8,9},{11,10... | collective-permute-start | bytes 196616 | tf_op jit(solution)/shard_map/ppermute | solution.py:438
  111.5 23.6 %collective-permute-start.19 = (f32[64,256]{1,0:T(8,128)S(1)}, f32[64,256]{1,0:T(8,128)S(1)}, u32[]{:S(2)}, u32[]{:S(2)}) collective-permute-start(f32[64,256]{1,0:T(8,128)S(1)} %far.1.refs_9_.refs_0_), channel_id=1, source_target_pairs={{2,0},{3,1},{0,2},{1,3},{6,4},{7,5},{4,6},{5,7},{10,8},{11,9},{8,1... | collective-permute-start | bytes 196616 | tf_op jit(solution)/shard_map/ppermute | solution.py:438
  122.5 14.4 %collective-permute-start.20 = (f32[64,256]{1,0:T(8,128)S(1)}, f32[64,256]{1,0:T(8,128)S(1)}, u32[]{:S(2)}, u32[]{:S(2)}) collective-permute-start(f32[64,256]{1,0:T(8,128)S(1)} %far.1.refs_9_.refs_0_), channel_id=1, source_target_pairs={{3,0},{2,1},{1,2},{0,3},{7,4},{6,5},{5,6},{4,7},{11,8},{10,9},{9,1... | collective-permute-start | bytes 196616 | tf_op jit(solution)/shard_map/ppermute | solution.py:438
  (28 other events, 197.9 us)

commit v4 on v3

v4 whole, which is shorter than its diff:
```python
import math
from functools import partial

import jax
import jax.numpy as jnp
from jax import lax
from jax.experimental import pallas as pl
from jax.experimental.pallas import tpu as pltpu
from jax.sharding import PartitionSpec as P

F = 64
R = 256
LEAF = 512
SK = 256
FL = 4
EXTRA = 8

BF = jnp.bfloat16
F32 = jnp.float32
LOG2E = 1.0 / math.log(2.0)
SCALE = math.sqrt(0.5 * LOG2E)
BIAS = 0.0625 * F * LOG2E
VMEM_LIMIT = 24 * 1024 * 1024


def dot(a, b):
    return jnp.dot(a, b, preferred_element_type=F32)


def dot_t(a, b):
    return lax.dot_general(a, b, (((1,), (1,)), ((), ())), preferred_element_type=F32)


def halves(x):
    hi = x.astype(BF)
    lo = (x - hi.astype(F32)).astype(BF)
    return hi, lo


def dot3(a, b, mul=dot):
    a_hi, a_lo = halves(a)
    b_hi, b_lo = halves(b)
    return mul(a_hi, b_hi) + mul(a_lo, b_hi) + mul(a_hi, b_lo)


def target_side(x):
    hi, lo = halves(x)
    both = hi.astype(F32) + lo.astype(F32)
    off = BIAS - 0.5 * jnp.sum(both * both, axis=0, keepdims=True)
    return jnp.concatenate([hi, lo, hi, lo], axis=0), off


def source_side(x):
    xt = x.T
    hi, lo = halves(xt)
    both = hi.astype(F32) + lo.astype(F32)
    off = BIAS - 0.5 * jnp.sum(both * both, axis=1, keepdims=True)
    return jnp.concatenate([hi, hi, lo, lo], axis=1), off


def near_body(
    xs, sets, leaves_at, rows, row, has_acc, nout, pos_ref, times_ref, t_ref, tb_ref, *refs
):
    nset = len(sets)
    if has_acc:
        s_scr, sb_scr, w_scr, o_scr, k_scr, times_scr, list_ref = refs[-7:]
        outs = refs[-7 - nout : -7]
    else:
        o_scr, s_scr, sb_scr, w_scr, k_scr, times_scr, list_ref = refs[-7:]
    at = 0
    for k, (_, ready, chunks) in enumerate(sets):
        heads = refs[at : at + 1 + ready]
        parts = refs[at + 1 + ready : at + 1 + ready + chunks]
        at += 1 + ready + chunks
        each = rows // chunks
        for leaf in range(2):
            cols = slice(leaf * LEAF, (leaf + 1) * LEAF)
            j = 2 * k + leaf
            if ready:
                s_scr[j] = heads[0][leaf]
                sb_scr[j] = heads[1][leaf]
            else:
                side, off = source_side(heads[0][:F, cols] * SCALE)
                s_scr[j] = side
                sb_scr[j] = jnp.broadcast_to(off, (LEAF, 128))
            for c in range(chunks):
                hi, lo = halves(parts[c][:, cols])
                w_scr[j, c * each : (c + 1) * each, :] = hi
                w_scr[j, rows + c * each : rows + (c + 1) * each, :] = lo
    start, stop = leaves_at
    for t in range(start, stop):
        if has_acc:
            o_scr[t - start] = refs[at][t, row : row + rows, :]
        else:
            o_scr[t - start] = jnp.zeros((rows, LEAF), F32)

    x, core, group, leaves = pos_ref[0], pos_ref[1], pos_ref[2], pos_ref[3]
    odd = group % 2
    column = []
    for kind, _, _ in sets:
        relative = {"own": 1, "pair": 2 - 2 * odd, "next": 2 * odd}[kind]
        column.append(relative * leaves + 2 * (2 * x + core))

    count = jnp.int32(0)
    list_ref[0] = 0
    times_scr[0] = 0
    for t in range(start, stop):
        for j in range(2 * nset):
            helper = 2 * lax.rem(x + t // 4, xs) + (core if t // 2 % 2 == 0 else 1 - core)
            times = times_ref[(2 * helper + t % 2) * 128 + column[j // 2] + j % 2]

            @pl.when(times > 0)
            def _(count=count, t=t, j=j, times=times):
                list_ref[count] = t * 8 + j
                times_scr[count] = times

            count = count + (times > 0).astype(jnp.int32)

    def block(index, slot):
        code = list_ref[jnp.minimum(index, jnp.maximum(count - 1, 0))]
        t, j = code // 8, code % 8
        side = t_ref[t]
        off = tb_ref[t][:1, :]
        for half in range(2):
            part = slice(half * 256, (half + 1) * 256)
            cross = dot(s_scr[j, part, :], side)
            src_off = sb_scr[j, part, :]
            src_off = jnp.concatenate([src_off] * (LEAF // 128), axis=1)
            k_hi, k_lo = halves(jnp.exp2(cross + src_off + off))
            k_scr[slot, part, :] = k_hi
            k_scr[slot, LEAF + half * 256 : LEAF + (half + 1) * 256, :] = k_lo

    def apply(index, slot):
        code = list_ref[index]
        t, j = code // 8 - start, code % 8
        factor = times_scr[index].astype(F32)
        for half in range(2):
            cols = slice(half * 256, (half + 1) * 256)
            both = dot(w_scr[j], k_scr[slot, :LEAF, cols])
            low = dot(w_scr[j, :rows, :], k_scr[slot, LEAF:, cols])
            o_scr[t, :, cols] = o_scr[t, :, cols] + factor * (both[:rows] + both[rows:] + low)

    @pl.when(count > 0)
    def _():
        block(0, 0)

    def pair(index, carry):
        block(2 * index + 1, 1)
        apply(2 * index, 0)

        @pl.when(2 * index + 1 < count)
        def _():
            block(2 * index + 2, 0)
            apply(2 * index + 1, 1)

        return carry

    lax.fori_loop(0, (count + 1) // 2, pair, jnp.int32(0))
    if has_acc:
        tall = outs[0].shape[0]
        for n, ref in enumerate(outs):
            t, top = 2 * (n // (rows // tall)), n % (rows // tall) * tall
            for leaf in range(2):
                cols = slice(leaf * LEAF, (leaf + 1) * LEAF)
                ref[:, cols] = o_scr[t + leaf, top : top + tall, :]


def near_call(name, where, targets, leaves_at, sources, rows, row=0, acc=None, after=()):
    nset = len(sources)
    start, stop = leaves_at
    tall = R // 2
    vmem = pl.BlockSpec(memory_space=pltpu.VMEM)
    smem = pl.BlockSpec(memory_space=pltpu.SMEM)
    operands = [a for _, heads, chunks in sources for a in (*heads, *chunks)]
    scratch = [
        pltpu.VMEM((2 * nset, LEAF, 4 * F), BF),
        pltpu.VMEM((2 * nset, LEAF, 128), F32),
        pltpu.VMEM((2 * nset, 2 * rows, LEAF), BF),
        pltpu.VMEM((stop - start, rows, LEAF), F32),
        pltpu.VMEM((2, 2 * LEAF, LEAF), BF),
        pltpu.SMEM((2 * nset * (stop - start),), jnp.int32),
        pltpu.SMEM((2 * nset * (stop - start),), jnp.int32),
    ]
    if acc is None:
        out = [jax.ShapeDtypeStruct((stop - start, rows, LEAF), F32)]
        scratch.pop(3)
    else:
        operands.append(acc)
        out = [jax.ShapeDtypeStruct((tall, 2 * LEAF), F32)] * ((stop - start) // 2 * (rows // tall))
    sets = tuple((kind, len(heads) - 1, len(chunks)) for kind, heads, chunks in sources)
    return pl.pallas_call(
        partial(
            near_body, targets[0].shape[0] // 4, sets, leaves_at, rows, row, acc is not None, len(out)
        ),
        name=name,
        out_shape=out,
        in_specs=[smem, smem]
        + [vmem] * (2 + len(operands))
        + [pl.BlockSpec(memory_space=pl.ANY)] * len(after),
        out_specs=[vmem] * len(out),
        scratch_shapes=scratch,
        compiler_params=pltpu.CompilerParams(vmem_limit_bytes=VMEM_LIMIT),
    )(*where, *targets, *operands, *after)


def source_body(pts_ref, side_ref, off_ref):
    for leaf in range(2):
        cols = slice(leaf * LEAF, (leaf + 1) * LEAF)
        side, off = source_side(pts_ref[:, cols] * SCALE)
        side_ref[leaf] = side
        off_ref[leaf] = jnp.broadcast_to(off, (LEAF, 128))


def source_call(pts):
    vmem = pl.BlockSpec(memory_space=pltpu.VMEM)
    return pl.pallas_call(
        source_body,
        name="source_side",
        out_shape=[
            jax.ShapeDtypeStruct((2, LEAF, 4 * F), BF),
            jax.ShapeDtypeStruct((2, LEAF, 128), F32),
        ],
        in_specs=[vmem],
        out_specs=[vmem, vmem],
        compiler_params=pltpu.CompilerParams(vmem_limit_bytes=VMEM_LIMIT),
    )(pts)


def share_rows(xs):
    return R // (2 * xs) * SK // (2 * LEAF)


def leaf_body(xs, pos_ref, count_ref, src_ref, pts_in, w_in, interp_in, *refs):
    msg, pts_ref, w_ref, interp_ref, scr, sems = refs
    copies = [
        pltpu.make_async_copy(pts_in, pts_ref, sems.at[0]),
        pltpu.make_async_copy(w_in, w_ref, sems.at[1]),
        pltpu.make_async_copy(interp_in, interp_ref, sems.at[2]),
    ]
    for copy in copies:
        copy.start()
    group, leaves = pos_ref[2], pos_ref[3]
    lane = lax.broadcasted_iota(jnp.int32, (1, 128), 1) + (group - 1) * leaves
    times = []
    for leaf in range(2):
        row = jnp.zeros((1, 128), F32)
        for slot in range(src_ref.shape[1]):
            name = jnp.where(slot < count_ref[0, leaf], src_ref[leaf, slot], -1 - 128 * leaves)
            row = row + (lane == name).astype(F32)
        times.append(row)
    times = jnp.concatenate(times + [jnp.zeros((EXTRA - 2, 128), F32)], axis=0)
    for copy in copies:
        copy.wait()
    total = jnp.zeros((R, SK), F32)
    for leaf in range(2):
        total = total + dot3(w_ref[:, leaf * LEAF : (leaf + 1) * LEAF], interp_ref[leaf])
    scr[...] = total
    rows = R // (2 * xs)
    tall = share_rows(xs)
    for helper in range(2 * xs):
        msg[helper, :F, :] = pts_ref[...]
        msg[helper, F : F + EXTRA, :] = jnp.zeros((EXTRA, 2 * LEAF), F32)
        msg[helper, F : F + EXTRA, :128] = times
        for i in range(rows // tall):
            at = helper * rows + i * tall
            msg[helper, F + EXTRA :, i * SK : (i + 1) * SK] = scr[at : at + tall, :]


def leaf_call(xs, pos, near_count, near_src, points, weights, interp):
    vmem = pl.BlockSpec(memory_space=pltpu.VMEM)
    smem = pl.BlockSpec(memory_space=pltpu.SMEM)
    anywhere = pl.BlockSpec(memory_space=pl.ANY)
    height = F + EXTRA + share_rows(xs)
    return pl.pallas_call(
        partial(leaf_body, xs),
        name="leaf_up",
        out_shape=jax.ShapeDtypeStruct((2 * xs, height, 2 * LEAF), F32),
        in_specs=[smem, smem, smem, anywhere, anywhere, anywhere],
        out_specs=vmem,
        scratch_shapes=[
            pltpu.VMEM(points.shape, F32),
            pltpu.VMEM(weights.shape, F32),
            pltpu.VMEM(interp.shape, F32),
            pltpu.VMEM((R, SK), F32),
            pltpu.SemaphoreType.DMA((3,)),
        ],
        compiler_params=pltpu.CompilerParams(vmem_limit_bytes=VMEM_LIMIT),
    )(pos, near_count, near_src, points, weights, interp)


def skel_body(xs, pos_ref, index_ref, msgs, out_ref, side_ref, off_ref):
    nblk = 2 * xs
    rows = R // nblk
    tall = share_rows(xs)
    total = jnp.zeros((2 * F, SK), F32)
    value = jnp.zeros((tall, 2 * LEAF), F32)
    spot = lax.broadcasted_iota(jnp.int32, (2 * LEAF, SK), 0)
    x, core = pos_ref[0], pos_ref[1]
    for b in range(nblk):
        helper = 2 * lax.rem(x + b // 2, xs) + (core if b % 2 == 0 else 1 - core)
        side, off = target_side(msgs[helper, :F, :] * SCALE)
        for leaf in range(2):
            part = slice(leaf * LEAF, (leaf + 1) * LEAF)
            side_ref[2 * b + leaf] = side[:, part]
            off_ref[2 * b + leaf] = jnp.broadcast_to(off[:, part], (8, LEAF))
        hot = spot + helper * (2 * LEAF) == index_ref[...]
        total = total + dot(side[: 2 * F], hot.astype(F32).astype(BF))
        value = value + msgs[helper, F + EXTRA :, :]
    out_ref[:F, :] = total[:F] + total[F:]
    for i in range(rows // tall):
        out_ref[F + i * tall : F + (i + 1) * tall, :] = value[:, i * SK : (i + 1) * SK]


def skel_call(xs, pos, index, msgs):
    rows = R // (2 * xs)
    nblk = 2 * xs
    vmem = pl.BlockSpec(memory_space=pltpu.VMEM)
    return pl.pallas_call(
        partial(skel_body, xs),
        name="skeleton",
        out_shape=[
            jax.ShapeDtypeStruct((F + rows, SK), F32),
            jax.ShapeDtypeStruct((2 * nblk, 4 * F, LEAF), BF),
            jax.ShapeDtypeStruct((2 * nblk, 8, LEAF), F32),
        ],
        in_specs=[pl.BlockSpec(memory_space=pltpu.SMEM)] + [vmem] * 2,
        out_specs=[vmem] * 3,
        compiler_params=pltpu.CompilerParams(vmem_limit_bytes=VMEM_LIMIT),
    )(pos, index, msgs)


def upper_start(level, groups):
    return sum((groups >> step for step in range(1, level)))


def list_start(level, groups):
    return sum((groups >> step for step in range(level)))


def far_body(groups, rows, pos_ref, far_ref, node_ref, transfer_ref, *refs):
    pieces, beside = refs[: groups // 2], refs[groups // 2]
    out_ref, p_scr, u_scr, f_scr = refs[-4:]
    levels = groups.bit_length() - 1
    group = pos_ref[2]
    start = [sum(groups >> step for step in range(level)) for level in range(levels)]
    for n, piece in enumerate(pieces):
        p_scr[2 * n] = piece[:F, :]
        u_scr[2 * n] = piece[F:, :]
        p_scr[2 * n + 1] = beside[n, :F, :]
        u_scr[2 * n + 1] = beside[n, F:, :]
    spot = lax.broadcasted_iota(jnp.int32, (2 * SK, SK), 0)
    for level in range(1, levels):
        bit = (group >> (level - 1)) & 1
        for m in range(groups >> level):
            row = upper_start(level, groups) + (m ^ (group >> level))
            left = start[level - 1] + 2 * m + bit
            right = start[level - 1] + 2 * m + 1 - bit
            hot = (spot == node_ref[row]).astype(F32).astype(BF)
            pts = jnp.concatenate([p_scr[left], p_scr[right]], axis=1)
            hi, lo = halves(pts)
            both = dot(jnp.concatenate([hi, lo], axis=0), hot)
            p_scr[start[level] + m] = both[:F] + both[F:]
            vals = jnp.concatenate([u_scr[left], u_scr[right]], axis=1)
            u_scr[start[level] + m] = dot3(vals, transfer_ref[row])
    for level in range(levels):
        node = group >> level
        side, off = target_side(p_scr[start[level]])
        f_scr[level] = jnp.zeros((rows, SK), F32)

        def one(m, carry, level=level, node=node, side=side, off=off):
            hits = jnp.int32(0)
            for slot in range(FL):
                entry = far_ref[list_start(level, groups) + node, slot]
                hits = hits + (entry == (m ^ node)).astype(jnp.int32)

            @pl.when(hits > 0)
            def _():
                src, src_off = source_side(p_scr[start[level] + m])
                block = jnp.exp2(dot(src, side) + src_off + off)
                term = dot3(u_scr[start[level] + m], block)
                f_scr[level] = f_scr[level] + hits.astype(F32) * term

            return carry

        lax.fori_loop(0, groups >> level, one, jnp.int32(0))
    local = f_scr[levels - 1]
    for level in range(levels - 1, 0, -1):
        row = upper_start(level, groups) + (group >> level)
        bit = (group >> (level - 1)) & 1
        matrix = transfer_ref[row, pl.ds(pl.multiple_of(bit * SK, SK), SK), :]
        local = f_scr[level - 1] + dot3(local, matrix, dot_t)
    out_ref[...] = local


def far_call(groups, pos, far_nodes, skel_node, transfer, pieces, beside, after):
    rows = pieces[0].shape[0] - F
    vmem = pl.BlockSpec(memory_space=pltpu.VMEM)
    smem = pl.BlockSpec(memory_space=pltpu.SMEM)
    nodes = 2 * groups
    return pl.pallas_call(
        partial(far_body, groups, rows),
        name="far",
        out_shape=jax.ShapeDtypeStruct((rows, SK), F32),
        in_specs=[smem, smem, vmem, vmem]
        + [vmem] * (len(pieces) + 1)
        + [pl.BlockSpec(memory_space=pl.ANY)] * len(after),
        out_specs=vmem,
        scratch_shapes=[
            pltpu.VMEM((nodes, F, SK), F32),
            pltpu.VMEM((nodes, rows, SK), F32),
            pltpu.VMEM((groups.bit_length(), rows, SK), F32),
        ],
        compiler_params=pltpu.CompilerParams(vmem_limit_bytes=VMEM_LIMIT),
    )(pos, far_nodes, skel_node[:, None, :], transfer, *pieces, beside, *after)


def final_body(xs, pos_ref, interp_ref, *refs):
    values, sums = refs[: 2 * xs], refs[2 * xs : -2]
    out_ref, v_scr = refs[-2:]
    rows = R // (2 * xs)
    x, core = pos_ref[0], pos_ref[1]
    for n, ref in enumerate(values):
        helper = 2 * lax.rem(x + n // 2, xs) + (core if n % 2 == 0 else 1 - core)
        v_scr[pl.ds(pl.multiple_of(helper * rows, rows), rows), :] = ref[...]
    value = v_scr[...]
    for leaf in range(2):
        cols = slice(leaf * LEAF, (leaf + 1) * LEAF)
        total = dot3(value, interp_ref[leaf], dot_t)
        for c in range(2):
            part = slice(c * R // 2, (c + 1) * R // 2)
            out_ref[part, cols] = total[part] + sums[c][:, cols] + sums[2 + c][:, cols]


def add_body(*refs):
    count = (len(refs) - 2) // 2
    for c in range(2):
        total = refs[c * count][...]
        for ref in refs[c * count + 1 : (c + 1) * count]:
            total = total + ref[...]
        refs[c - 2][...] = total


def add_call(home, parts):
    vmem = pl.BlockSpec(memory_space=pltpu.VMEM)
    operands = [home[0], *parts[0], home[1], *parts[1]]
    return pl.pallas_call(
        add_body,
        name="add_parts",
        out_shape=[jax.ShapeDtypeStruct(home[0].shape, F32)] * 2,
        in_specs=[vmem] * len(operands),
        out_specs=[vmem] * 2,
        compiler_params=pltpu.CompilerParams(vmem_limit_bytes=VMEM_LIMIT),
    )(*operands)


def final_call(xs, pos, interp, home, mate, values):
    vmem = pl.BlockSpec(memory_space=pltpu.VMEM)
    return pl.pallas_call(
        partial(final_body, xs),
        name="join",
        out_shape=jax.ShapeDtypeStruct((R, 2 * LEAF), F32),
        in_specs=[pl.BlockSpec(memory_space=pltpu.SMEM)] + [vmem] * (1 + 2 * xs + 4),
        out_specs=vmem,
        scratch_shapes=[pltpu.VMEM((R, SK), F32)],
        compiler_params=pltpu.CompilerParams(vmem_limit_bytes=VMEM_LIMIT),
    )(pos, interp, *values, *home, *mate)


def help_pairs(xs, dx, dc):
    return [
        (2 * ((x + dx) % xs) + (core ^ dc), 2 * x + core) for x in range(xs) for core in range(2)
    ]


def shards(
    points, weights, interp, transfer, near_count, near_src, skel_group, skel_node, far_nodes
):
    helpers = lax.axis_size("help")
    groups = lax.axis_size("leaf")
    xs = helpers // 2
    helper = lax.axis_index("help")
    group = lax.axis_index("leaf")
    x, core = helper // 2, helper % 2
    leaves = 2 * helpers
    pos = jnp.stack([x, core, group, jnp.int32(leaves)]).astype(jnp.int32)
    rows = R // 2

    def from_help(value, dx, dc):
        return lax.ppermute(value, "help", help_pairs(xs, dx, dc))

    def to_help(value, dx):
        return lax.ppermute(value, "help", help_pairs(xs, -dx, 0))

    def together(*values):
        return lax.optimization_barrier(values)

    beside = [(i, i ^ 1) for i in range(groups)]
    across = [(i, i + 2) for i in range(0, groups - 2, 2)]
    across += [(i, i - 2) for i in range(3, groups, 2)]
    order = [(dx, dc) for dx in range(xs) for dc in range(2)]

    pts_y = lax.ppermute(points, "leaf", beside)
    w_own = [weights[:rows], weights[rows:]]
    w_y = [lax.ppermute(chunk, "leaf", beside) for chunk in w_own]
    msgs = leaf_call(xs, pos, near_count, near_src, points, weights, interp)
    got = lax.all_to_all(msgs, "help", 0, 0)
    pts_z = lax.ppermute(pts_y, "leaf", across)
    pts_z, w_y[0] = together(pts_z, w_y[0])
    w_z = [lax.ppermute(w_y[0], "leaf", across)]
    got, w_y = together(got, w_y)
    w_z.append(lax.ppermute(w_y[1], "leaf", across))

    times = got[:, F : F + 2, :128].astype(jnp.int32).reshape(-1)
    where = (pos, times)
    payload, *targets = skel_call(xs, pos, skel_group, got)
    pieces = [payload]
    for mask in range(2, groups, 2):
        pieces.append(lax.ppermute(payload, "leaf", [(i, i ^ mask) for i in range(groups)]))

    sources = [("own", (points,), w_own), ("pair", (pts_y,), w_y)]
    (near,) = near_call("near_own_pair", where, targets, (0, 2 * helpers), sources, R)
    z_side = source_call(pts_z)
    sums, part = [], []
    for c in range(2):
        part = near_call(
            "near_next_away", where, targets, (4, 2 * helpers), [("next", z_side, w_z[c : c + 1])],
            rows, c * rows, near, part[:1],
        )
        kept, given = part[::2], part[1::2]
        sums.append((kept, [from_help(value, 0, 1) for value in given]))
    pieces, part = together(pieces, part)
    side = lax.ppermute(jnp.stack(pieces), "leaf", beside)
    parts = []
    for c in range(2):
        kept, mates = sums[c]
        if c == 0:
            mates, pieces = together(mates, pieces)
        both = [k + m for k, m in zip(kept, mates)]
        parts.append([to_help(value, dx + 1) for dx, value in enumerate(both)])
    v_own = far_call(groups, pos, far_nodes, skel_node, transfer, pieces, side, both[:1])
    values = [v_own] + [from_help(v_own, dx, dc) for dx, dc in order[1:]]
    home = near_call(
        "near_next_home", where, targets, (0, 4), [("next", z_side, w_z)], R, 0, near, [v_own]
    )
    mate = [from_help(value, 0, 1) for value in home[2:]]
    return final_call(xs, pos, interp, add_call(home[:2], parts), mate, values)


def solution(mesh):
    placed = (
        P(None, ("leaf", "help")),
        P(None, ("leaf", "help")),
        P(("leaf", "help"), None, None),
        P(),
        P("leaf", "help"),
        P(("leaf", "help"), None),
        P("leaf", None),
        P(),
        P(),
    )
    return jax.shard_map(
        shards, mesh=mesh, in_specs=placed, out_specs=P(None, ("leaf", "help")), check_vma=False
    )
```

time: 140 us -> 124 us (0.89)
  the two profiles are of different devices: /device:TPU:15 before, /device:TPU:8 now
where the time goes in v4:
time: 124 us
  starting transfers between devices  43.8 us (35%)
  Pallas kernels  35.4 us (29%)
  waiting for transfers between devices  27.1 us (22%)
  local copies, waits for them, and re-layouts  15 us (12%)
  other arithmetic  1.86 us (2%)
    pallas_call x4, Pallas kernels, near_call(): pl.pallas_call(partial(near_body, targets[0].shape[0] // 4, sets, leaves_...  19.8 us
    unnamed x69, local copies, waits for them, and re-layouts  14.9 us
    ppermute x2, waiting for transfers between devices, shards(): w_y = [lax.ppermute(chunk, 'leaf', beside) for chunk in w_own]  9.36 us
    ppermute x7, starting transfers between devices, from_help(): return lax.ppermute(value, 'help', help_pairs(xs, dx, dc))  9.03 us
    ppermute x1, starting transfers between devices, shards(): side = lax.ppermute(jnp.stack(pieces), 'leaf', beside)  7.62 us
    pallas_call x1, Pallas kernels, far_call(): pl.pallas_call(partial(far_body, groups, rows), name='far', out_shape=jax...  7.03 us
    ppermute x1, waiting for transfers between devices, shards(): side = lax.ppermute(jnp.stack(pieces), 'leaf', beside)  5.99 us
    ppermute x2, starting transfers between devices, to_help(): return lax.ppermute(value, 'help', help_pairs(xs, -dx, 0))  5.76 us
  transfers between devices with their start and end apart: 20, of which 7 were waited for; matrix products, arithmetic and copies ran while one was open for 2% of the time, Pallas kernels for 24%

profile of v4, /device:TPU:8, one launch (start us, length us, event | category | flops | bytes accessed | tf_op | source)
XLA Modules:
  0.0 123.5 jit_solution(17460772293294772071)
XLA Ops:
  3.9 3.3 %leaf_up.1 = f32[4,88,1024]{2,1,0:T(8,128)} custom-call(s32[4]{0:T(128)S(1)} %pad_add_fusion.pos_ref, s32[1,2]{1,0:T(1,128)S(1)} %copy-done.31, s32[2,32]{1,0:T(2,128)S(1)} %copy-done.29, f32[64,1024]{1,0:T(8,128)} %refs_0_.1, f32[256,1024]{1,0:T(8,128)S(1)} %copy-done.8, f32[2,512,256]{2,1,0:T(8,128)S(1)} %copy-done.6), custom_call_target="tpu_custom_call" | custom-call | tf_op jit(solution)/shard_map/leaf_up/pallas_call | solution.py:274
  7.2 3.7 %all-to-all-start = ((f32[4,88,1024]{2,1,0:T(8,128)}), f32[4,88,1024]{2,1,0:T(8,128)S(1)}, u32[]{:S(2)}, u32[]{:S(2)}) async-start(f32[4,88,1024]{2,1,0:T(8,128)} %leaf_up.1), calls=%async_computation | async-start | bytes 2883584 | tf_op jit(solution)/shard_map/all_to_all | solution.py:506
  10.9 1.6 %collective-permute-start = (f32[64,1024]{1,0:T(8,128)}, f32[64,1024]{1,0:T(8,128)S(1)}, u32[]{:S(2)}, u32[]{:S(2)}) collective-permute-start(f32[64,1024]{1,0:T(8,128)} %refs_0_.1), channel_id=1, source_target_pairs={{0,4},{4,0},{8,12},{12,8},{16,20},{20,16},{24,28},{28,24},{1,5},{5... | collective-permute-start | bytes 786440 | tf_op jit(solution)/shard_map/ppermute | solution.py:502
  13.9 1.5 %collective-permute-start.3 = (f32[128,1024]{1,0:T(8,128)S(1)}, f32[128,1024]{1,0:T(8,128)}, u32[]{:S(2)}, u32[]{:S(2)}) collective-permute-start(f32[128,1024]{1,0:T(8,128)S(1)} %get-tuple-element.63.refs_2_), channel_id=1, source_target_pairs={{0,4},{4,0},{8,12},{12,8},{16,20},{20,16},{24,28},{28,24},{1,5},{5... | collective-permute-start | bytes 1572872 | tf_op jit(solution)/shard_map/ppermute | solution.py:504
  16.2 4.0 %collective-permute-done.refs_3_ = f32[64,1024]{1,0:T(8,128)S(1)} collective-permute-done((f32[64,1024]{1,0:T(8,128)}, f32[64,1024]{1,0:T(8,128)S(1)}, u32[]{:S(2)}, u32[]{:S(2)}) %collective-permute-start) | collective-permute-done | bytes 262176 | tf_op jit(solution)/shard_map/ppermute | solution.py:502
  20.2 3.5 %collective-permute-start.1 = (f32[64,1024]{1,0:T(8,128)S(1)}, f32[64,1024]{1,0:T(8,128)S(1)}, u32[]{:S(2)}, u32[]{:S(2)}) collective-permute-start(f32[64,1024]{1,0:T(8,128)S(1)} %collective-permute-done.refs_3_), channel_id=1, source_target_pairs={{0,8},{8,16},{16,24},{12,4},{20,12},{28,20},{1,9},{9,17},{17,25},{... | collective-permute-start | bytes 786440 | tf_op jit(solution)/shard_map/ppermute | solution.py:507
  24.4 5.1 %collective-permute-done.1.pts_ref = f32[64,1024]{1,0:T(8,128)S(1)} collective-permute-done((f32[64,1024]{1,0:T(8,128)S(1)}, f32[64,1024]{1,0:T(8,128)S(1)}, u32[]{:S(2)}, u32[]{:S(2)}) %collective-permute-start.1) | collective-permute-done | bytes 262176 | tf_op jit(solution)/shard_map/ppermute | solution.py:507
  29.5 2.1 %collective-permute-done.2.refs_4_ = f32[128,1024]{1,0:T(8,128)} collective-permute-done((f32[128,1024]{1,0:T(8,128)S(1)}, f32[128,1024]{1,0:T(8,128)}, u32[]{:S(2)}, u32[]{:S(2)}) %collective-permute-start.2) | collective-permute-done | bytes 524320 | tf_op jit(solution)/shard_map/ppermute | solution.py:504
  31.6 3.5 %collective-permute-start.4 = (f32[128,1024]{1,0:T(8,128)}, f32[128,1024]{1,0:T(8,128)}, u32[]{:S(2)}, u32[]{:S(2)}) collective-permute-start(f32[128,1024]{1,0:T(8,128)} %collective-permute-done.2.refs_4_), channel_id=1, source_target_pairs={{0,8},{8,16},{16,24},{12,4},{20,12},{28,20},{1,9},{9,17},{17,25},{... | collective-permute-start | bytes 1572872 | tf_op jit(solution)/shard_map/ppermute | solution.py:509
  35.1 7.3 %collective-permute-done.3.refs_5_ = f32[128,1024]{1,0:T(8,128)} collective-permute-done((f32[128,1024]{1,0:T(8,128)S(1)}, f32[128,1024]{1,0:T(8,128)}, u32[]{:S(2)}, u32[]{:S(2)}) %collective-permute-start.3) | collective-permute-done | bytes 524320 | tf_op jit(solution)/shard_map/ppermute | solution.py:504
  42.4 3.5 %collective-permute-start.9 = (f32[128,1024]{1,0:T(8,128)}, f32[128,1024]{1,0:T(8,128)S(1)}, u32[]{:S(2)}, u32[]{:S(2)}) collective-permute-start(f32[128,1024]{1,0:T(8,128)} %collective-permute-done.3.refs_5_), channel_id=1, source_target_pairs={{0,8},{8,16},{16,24},{12,4},{20,12},{28,20},{1,9},{9,17},{17,25},{... | collective-permute-start | bytes 1572872 | tf_op jit(solution)/shard_map/ppermute | solution.py:511
  47.7 1.6 %collective-permute-start.8 = (f32[128,256]{1,0:T(8,128)S(1)}, f32[128,256]{1,0:T(8,128)S(1)}, u32[]{:S(2)}, u32[]{:S(2)}) collective-permute-start(f32[128,256]{1,0:T(8,128)S(1)} %get-tuple-element.52.refs_0_), channel_id=1, source_target_pairs={{0,24},{4,28},{8,16},{12,20},{16,8},{20,12},{24,0},{28,4},{1,25},{... | collective-permute-start | bytes 393224 | tf_op jit(solution)/shard_map/ppermute | solution.py:518
  54.3 10.1 %near_own_pair.1.refs_3_.refs_4_ = f32[8,256,512]{2,1,0:T(8,128)S(1)} custom-call(s32[4]{0:T(128)S(1)} %pad_add_fusion.pos_ref, s32[1024]{0:T(1024)S(1)} %bitcast.12, bf16[8,256,512]{2,1,0:T(8,128)(2,1)S(1)} %get-tuple-element.36.t_ref, f32[8,8,512]{2,1,0:T(8,128)S(1)} %get-tuple-element.37.tb_ref, f32[64,1024]{1,0:T(8,128)} %refs_0_.1, ...), custom_call_target="tpu_custom_call" | custom-call | tf_op jit(solution)/shard_map/near_own_pair/pallas_call | solution.py:191
  64.5 2.7 %near_next_away.2 = (f32[128,1024]{1,0:T(8,128)S(1)}, f32[128,1024]{1,0:T(8,128)S(1)}) custom-call(s32[4]{0:T(128)S(1)} %pad_add_fusion.pos_ref, s32[1024]{0:T(1024)S(1)} %bitcast.13, bf16[8,256,512]{2,1,0:T(8,128)(2,1)S(1)} %get-tuple-element.36.t_ref, f32[8,8,512]{2,1,0:T(8,128)S(1)} %get-tuple-element.37.tb_ref, ...), custom_call_target="tpu_custom_call" | custom-call | tf_op jit(solution)/shard_map/near_next_away/pallas_call | solution.py:191
  67.8 2.0 %near_next_away.3 = (f32[128,1024]{1,0:T(8,128)S(1)}, f32[128,1024]{1,0:T(8,128)S(1)}) custom-call(s32[4]{0:T(128)S(1)} %pad_add_fusion.pos_ref, s32[1024]{0:T(1024)S(1)} %bitcast.14, bf16[8,256,512]{2,1,0:T(8,128)(2,1)S(1)} %get-tuple-element.36.t_ref, f32[8,8,512]{2,1,0:T(8,128)S(1)} %get-tuple-element.37.tb_ref, ...), custom_call_target="tpu_custom_call" | custom-call | tf_op jit(solution)/shard_map/near_next_away/pallas_call | solution.py:191
  71.4 7.6 %collective-permute-start.10 = (f32[4,128,256]{2,1,0:T(8,128)}, f32[4,128,256]{2,1,0:T(8,128)}, u32[]{:S(2)}, u32[]{:S(2)}) collective-permute-start(f32[4,128,256]{2,1,0:T(8,128)} %pad_maximum_fusion), channel_id=1, source_target_pairs={{0,4},{4,0},{8,12},{12,8},{16,20},{20,16},{24,28},{28,24},{1,5},{5... | collective-permute-start | bytes 1572872 | tf_op jit(solution)/shard_map/ppermute | solution.py:532
  79.9 5.7 %collective-permute-start.15 = (f32[128,1024]{1,0:T(8,128)}, f32[128,1024]{1,0:T(8,128)}, u32[]{:S(2)}, u32[]{:S(2)}) collective-permute-start(f32[128,1024]{1,0:T(8,128)} %add.13), channel_id=1, source_target_pairs={{2,0},{3,1},{0,2},{1,3},{6,4},{7,5},{4,6},{5,7},{10,8},{11,9},{8,1... | collective-permute-start | bytes 1572872 | tf_op jit(solution)/shard_map/ppermute | solution.py:492
  85.9 6.0 %collective-permute-done.10.refs_4_ = f32[4,128,256]{2,1,0:T(8,128)} collective-permute-done((f32[4,128,256]{2,1,0:T(8,128)}, f32[4,128,256]{2,1,0:T(8,128)}, u32[]{:S(2)}, u32[]{:S(2)}) %collective-permute-start.10) | collective-permute-done | bytes 524320 | tf_op jit(solution)/shard_map/ppermute | solution.py:532
  91.9 1.9 %copy-done.10 = f32[6,512,256]{2,1,0:T(8,128)S(1)} copy-done((f32[6,512,256]{2,1,0:T(8,128)S(1)}, f32[6,512,256]{2,1,0:T(8,128)}, u32[]{:S(2)}) %copy-start.10) | copy-done | bytes 3145752
  96.5 7.0 %far.1.refs_5_.refs_0_ = f32[64,256]{1,0:T(8,128)S(1)} custom-call(s32[4]{0:T(128)S(1)} %pad_add_fusion.pos_ref, s32[14,4]{1,0:T(8,128)S(1)} %copy.10.far_ref, s32[6,1,256]{2,1,0:T(1,128)S(1)} %broadcast_in_dim.3.node_ref, f32[6,512,256]{2,1,0:T(8,128)S(1)} %copy-done.10, f32[128,256]{1,0:T(8,128)S(1)} %copy-done.20, f32[128,256]{1,0:T(8,128)S(1)} %copy-done.26, ...), custom_call_target="tpu_custom_call" | custom-call | tf_op jit(solution)/shard_map/far/pallas_call | solution.py:400
  104.7 4.9 %near_next_home.1 = (f32[128,1024]{1,0:T(8,128)S(1)}, f32[128,1024]{1,0:T(8,128)S(1)}, f32[128,1024]{1,0:T(8,128)S(1)}, f32[128,1024]{1,0:T(8,128)S(1)}) custom-call(s32[4]{0:T(128)S(1)} %pad_add_fusion.pos_ref, s32[1024]{0:T(1024)S(1)} %bitcast.15, bf16[8,256,512]{2,1,0:T(8,128)(2,1)S(1)} %get-tuple-element.36.t_ref, f32[8,8,512]{2,1,0:T(8,128)S(1)} %copy-done.12, ...), custom_call_target="tpu_custom_call" | custom-call | tf_op jit(solution)/shard_map/near_next_home/pallas_call | solution.py:191
  110.4 6.4 %collective-permute-start.14 = (f32[64,256]{1,0:T(8,128)S(1)}, f32[64,256]{1,0:T(8,128)S(1)}, u32[]{:S(2)}, u32[]{:S(2)}) collective-permute-start(f32[64,256]{1,0:T(8,128)S(1)} %far.1.refs_5_.refs_0_), channel_id=1, source_target_pairs={{3,0},{2,1},{1,2},{0,3},{7,4},{6,5},{5,6},{4,7},{11,8},{10,9},{9,1... | collective-permute-start | bytes 196616 | tf_op jit(solution)/shard_map/ppermute | solution.py:489
  119.3 2.0 %collective-permute-done.13.refs_2_ = f32[64,256]{1,0:T(8,128)S(1)} collective-permute-done((f32[64,256]{1,0:T(8,128)S(1)}, f32[64,256]{1,0:T(8,128)S(1)}, u32[]{:S(2)}, u32[]{:S(2)}) %collective-permute-start.13) | collective-permute-done | bytes 65568 | tf_op jit(solution)/shard_map/ppermute | solution.py:489
  121.3 2.2 %join.1 = f32[256,1024]{1,0:T(8,128)} custom-call(s32[4]{0:T(128)S(1)} %pad_add_fusion.pos_ref, f32[2,512,256]{2,1,0:T(8,128)S(1)} %copy-done.7, f32[64,256]{1,0:T(8,128)S(1)} %far.1.refs_5_.refs_0_, f32[64,256]{1,0:T(8,128)S(1)} %collective-permute-done.12.refs_1_, f32[64,256]{1,0:T(8,128)S(1)} %collective-permute-done.13.refs_2_, ...), custom_call_target="tpu_custom_call" | custom-call | tf_op jit(solution)/shard_map/join/pallas_call | solution.py:458
  (102 shorter events, 24.0 us)
Async XLA Ops:
  7.1 39.2 %copy-start.30 = (s32[1,256]{1,0:T(1,128)S(1)}, s32[1,256]{1,0:T(1,128)}, u32[]{:S(2)}) copy-start(s32[1,256]{1,0:T(1,128)} %index_ref.1) | copy-start | bytes 3076
  7.2 35.2 %all-to-all-start = ((f32[4,88,1024]{2,1,0:T(8,128)}), f32[4,88,1024]{2,1,0:T(8,128)S(1)}, u32[]{:S(2)}, u32[]{:S(2)}) async-start(f32[4,88,1024]{2,1,0:T(8,128)} %leaf_up.1), calls=%async_computation | async-start | bytes 2883584 | tf_op jit(solution)/shard_map/all_to_all | solution.py:506
  10.9 9.4 %collective-permute-start = (f32[64,1024]{1,0:T(8,128)}, f32[64,1024]{1,0:T(8,128)S(1)}, u32[]{:S(2)}, u32[]{:S(2)}) collective-permute-start(f32[64,1024]{1,0:T(8,128)} %refs_0_.1), channel_id=1, source_target_pairs={{0,4},{4,0},{8,12},{12,8},{16,20},{20,16},{24,28},{28,24},{1,5},{5... | collective-permute-start | bytes 786440 | tf_op jit(solution)/shard_map/ppermute | solution.py:502
  12.6 19.0 %collective-permute-start.2 = (f32[128,1024]{1,0:T(8,128)S(1)}, f32[128,1024]{1,0:T(8,128)}, u32[]{:S(2)}, u32[]{:S(2)}) collective-permute-start(f32[128,1024]{1,0:T(8,128)S(1)} %get-tuple-element.64.refs_1_), channel_id=1, source_target_pairs={{0,4},{4,0},{8,12},{12,8},{16,20},{20,16},{24,28},{28,24},{1,5},{5... | collective-permute-start | bytes 1572872 | tf_op jit(solution)/shard_map/ppermute | solution.py:504
  13.9 28.4 %collective-permute-start.3 = (f32[128,1024]{1,0:T(8,128)S(1)}, f32[128,1024]{1,0:T(8,128)}, u32[]{:S(2)}, u32[]{:S(2)}) collective-permute-start(f32[128,1024]{1,0:T(8,128)S(1)} %get-tuple-element.63.refs_2_), channel_id=1, source_target_pairs={{0,4},{4,0},{8,12},{12,8},{16,20},{20,16},{24,28},{28,24},{1,5},{5... | collective-permute-start | bytes 1572872 | tf_op jit(solution)/shard_map/ppermute | solution.py:504
  20.2 9.3 %collective-permute-start.1 = (f32[64,1024]{1,0:T(8,128)S(1)}, f32[64,1024]{1,0:T(8,128)S(1)}, u32[]{:S(2)}, u32[]{:S(2)}) collective-permute-start(f32[64,1024]{1,0:T(8,128)S(1)} %collective-permute-done.refs_3_), channel_id=1, source_target_pairs={{0,8},{8,16},{16,24},{12,4},{20,12},{28,20},{1,9},{9,17},{17,25},{... | collective-permute-start | bytes 786440 | tf_op jit(solution)/shard_map/ppermute | solution.py:507
  31.6 32.9 %collective-permute-start.4 = (f32[128,1024]{1,0:T(8,128)}, f32[128,1024]{1,0:T(8,128)}, u32[]{:S(2)}, u32[]{:S(2)}) collective-permute-start(f32[128,1024]{1,0:T(8,128)} %collective-permute-done.2.refs_4_), channel_id=1, source_target_pairs={{0,8},{8,16},{16,24},{12,4},{20,12},{28,20},{1,9},{9,17},{17,25},{... | collective-permute-start | bytes 1572872 | tf_op jit(solution)/shard_map/ppermute | solution.py:509
  42.4 25.4 %collective-permute-start.9 = (f32[128,1024]{1,0:T(8,128)}, f32[128,1024]{1,0:T(8,128)S(1)}, u32[]{:S(2)}, u32[]{:S(2)}) collective-permute-start(f32[128,1024]{1,0:T(8,128)} %collective-permute-done.3.refs_5_), channel_id=1, source_target_pairs={{0,8},{8,16},{16,24},{12,4},{20,12},{28,20},{1,9},{9,17},{17,25},{... | collective-permute-start | bytes 1572872 | tf_op jit(solution)/shard_map/ppermute | solution.py:511
  46.4 21.4 %copy-start.2 = (bf16[2,512,256]{2,1,0:T(8,128)(2,1)}, bf16[2,512,256]{2,1,0:T(8,128)(2,1)S(1)}, u32[]{:S(2)}) copy-start(bf16[2,512,256]{2,1,0:T(8,128)(2,1)S(1)} %get-tuple-element.39.refs_0_) | copy-start | bytes 1572868
  46.4 21.4 %copy-start.4 = (f32[2,512,128]{2,1,0:T(8,128)}, f32[2,512,128]{2,1,0:T(8,128)S(1)}, u32[]{:S(2)}) copy-start(f32[2,512,128]{2,1,0:T(8,128)S(1)} %get-tuple-element.40.refs_1_) | copy-start | bytes 1572868
  47.7 22.8 %copy-start.19 = (f32[128,256]{1,0:T(8,128)}, f32[128,256]{1,0:T(8,128)S(1)}, u32[]{:S(2)}) copy-start(f32[128,256]{1,0:T(8,128)S(1)} %get-tuple-element.52.refs_0_) | copy-start | bytes 393220
  47.7 22.8 %collective-permute-start.8 = (f32[128,256]{1,0:T(8,128)S(1)}, f32[128,256]{1,0:T(8,128)S(1)}, u32[]{:S(2)}, u32[]{:S(2)}) collective-permute-start(f32[128,256]{1,0:T(8,128)S(1)} %get-tuple-element.52.refs_0_), channel_id=1, source_target_pairs={{0,24},{4,28},{8,16},{12,20},{16,8},{20,12},{24,0},{28,4},{1,25},{... | collective-permute-start | bytes 393224 | tf_op jit(solution)/shard_map/ppermute | solution.py:518
  49.4 21.1 %collective-permute-start.7 = (f32[128,256]{1,0:T(8,128)S(1)}, f32[128,256]{1,0:T(8,128)S(1)}, u32[]{:S(2)}, u32[]{:S(2)}) collective-permute-start(f32[128,256]{1,0:T(8,128)S(1)} %get-tuple-element.52.refs_0_), channel_id=1, source_target_pairs={{0,16},{4,20},{8,24},{12,28},{16,0},{20,4},{24,8},{28,12},{1,17},{... | collective-permute-start | bytes 393224 | tf_op jit(solution)/shard_map/ppermute | solution.py:518
  50.6 19.9 %collective-permute-start.6 = (f32[128,256]{1,0:T(8,128)S(1)}, f32[128,256]{1,0:T(8,128)S(1)}, u32[]{:S(2)}, u32[]{:S(2)}) collective-permute-start(f32[128,256]{1,0:T(8,128)S(1)} %get-tuple-element.52.refs_0_), channel_id=1, source_target_pairs={{0,8},{4,12},{8,0},{12,4},{16,24},{20,28},{24,16},{28,20},{1,9},{5... | collective-permute-start | bytes 393224 | tf_op jit(solution)/shard_map/ppermute | solution.py:518
  67.2 11.9 %collective-permute-start.5 = (f32[128,1024]{1,0:T(8,128)S(1)}, f32[128,1024]{1,0:T(8,128)S(1)}, u32[]{:S(2)}, u32[]{:S(2)}) collective-permute-start(f32[128,1024]{1,0:T(8,128)S(1)} %get-tuple-element.43), channel_id=1, source_target_pairs={{1,0},{0,1},{3,2},{2,3},{5,4},{4,5},{7,6},{6,7},{9,8},{8,9},{11,10... | collective-permute-start | bytes 1572872 | tf_op jit(solution)/shard_map/ppermute | solution.py:489
  69.9 15.7 %collective-permute-start.11 = (f32[128,1024]{1,0:T(8,128)S(1)}, f32[128,1024]{1,0:T(8,128)S(1)}, u32[]{:S(2)}, u32[]{:S(2)}) collective-permute-start(f32[128,1024]{1,0:T(8,128)S(1)} %get-tuple-element.47), channel_id=1, source_target_pairs={{1,0},{0,1},{3,2},{2,3},{5,4},{4,5},{7,6},{6,7},{9,8},{8,9},{11,10... | collective-permute-start | bytes 1572872 | tf_op jit(solution)/shard_map/ppermute | solution.py:489
  71.4 20.5 %collective-permute-start.10 = (f32[4,128,256]{2,1,0:T(8,128)}, f32[4,128,256]{2,1,0:T(8,128)}, u32[]{:S(2)}, u32[]{:S(2)}) collective-permute-start(f32[4,128,256]{2,1,0:T(8,128)} %pad_maximum_fusion), channel_id=1, source_target_pairs={{0,4},{4,0},{8,12},{12,8},{16,20},{20,16},{24,28},{28,24},{1,5},{5... | collective-permute-start | bytes 1572872 | tf_op jit(solution)/shard_map/ppermute | solution.py:532
  79.9 37.0 %collective-permute-start.15 = (f32[128,1024]{1,0:T(8,128)}, f32[128,1024]{1,0:T(8,128)}, u32[]{:S(2)}, u32[]{:S(2)}) collective-permute-start(f32[128,1024]{1,0:T(8,128)} %add.13), channel_id=1, source_target_pairs={{2,0},{3,1},{0,2},{1,3},{6,4},{7,5},{4,6},{5,7},{10,8},{11,9},{8,1... | collective-permute-start | bytes 1572872 | tf_op jit(solution)/shard_map/ppermute | solution.py:492
  85.7 31.5 %collective-permute-start.16 = (f32[128,1024]{1,0:T(8,128)S(1)}, f32[128,1024]{1,0:T(8,128)}, u32[]{:S(2)}, u32[]{:S(2)}) collective-permute-start(f32[128,1024]{1,0:T(8,128)S(1)} %add.12.refs_5_), channel_id=1, source_target_pairs={{2,0},{3,1},{0,2},{1,3},{6,4},{7,5},{4,6},{5,7},{10,8},{11,9},{8,1... | collective-permute-start | bytes 1572872 | tf_op jit(solution)/shard_map/ppermute | solution.py:492
  109.6 11.7 %collective-permute-start.17 = (f32[128,1024]{1,0:T(8,128)S(1)}, f32[128,1024]{1,0:T(8,128)S(1)}, u32[]{:S(2)}, u32[]{:S(2)}) collective-permute-start(f32[128,1024]{1,0:T(8,128)S(1)} %get-tuple-element.61), channel_id=1, source_target_pairs={{1,0},{0,1},{3,2},{2,3},{5,4},{4,5},{7,6},{6,7},{9,8},{8,9},{11,10... | collective-permute-start | bytes 1572872 | tf_op jit(solution)/shard_map/ppermute | solution.py:489
  110.3 11.0 %collective-permute-start.18 = (f32[128,1024]{1,0:T(8,128)S(1)}, f32[128,1024]{1,0:T(8,128)S(1)}, u32[]{:S(2)}, u32[]{:S(2)}) collective-permute-start(f32[128,1024]{1,0:T(8,128)S(1)} %get-tuple-element.62), channel_id=1, source_target_pairs={{1,0},{0,1},{3,2},{2,3},{5,4},{4,5},{7,6},{6,7},{9,8},{8,9},{11,10... | collective-permute-start | bytes 1572872 | tf_op jit(solution)/shard_map/ppermute | solution.py:489
  110.4 8.9 %collective-permute-start.14 = (f32[64,256]{1,0:T(8,128)S(1)}, f32[64,256]{1,0:T(8,128)S(1)}, u32[]{:S(2)}, u32[]{:S(2)}) collective-permute-start(f32[64,256]{1,0:T(8,128)S(1)} %far.1.refs_5_.refs_0_), channel_id=1, source_target_pairs={{3,0},{2,1},{1,2},{0,3},{7,4},{6,5},{5,6},{4,7},{11,8},{10,9},{9,1... | collective-permute-start | bytes 196616 | tf_op jit(solution)/shard_map/ppermute | solution.py:489
  116.9 4.4 %collective-permute-start.13 = (f32[64,256]{1,0:T(8,128)S(1)}, f32[64,256]{1,0:T(8,128)S(1)}, u32[]{:S(2)}, u32[]{:S(2)}) collective-permute-start(f32[64,256]{1,0:T(8,128)S(1)} %far.1.refs_5_.refs_0_), channel_id=1, source_target_pairs={{2,0},{3,1},{0,2},{1,3},{6,4},{7,5},{4,6},{5,7},{10,8},{11,9},{8,1... | collective-permute-start | bytes 196616 | tf_op jit(solution)/shard_map/ppermute | solution.py:489
  117.2 4.1 %collective-permute-start.12 = (f32[64,256]{1,0:T(8,128)S(1)}, f32[64,256]{1,0:T(8,128)S(1)}, u32[]{:S(2)}, u32[]{:S(2)}) collective-permute-start(f32[64,256]{1,0:T(8,128)S(1)} %far.1.refs_5_.refs_0_), channel_id=1, source_target_pairs={{1,0},{0,1},{3,2},{2,3},{5,4},{4,5},{7,6},{6,7},{9,8},{8,9},{11,10... | collective-permute-start | bytes 196616 | tf_op jit(solution)/shard_map/ppermute | solution.py:489
  (30 other events, 225.1 us)

commit v5 on v4

--- a/solution.py
+++ b/solution.py
@@ -59,14 +59,16 @@
 
 
 def near_body(
-    xs, sets, leaves_at, rows, row, has_acc, nout, pos_ref, times_ref, t_ref, tb_ref, *refs
+    xs, sets, leaves_at, rows, row, nacc, nout, pos_ref, got_ref, t_ref, tb_ref, *refs
 ):
     nset = len(sets)
-    if has_acc:
-        s_scr, sb_scr, w_scr, o_scr, k_scr, times_scr, list_ref = refs[-7:]
-        outs = refs[-7 - nout : -7]
+    if nacc:
+        s_scr, sb_scr, w_scr, o_scr, k_scr, times_scr, list_ref, times_ref, sem = refs[-9:]
+        outs = refs[-9 - nout : -9]
     else:
-        o_scr, s_scr, sb_scr, w_scr, k_scr, times_scr, list_ref = refs[-7:]
+        o_scr, s_scr, sb_scr, w_scr, k_scr, times_scr, list_ref, times_ref, sem = refs[-9:]
+    copy = pltpu.make_async_copy(got_ref.at[:, F : F + EXTRA, :128], times_ref, sem)
+    copy.start()
     at = 0
     for k, (_, ready, chunks) in enumerate(sets):
         heads = refs[at : at + 1 + ready]
@@ -89,8 +91,8 @@
                 w_scr[j, rows + c * each : rows + (c + 1) * each, :] = lo
     start, stop = leaves_at
     for t in range(start, stop):
-        if has_acc:
-            o_scr[t - start] = refs[at][t, row : row + rows, :]
+        if nacc:
+            o_scr[t - start] = sum(ref[t, row : row + rows, :] for ref in refs[at : at + nacc])
         else:
             o_scr[t - start] = jnp.zeros((rows, LEAF), F32)
 
@@ -101,13 +103,13 @@
         relative = {"own": 1, "pair": 2 - 2 * odd, "next": 2 * odd}[kind]
         column.append(relative * leaves + 2 * (2 * x + core))
 
+    copy.wait()
     count = jnp.int32(0)
     list_ref[0] = 0
-    times_scr[0] = 0
     for t in range(start, stop):
         for j in range(2 * nset):
             helper = 2 * lax.rem(x + t // 4, xs) + (core if t // 2 % 2 == 0 else 1 - core)
-            times = times_ref[(2 * helper + t % 2) * 128 + column[j // 2] + j % 2]
+            times = times_ref[helper, t % 2, column[j // 2] + j % 2]
 
             @pl.when(times > 0)
             def _(count=count, t=t, j=j, times=times):
@@ -133,7 +135,7 @@
     def apply(index, slot):
         code = list_ref[index]
         t, j = code // 8 - start, code % 8
-        factor = times_scr[index].astype(F32)
+        factor = times_scr[index]
         for half in range(2):
             cols = slice(half * 256, (half + 1) * 256)
             both = dot(w_scr[j], k_scr[slot, :LEAF, cols])
@@ -156,7 +158,7 @@
         return carry
 
     lax.fori_loop(0, (count + 1) // 2, pair, jnp.int32(0))
-    if has_acc:
+    if nacc:
         tall = outs[0].shape[0]
         for n, ref in enumerate(outs):
             t, top = 2 * (n // (rows // tall)), n % (rows // tall) * tall
@@ -165,7 +167,7 @@
                 ref[:, cols] = o_scr[t + leaf, top : top + tall, :]
 
 
-def near_call(name, where, targets, leaves_at, sources, rows, row=0, acc=None, after=()):
+def near_call(name, where, targets, leaves_at, sources, rows, row=0, acc=(), after=()):
     nset = len(sources)
     start, stop = leaves_at
     tall = R // 2
@@ -178,23 +180,25 @@
         pltpu.VMEM((2 * nset, 2 * rows, LEAF), BF),
         pltpu.VMEM((stop - start, rows, LEAF), F32),
         pltpu.VMEM((2, 2 * LEAF, LEAF), BF),
+        pltpu.SMEM((2 * nset * (stop - start),), F32),
         pltpu.SMEM((2 * nset * (stop - start),), jnp.int32),
-        pltpu.SMEM((2 * nset * (stop - start),), jnp.int32),
+        pltpu.SMEM((where[1].shape[0], EXTRA, 128), F32),
+        pltpu.SemaphoreType.DMA,
     ]
-    if acc is None:
+    if not acc:
         out = [jax.ShapeDtypeStruct((stop - start, rows, LEAF), F32)]
         scratch.pop(3)
     else:
-        operands.append(acc)
+        operands += list(acc)
         out = [jax.ShapeDtypeStruct((tall, 2 * LEAF), F32)] * ((stop - start) // 2 * (rows // tall))
     sets = tuple((kind, len(heads) - 1, len(chunks)) for kind, heads, chunks in sources)
     return pl.pallas_call(
         partial(
-            near_body, targets[0].shape[0] // 4, sets, leaves_at, rows, row, acc is not None, len(out)
+            near_body, targets[0].shape[0] // 4, sets, leaves_at, rows, row, len(acc), len(out)
         ),
         name=name,
         out_shape=out,
-        in_specs=[smem, smem]
+        in_specs=[smem, pl.BlockSpec(memory_space=pl.ANY)]
         + [vmem] * (2 + len(operands))
         + [pl.BlockSpec(memory_space=pl.ANY)] * len(after),
         out_specs=[vmem] * len(out),
@@ -269,13 +273,13 @@
 def leaf_call(xs, pos, near_count, near_src, points, weights, interp):
     vmem = pl.BlockSpec(memory_space=pltpu.VMEM)
     smem = pl.BlockSpec(memory_space=pltpu.SMEM)
-    anywhere = pl.BlockSpec(memory_space=pl.ANY)
+    hbm = pl.BlockSpec(memory_space=pltpu.HBM)
     height = F + EXTRA + share_rows(xs)
     return pl.pallas_call(
         partial(leaf_body, xs),
         name="leaf_up",
         out_shape=jax.ShapeDtypeStruct((2 * xs, height, 2 * LEAF), F32),
-        in_specs=[smem, smem, smem, anywhere, anywhere, anywhere],
+        in_specs=[smem, smem, smem, hbm, hbm, hbm],
         out_specs=vmem,
         scratch_shapes=[
             pltpu.VMEM(points.shape, F32),
@@ -306,12 +310,14 @@
         hot = spot + helper * (2 * LEAF) == index_ref[...]
         total = total + dot(side[: 2 * F], hot.astype(F32).astype(BF))
         value = value + msgs[helper, F + EXTRA :, :]
-    out_ref[:F, :] = total[:F] + total[F:]
-    for i in range(rows // tall):
-        out_ref[F + i * tall : F + (i + 1) * tall, :] = value[:, i * SK : (i + 1) * SK]
-
-
-def skel_call(xs, pos, index, msgs):
+    for n in range(out_ref.shape[0]):
+        out_ref[n, :F, :] = total[:F] + total[F:]
+        for i in range(rows // tall):
+            part = slice(F + i * tall, F + (i + 1) * tall)
+            out_ref[n, part, :] = value[:, i * SK : (i + 1) * SK]
+
+
+def skel_call(xs, copies, pos, index, msgs):
     rows = R // (2 * xs)
     nblk = 2 * xs
     vmem = pl.BlockSpec(memory_space=pltpu.VMEM)
@@ -319,7 +325,7 @@
         partial(skel_body, xs),
         name="skeleton",
         out_shape=[
-            jax.ShapeDtypeStruct((F + rows, SK), F32),
+            jax.ShapeDtypeStruct((copies, F + rows, SK), F32),
             jax.ShapeDtypeStruct((2 * nblk, 4 * F, LEAF), BF),
             jax.ShapeDtypeStruct((2 * nblk, 8, LEAF), F32),
         ],
@@ -337,47 +343,43 @@
     return sum((groups >> step for step in range(level)))
 
 
-def far_body(groups, rows, pos_ref, far_ref, node_ref, transfer_ref, *refs):
-    pieces, beside = refs[: groups // 2], refs[groups // 2]
+def far_body(groups, rows, pos_ref, far_ref, node_ref, transfer_ref, alike_ref, beside_ref, *refs):
     out_ref, p_scr, u_scr, f_scr = refs[-4:]
     levels = groups.bit_length() - 1
     group = pos_ref[2]
-    start = [sum(groups >> step for step in range(level)) for level in range(levels)]
-    for n, piece in enumerate(pieces):
-        p_scr[2 * n] = piece[:F, :]
-        u_scr[2 * n] = piece[F:, :]
-        p_scr[2 * n + 1] = beside[n, :F, :]
-        u_scr[2 * n + 1] = beside[n, F:, :]
+    odd = group % 2
+    start = [list_start(level, groups) for level in range(levels)]
+    for n in range(groups // 2):
+        p_scr[2 * n + odd] = alike_ref[n, :F, :]
+        u_scr[2 * n + odd] = alike_ref[n, F:, :]
+        p_scr[2 * n + 1 - odd] = beside_ref[n, :F, :]
+        u_scr[2 * n + 1 - odd] = beside_ref[n, F:, :]
     spot = lax.broadcasted_iota(jnp.int32, (2 * SK, SK), 0)
     for level in range(1, levels):
-        bit = (group >> (level - 1)) & 1
-        for m in range(groups >> level):
-            row = upper_start(level, groups) + (m ^ (group >> level))
-            left = start[level - 1] + 2 * m + bit
-            right = start[level - 1] + 2 * m + 1 - bit
+        for n in range(groups >> level):
+            row = upper_start(level, groups) + n
+            left = start[level - 1] + 2 * n
             hot = (spot == node_ref[row]).astype(F32).astype(BF)
-            pts = jnp.concatenate([p_scr[left], p_scr[right]], axis=1)
-            hi, lo = halves(pts)
+            hi, lo = halves(jnp.concatenate([p_scr[left], p_scr[left + 1]], axis=1))
             both = dot(jnp.concatenate([hi, lo], axis=0), hot)
-            p_scr[start[level] + m] = both[:F] + both[F:]
-            vals = jnp.concatenate([u_scr[left], u_scr[right]], axis=1)
-            u_scr[start[level] + m] = dot3(vals, transfer_ref[row])
+            p_scr[start[level] + n] = both[:F] + both[F:]
+            vals = jnp.concatenate([u_scr[left], u_scr[left + 1]], axis=1)
+            u_scr[start[level] + n] = dot3(vals, transfer_ref[row])
     for level in range(levels):
         node = group >> level
-        side, off = target_side(p_scr[start[level]])
+        side, off = target_side(p_scr[start[level] + node])
         f_scr[level] = jnp.zeros((rows, SK), F32)
 
-        def one(m, carry, level=level, node=node, side=side, off=off):
+        def one(n, carry, level=level, node=node, side=side, off=off):
             hits = jnp.int32(0)
             for slot in range(FL):
-                entry = far_ref[list_start(level, groups) + node, slot]
-                hits = hits + (entry == (m ^ node)).astype(jnp.int32)
+                hits = hits + (far_ref[slot, start[level] + node] == n).astype(jnp.int32)
 
             @pl.when(hits > 0)
             def _():
-                src, src_off = source_side(p_scr[start[level] + m])
+                src, src_off = source_side(p_scr[start[level] + n])
                 block = jnp.exp2(dot(src, side) + src_off + off)
-                term = dot3(u_scr[start[level] + m], block)
+                term = dot3(u_scr[start[level] + n], block)
                 f_scr[level] = f_scr[level] + hits.astype(F32) * term
 
             return carry
@@ -392,8 +394,8 @@
     out_ref[...] = local
 
 
-def far_call(groups, pos, far_nodes, skel_node, transfer, pieces, beside, after):
-    rows = pieces[0].shape[0] - F
+def far_call(groups, pos, far_nodes, skel_node, transfer, alike, beside, after):
+    rows = alike.shape[1] - F
     vmem = pl.BlockSpec(memory_space=pltpu.VMEM)
     smem = pl.BlockSpec(memory_space=pltpu.SMEM)
     nodes = 2 * groups
@@ -401,8 +403,7 @@
         partial(far_body, groups, rows),
         name="far",
         out_shape=jax.ShapeDtypeStruct((rows, SK), F32),
-        in_specs=[smem, smem, vmem, vmem]
-        + [vmem] * (len(pieces) + 1)
+        in_specs=[smem, smem, vmem, vmem, vmem, vmem]
         + [pl.BlockSpec(memory_space=pl.ANY)] * len(after),
         out_specs=vmem,
         scratch_shapes=[
@@ -411,7 +412,7 @@
             pltpu.VMEM((groups.bit_length(), rows, SK), F32),
         ],
         compiler_params=pltpu.CompilerParams(vmem_limit_bytes=VMEM_LIMIT),
-    )(pos, far_nodes, skel_node[:, None, :], transfer, *pieces, beside, *after)
+    )(pos, far_nodes.T, skel_node[:, None, :], transfer, alike, beside, *after)
 
 
 def final_body(xs, pos_ref, interp_ref, *refs):
@@ -431,24 +432,23 @@
             out_ref[part, cols] = total[part] + sums[c][:, cols] + sums[2 + c][:, cols]
 
 
-def add_body(*refs):
-    count = (len(refs) - 2) // 2
-    for c in range(2):
-        total = refs[c * count][...]
-        for ref in refs[c * count + 1 : (c + 1) * count]:
+def add_body(count, *refs):
+    for n, out_ref in enumerate(refs[-(len(refs) // (count + 1)) :]):
+        total = refs[n * count][...]
+        for ref in refs[n * count + 1 : (n + 1) * count]:
             total = total + ref[...]
-        refs[c - 2][...] = total
-
-
-def add_call(home, parts):
-    vmem = pl.BlockSpec(memory_space=pltpu.VMEM)
-    operands = [home[0], *parts[0], home[1], *parts[1]]
-    return pl.pallas_call(
-        add_body,
+        out_ref[...] = total
+
+
+def add_call(*sums):
+    vmem = pl.BlockSpec(memory_space=pltpu.VMEM)
+    operands = [value for terms in sums for value in terms]
+    return pl.pallas_call(
+        partial(add_body, len(sums[0])),
         name="add_parts",
-        out_shape=[jax.ShapeDtypeStruct(home[0].shape, F32)] * 2,
+        out_shape=[jax.ShapeDtypeStruct(sums[0][0].shape, F32)] * len(sums),
         in_specs=[vmem] * len(operands),
-        out_specs=[vmem] * 2,
+        out_specs=[vmem] * len(sums),
         compiler_params=pltpu.CompilerParams(vmem_limit_bytes=VMEM_LIMIT),
     )(*operands)
 
@@ -500,50 +500,52 @@
     order = [(dx, dc) for dx in range(xs) for dc in range(2)]
 
     pts_y = lax.ppermute(points, "leaf", beside)
-    w_own = [weights[:rows], weights[rows:]]
-    w_y = [lax.ppermute(chunk, "leaf", beside) for chunk in w_own]
+    w_y = [lax.ppermute(weights[c * rows : (c + 1) * rows], "leaf", beside) for c in range(2)]
     msgs = leaf_call(xs, pos, near_count, near_src, points, weights, interp)
     got = lax.all_to_all(msgs, "help", 0, 0)
     pts_z = lax.ppermute(pts_y, "leaf", across)
+
+    payload, *targets = skel_call(xs, groups // 2, pos, skel_group, got)
+    where = (pos, got)
+    parity = [[n for n in range(groups) if n % 2 == odd] for odd in range(2)]
+    alike = lax.all_to_all(payload, "leaf", 0, 0, axis_index_groups=parity)
     pts_z, w_y[0] = together(pts_z, w_y[0])
     w_z = [lax.ppermute(w_y[0], "leaf", across)]
-    got, w_y = together(got, w_y)
+    (own,) = near_call(
+        "near_own", where, targets, (0, 2 * helpers), [("own", (points,), [weights])], R
+    )
+    own, w_y[1] = together(own, w_y[1])
     w_z.append(lax.ppermute(w_y[1], "leaf", across))
-
-    times = got[:, F : F + 2, :128].astype(jnp.int32).reshape(-1)
-    where = (pos, times)
-    payload, *targets = skel_call(xs, pos, skel_group, got)
-    pieces = [payload]
-    for mask in range(2, groups, 2):
-        pieces.append(lax.ppermute(payload, "leaf", [(i, i ^ mask) for i in range(groups)]))
-
-    sources = [("own", (points,), w_own), ("pair", (pts_y,), w_y)]
-    (near,) = near_call("near_own_pair", where, targets, (0, 2 * helpers), sources, R)
     z_side = source_call(pts_z)
+    alike, w_y[1] = together(alike, w_y[1])
+    side = lax.ppermute(alike, "leaf", beside)
+    (pair,) = near_call(
+        "near_pair", where, targets, (0, 2 * helpers), [("pair", (pts_y,), w_y)], R
+    )
+
     sums, part = [], []
     for c in range(2):
         part = near_call(
             "near_next_away", where, targets, (4, 2 * helpers), [("next", z_side, w_z[c : c + 1])],
-            rows, c * rows, near, part[:1],
+            rows, c * rows, (own, pair), part[:1],
         )
         kept, given = part[::2], part[1::2]
         sums.append((kept, [from_help(value, 0, 1) for value in given]))
-    pieces, part = together(pieces, part)
-    side = lax.ppermute(jnp.stack(pieces), "leaf", beside)
     parts = []
     for c in range(2):
         kept, mates = sums[c]
         if c == 0:
-            mates, pieces = together(mates, pieces)
-        both = [k + m for k, m in zip(kept, mates)]
+            mates, side = together(mates, side)
+        both = add_call(*zip(kept, mates))
         parts.append([to_help(value, dx + 1) for dx, value in enumerate(both)])
-    v_own = far_call(groups, pos, far_nodes, skel_node, transfer, pieces, side, both[:1])
+    v_own = far_call(groups, pos, far_nodes, skel_node, transfer, alike, side, both[:1])
     values = [v_own] + [from_help(v_own, dx, dc) for dx, dc in order[1:]]
     home = near_call(
-        "near_next_home", where, targets, (0, 4), [("next", z_side, w_z)], R, 0, near, [v_own]
+        "near_next_home", where, targets, (0, 4), [("next", z_side, w_z)], R, 0, (own, pair), [v_own]
     )
     mate = [from_help(value, 0, 1) for value in home[2:]]
-    return final_call(xs, pos, interp, add_call(home[:2], parts), mate, values)
+    mine = add_call(*[[home[c], *parts[c]] for c in range(2)])
+    return final_call(xs, pos, interp, mine, mate, values)
 
 
 def solution(mesh):

time: 124 us -> 132 us (1.065)
  the two profiles are of different devices: /device:TPU:8 before, /device:TPU:6 now
where the time goes in v5:
time: 132 us
  Pallas kernels  47.8 us (36%)
  waiting for transfers between devices  41.8 us (32%)
  starting transfers between devices  27.7 us (21%)
  local copies, waits for them, and re-layouts  14.1 us (11%)
    pallas_call x5, Pallas kernels, near_call(): pl.pallas_call(partial(near_body, targets[0].shape[0] // 4, sets, leaves_...  34.5 us
    ppermute x1, waiting for transfers between devices, shards(): pts_z = lax.ppermute(pts_y, 'leaf', across)  15.3 us
    all_to_all x1, waiting for transfers between devices, shards(): got = lax.all_to_all(msgs, 'help', 0, 0)  13.8 us
    unnamed x46, local copies, waits for them, and re-layouts  13 us
    ppermute x2, waiting for transfers between devices, to_help(): return lax.ppermute(value, 'help', help_pairs(xs, -dx, 0))  8.91 us
    ppermute x1, starting transfers between devices, shards(): side = lax.ppermute(alike, 'leaf', beside)  8.16 us
    pallas_call x1, Pallas kernels, far_call(): pl.pallas_call(partial(far_body, groups, rows), name='far', out_shape=jax...  6.9 us
    all_to_all x1, starting transfers between devices, shards(): alike = lax.all_to_all(payload, 'leaf', 0, 0, axis_index_groups=parity)  4.87 us
  transfers between devices with their start and end apart: 18, of which 5 were waited for; matrix products, arithmetic and copies ran while one was open for 1% of the time, Pallas kernels for 33%

profile of v5, /device:TPU:6, one launch (start us, length us, event | category | flops | bytes accessed | tf_op | source)
XLA Modules:
  0.0 131.9 jit_solution(12915021862271815939)
XLA Ops:
  0.1 1.2 copy-done.2
  3.9 2.2 %leaf_up.1 = f32[4,88,1024]{2,1,0:T(8,128)S(1)} custom-call(s32[4]{0:T(128)S(1)} %pad_add_fusion.pos_ref, s32[1,2]{1,0:T(1,128)S(1)} %copy-done.21, s32[2,32]{1,0:T(2,128)S(1)} %copy-done.19, f32[64,1024]{1,0:T(8,128)} %refs_0_.1, f32[256,1024]{1,0:T(8,128)S(1)} %copy-done.2, f32[2,512,256]{2,1,0:T(8,128)S(1)} %copy-done.10), custom_call_target="tpu_custom_call" | custom-call | tf_op jit(solution)/shard_map/leaf_up/pallas_call | solution.py:278
  7.2 4.2 %all-to-all-start = ((f32[4,88,1024]{2,1,0:T(8,128)}), f32[4,88,1024]{2,1,0:T(8,128)S(1)}, u32[]{:S(2)}, u32[]{:S(2)}) async-start(f32[4,88,1024]{2,1,0:T(8,128)} %copy-done.5), calls=%async_computation | async-start | bytes 2883584 | tf_op jit(solution)/shard_map/all_to_all | solution.py:505
  12.6 2.0 %collective-permute-start.3 = (f32[128,1024]{1,0:T(8,128)}, f32[128,1024]{1,0:T(8,128)}, u32[]{:S(2)}, u32[]{:S(2)}) collective-permute-start(f32[128,1024]{1,0:T(8,128)} %get-tuple-element.51), channel_id=1, source_target_pairs={{0,4},{4,0},{8,12},{12,8},{16,20},{20,16},{24,28},{28,24},{1,5},{5... | collective-permute-start | bytes 1572872 | tf_op jit(solution)/shard_map/ppermute | solution.py:503
  14.6 13.8 %all-to-all-done.msgs.got_ref = f32[4,88,1024]{2,1,0:T(8,128)S(1)} async-done(((f32[4,88,1024]{2,1,0:T(8,128)}), f32[4,88,1024]{2,1,0:T(8,128)S(1)}, u32[]{:S(2)}, u32[]{:S(2)}) %all-to-all-start) | async-done | bytes 1441824 | tf_op jit(solution)/shard_map/all_to_all | solution.py:505
  28.4 1.3 skeleton.1
  31.2 4.9 %all-to-all-start.1 = ((f32[4,128,256]{2,1,0:T(8,128)}), f32[4,128,256]{2,1,0:T(8,128)}, u32[]{:S(2)}, u32[]{:S(2)}) async-start(f32[4,128,256]{2,1,0:T(8,128)} %copy-done.17), calls=%async_computation.1 | async-start | bytes 1048576 | tf_op jit(solution)/shard_map/all_to_all | solution.py:511
  36.1 1.3 collective-permute-start.2
  37.3 15.3 %collective-permute-done.2.pts_ref = f32[64,1024]{1,0:T(8,128)S(1)} collective-permute-done((f32[64,1024]{1,0:T(8,128)}, f32[64,1024]{1,0:T(8,128)S(1)}, u32[]{:S(2)}, u32[]{:S(2)}) %collective-permute-start.2) | collective-permute-done | bytes 262176 | tf_op jit(solution)/shard_map/ppermute | solution.py:506
  52.6 1.3 collective-permute-start.4
  56.1 10.7 %near_own.1.refs_3_.refs_4_ = f32[8,256,512]{2,1,0:T(8,128)S(1)} custom-call(s32[4]{0:T(128)S(1)} %pad_add_fusion.pos_ref, f32[4,88,1024]{2,1,0:T(8,128)S(1)} %all-to-all-done.msgs.got_ref, bf16[8,256,512]{2,1,0:T(8,128)(2,1)S(1)} %get-tuple-element.29.t_ref, f32[8,8,512]{2,1,0:T(8,128)S(1)} %copy-done.13, f32[64,1024]{1,0:T(8,128)} %refs_0_.1, ...), custom_call_target="tpu_custom_call" | custom-call | tf_op jit(solution)/shard_map/near_own/pallas_call | solution.py:195
  66.8 1.9 %copy-done = f32[8,256,512]{2,1,0:T(8,128)} copy-done((f32[8,256,512]{2,1,0:T(8,128)}, f32[8,256,512]{2,1,0:T(8,128)S(1)}, u32[]{:S(2)}) %copy-start) | copy-done | bytes 4194328
  68.8 1.3 collective-permute-start.7
  72.2 8.2 %collective-permute-start.6 = (f32[4,128,256]{2,1,0:T(8,128)}, f32[4,128,256]{2,1,0:T(8,128)S(1)}, u32[]{:S(2)}, u32[]{:S(2)}) collective-permute-start(f32[4,128,256]{2,1,0:T(8,128)} %all-to-all-done.1.alike_ref), channel_id=1, source_target_pairs={{0,4},{4,0},{8,12},{12,8},{16,20},{20,16},{24,28},{28,24},{1,5},{5... | collective-permute-start | bytes 1572872 | tf_op jit(solution)/shard_map/ppermute | solution.py:521
  81.3 8.8 %near_pair.1.refs_4_.refs_5_ = f32[8,256,512]{2,1,0:T(8,128)S(1)} custom-call(s32[4]{0:T(128)S(1)} %pad_add_fusion.pos_ref, f32[4,88,1024]{2,1,0:T(8,128)S(1)} %all-to-all-done.msgs.got_ref, bf16[8,256,512]{2,1,0:T(8,128)(2,1)S(1)} %get-tuple-element.29.t_ref, f32[8,8,512]{2,1,0:T(8,128)S(1)} %copy-done.14, f32[64,1024]{1,0:T(8,128)} %collective-permute-done.1.refs_0_, ...), custom_call_target="tpu_custom_call" | custom-call | tf_op jit(solution)/shard_map/near_pair/pallas_call | solution.py:195
  90.2 4.6 %near_next_away.2 = (f32[128,1024]{1,0:T(8,128)S(1)}, f32[128,1024]{1,0:T(8,128)S(1)}) custom-call(s32[4]{0:T(128)S(1)} %pad_add_fusion.pos_ref, f32[4,88,1024]{2,1,0:T(8,128)S(1)} %all-to-all-done.msgs.got_ref, bf16[8,256,512]{2,1,0:T(8,128)(2,1)S(1)} %get-tuple-element.29.t_ref, f32[8,8,512]{2,1,0:T(8,128)S(1)} %copy-done.15, ...), custom_call_target="tpu_custom_call" | custom-call | tf_op jit(solution)/shard_map/near_next_away/pallas_call | solution.py:195
  94.8 4.7 %near_next_away.3 = (f32[128,1024]{1,0:T(8,128)S(1)}, f32[128,1024]{1,0:T(8,128)S(1)}) custom-call(s32[4]{0:T(128)S(1)} %pad_add_fusion.pos_ref, f32[4,88,1024]{2,1,0:T(8,128)S(1)} %all-to-all-done.msgs.got_ref, bf16[8,256,512]{2,1,0:T(8,128)(2,1)S(1)} %get-tuple-element.29.t_ref, f32[8,8,512]{2,1,0:T(8,128)S(1)} %copy-done.15, ...), custom_call_target="tpu_custom_call" | custom-call | tf_op jit(solution)/shard_map/near_next_away/pallas_call | solution.py:195
  99.7 1.9 %collective-permute-done.8.refs_1_ = f32[128,1024]{1,0:T(8,128)S(1)} collective-permute-done((f32[128,1024]{1,0:T(8,128)S(1)}, f32[128,1024]{1,0:T(8,128)S(1)}, u32[]{:S(2)}, u32[]{:S(2)}) %collective-permute-start.8) | collective-permute-done | bytes 524320 | tf_op jit(solution)/shard_map/ppermute | solution.py:489
  101.8 2.1 %collective-permute-start.12 = (f32[128,1024]{1,0:T(8,128)S(1)}, f32[128,1024]{1,0:T(8,128)S(1)}, u32[]{:S(2)}, u32[]{:S(2)}) collective-permute-start(f32[128,1024]{1,0:T(8,128)S(1)} %add_parts.4), channel_id=1, source_target_pairs={{2,0},{3,1},{0,2},{1,3},{6,4},{7,5},{4,6},{5,7},{10,8},{11,9},{8,1... | collective-permute-start | bytes 1572872 | tf_op jit(solution)/shard_map/ppermute | solution.py:492
  103.9 6.9 %far.1.refs_6_.refs_0_ = f32[64,256]{1,0:T(8,128)S(1)} custom-call(s32[4]{0:T(128)S(1)} %pad_add_fusion.pos_ref, s32[4,14]{1,0:T(4,128)S(1)} %bitcast.4, s32[6,1,256]{2,1,0:T(1,128)S(1)} %broadcast_in_dim.3.node_ref, f32[6,512,256]{2,1,0:T(8,128)S(1)} %copy-done.16, f32[4,128,256]{2,1,0:T(8,128)} %all-to-all-done.1.alike_ref, ...), custom_call_target="tpu_custom_call" | custom-call | tf_op jit(solution)/shard_map/far/pallas_call | solution.py:402
  110.8 5.7 %near_next_home.1 = (f32[128,1024]{1,0:T(8,128)S(1)}, f32[128,1024]{1,0:T(8,128)S(1)}, f32[128,1024]{1,0:T(8,128)S(1)}, f32[128,1024]{1,0:T(8,128)S(1)}) custom-call(s32[4]{0:T(128)S(1)} %pad_add_fusion.pos_ref, f32[4,88,1024]{2,1,0:T(8,128)S(1)} %all-to-all-done.msgs.got_ref, bf16[8,256,512]{2,1,0:T(8,128)(2,1)S(1)} %get-tuple-element.29.t_ref, ...), custom_call_target="tpu_custom_call" | custom-call | tf_op jit(solution)/shard_map/near_next_home/pallas_call | solution.py:195
  118.8 8.9 %collective-permute-done.12.refs_1_ = f32[128,1024]{1,0:T(8,128)S(1)} collective-permute-done((f32[128,1024]{1,0:T(8,128)S(1)}, f32[128,1024]{1,0:T(8,128)S(1)}, u32[]{:S(2)}, u32[]{:S(2)}) %collective-permute-start.12) | collective-permute-done | bytes 524320 | tf_op jit(solution)/shard_map/ppermute | solution.py:492
  127.8 1.9 %collective-permute-done.10.refs_2_ = f32[64,256]{1,0:T(8,128)S(1)} collective-permute-done((f32[64,256]{1,0:T(8,128)S(1)}, f32[64,256]{1,0:T(8,128)S(1)}, u32[]{:S(2)}, u32[]{:S(2)}) %collective-permute-start.10) | collective-permute-done | bytes 65568 | tf_op jit(solution)/shard_map/ppermute | solution.py:489
  129.7 2.1 %join.1 = f32[256,1024]{1,0:T(8,128)} custom-call(s32[4]{0:T(128)S(1)} %pad_add_fusion.pos_ref, f32[2,512,256]{2,1,0:T(8,128)S(1)} %copy-done.11, f32[64,256]{1,0:T(8,128)S(1)} %far.1.refs_6_.refs_0_, f32[64,256]{1,0:T(8,128)S(1)} %collective-permute-done.9.refs_1_, f32[64,256]{1,0:T(8,128)S(1)} %collective-permute-done.10.refs_2_, ...), custom_call_target="tpu_custom_call" | custom-call | tf_op jit(solution)/shard_map/join/pallas_call | solution.py:458
  (74 shorter events, 14.4 us)
Async XLA Ops:
  7.2 21.2 %copy-start.20 = (s32[1,256]{1,0:T(1,128)S(1)}, s32[1,256]{1,0:T(1,128)}, u32[]{:S(2)}) copy-start(s32[1,256]{1,0:T(1,128)} %index_ref.1) | copy-start | bytes 3076
  7.2 21.2 %all-to-all-start = ((f32[4,88,1024]{2,1,0:T(8,128)}), f32[4,88,1024]{2,1,0:T(8,128)S(1)}, u32[]{:S(2)}, u32[]{:S(2)}) async-start(f32[4,88,1024]{2,1,0:T(8,128)} %copy-done.5), calls=%async_computation | async-start | bytes 2883584 | tf_op jit(solution)/shard_map/all_to_all | solution.py:505
  11.4 24.6 %collective-permute-start.1 = (f32[64,1024]{1,0:T(8,128)}, f32[64,1024]{1,0:T(8,128)}, u32[]{:S(2)}, u32[]{:S(2)}) collective-permute-start(f32[64,1024]{1,0:T(8,128)} %refs_0_.1), channel_id=1, source_target_pairs={{0,4},{4,0},{8,12},{12,8},{16,20},{20,16},{24,28},{28,24},{1,5},{5... | collective-permute-start | bytes 786440 | tf_op jit(solution)/shard_map/ppermute | solution.py:502
  12.6 40.1 %collective-permute-start.3 = (f32[128,1024]{1,0:T(8,128)}, f32[128,1024]{1,0:T(8,128)}, u32[]{:S(2)}, u32[]{:S(2)}) collective-permute-start(f32[128,1024]{1,0:T(8,128)} %get-tuple-element.51), channel_id=1, source_target_pairs={{0,4},{4,0},{8,12},{12,8},{16,20},{20,16},{24,28},{28,24},{1,5},{5... | collective-permute-start | bytes 1572872 | tf_op jit(solution)/shard_map/ppermute | solution.py:503
  14.5 54.2 %collective-permute-start = (f32[128,1024]{1,0:T(8,128)}, f32[128,1024]{1,0:T(8,128)}, u32[]{:S(2)}, u32[]{:S(2)}) collective-permute-start(f32[128,1024]{1,0:T(8,128)} %get-tuple-element.52), channel_id=1, source_target_pairs={{0,4},{4,0},{8,12},{12,8},{16,20},{20,16},{24,28},{28,24},{1,5},{5... | collective-permute-start | bytes 1572872 | tf_op jit(solution)/shard_map/ppermute | solution.py:503
  31.2 41.1 %all-to-all-start.1 = ((f32[4,128,256]{2,1,0:T(8,128)}), f32[4,128,256]{2,1,0:T(8,128)}, u32[]{:S(2)}, u32[]{:S(2)}) async-start(f32[4,128,256]{2,1,0:T(8,128)} %copy-done.17), calls=%async_computation.1 | async-start | bytes 1048576 | tf_op jit(solution)/shard_map/all_to_all | solution.py:511
  36.1 16.6 %collective-permute-start.2 = (f32[64,1024]{1,0:T(8,128)}, f32[64,1024]{1,0:T(8,128)S(1)}, u32[]{:S(2)}, u32[]{:S(2)}) collective-permute-start(f32[64,1024]{1,0:T(8,128)} %collective-permute-done.1.refs_0_), channel_id=1, source_target_pairs={{0,8},{8,16},{16,24},{12,4},{20,12},{28,20},{1,9},{9,17},{17,25},{... | collective-permute-start | bytes 786440 | tf_op jit(solution)/shard_map/ppermute | solution.py:506
  52.6 37.5 %collective-permute-start.4 = (f32[128,1024]{1,0:T(8,128)}, f32[128,1024]{1,0:T(8,128)}, u32[]{:S(2)}, u32[]{:S(2)}) collective-permute-start(f32[128,1024]{1,0:T(8,128)} %collective-permute-done.3.refs_1_), channel_id=1, source_target_pairs={{0,8},{8,16},{16,24},{12,4},{20,12},{28,20},{1,9},{9,17},{17,25},{... | collective-permute-start | bytes 1572872 | tf_op jit(solution)/shard_map/ppermute | solution.py:513
  68.8 26.1 %collective-permute-start.7 = (f32[128,1024]{1,0:T(8,128)}, f32[128,1024]{1,0:T(8,128)}, u32[]{:S(2)}, u32[]{:S(2)}) collective-permute-start(f32[128,1024]{1,0:T(8,128)} %collective-permute-done.refs_2_), channel_id=1, source_target_pairs={{0,8},{8,16},{16,24},{12,4},{20,12},{28,20},{1,9},{9,17},{17,25},{... | collective-permute-start | bytes 1572872 | tf_op jit(solution)/shard_map/ppermute | solution.py:518
  72.2 17.9 %copy-start.1 = (f32[8,256,512]{2,1,0:T(8,128)S(1)}, f32[8,256,512]{2,1,0:T(8,128)}, u32[]{:S(2)}) copy-start(f32[8,256,512]{2,1,0:T(8,128)} %copy-done) | copy-start | bytes 12582916
  72.2 17.9 %copy-start.7 = (bf16[2,512,256]{2,1,0:T(8,128)(2,1)S(1)}, bf16[2,512,256]{2,1,0:T(8,128)(2,1)}, u32[]{:S(2)}) copy-start(bf16[2,512,256]{2,1,0:T(8,128)(2,1)} %copy-done.6) | copy-start | bytes 1572868
  72.2 17.9 %copy-start.9 = (f32[2,512,128]{2,1,0:T(8,128)S(1)}, f32[2,512,128]{2,1,0:T(8,128)}, u32[]{:S(2)}) copy-start(f32[2,512,128]{2,1,0:T(8,128)} %copy-done.8) | copy-start | bytes 1572868
  72.2 27.5 %collective-permute-start.6 = (f32[4,128,256]{2,1,0:T(8,128)}, f32[4,128,256]{2,1,0:T(8,128)S(1)}, u32[]{:S(2)}, u32[]{:S(2)}) collective-permute-start(f32[4,128,256]{2,1,0:T(8,128)} %all-to-all-done.1.alike_ref), channel_id=1, source_target_pairs={{0,4},{4,0},{8,12},{12,8},{16,20},{20,16},{24,28},{28,24},{1,5},{5... | collective-permute-start | bytes 1572872 | tf_op jit(solution)/shard_map/ppermute | solution.py:521
  94.7 5.0 %collective-permute-start.5 = (f32[128,1024]{1,0:T(8,128)S(1)}, f32[128,1024]{1,0:T(8,128)S(1)}, u32[]{:S(2)}, u32[]{:S(2)}) collective-permute-start(f32[128,1024]{1,0:T(8,128)S(1)} %get-tuple-element.39), channel_id=1, source_target_pairs={{1,0},{0,1},{3,2},{2,3},{5,4},{4,5},{7,6},{6,7},{9,8},{8,9},{11,10... | collective-permute-start | bytes 1572872 | tf_op jit(solution)/shard_map/ppermute | solution.py:489
  94.8 9.0 %copy-start.22 = (s32[6,256]{1,0:T(8,128)S(1)}, s32[6,256]{1,0:T(8,128)}, u32[]{:S(2)}) copy-start(s32[6,256]{1,0:T(8,128)} %param.16) | copy-start | bytes 18436
  99.6 2.0 %collective-permute-start.8 = (f32[128,1024]{1,0:T(8,128)S(1)}, f32[128,1024]{1,0:T(8,128)S(1)}, u32[]{:S(2)}, u32[]{:S(2)}) collective-permute-start(f32[128,1024]{1,0:T(8,128)S(1)} %get-tuple-element.43), channel_id=1, source_target_pairs={{1,0},{0,1},{3,2},{2,3},{5,4},{4,5},{7,6},{6,7},{9,8},{8,9},{11,10... | collective-permute-start | bytes 1572872 | tf_op jit(solution)/shard_map/ppermute | solution.py:489
  101.6 16.5 %collective-permute-start.13 = (f32[128,1024]{1,0:T(8,128)S(1)}, f32[128,1024]{1,0:T(8,128)S(1)}, u32[]{:S(2)}, u32[]{:S(2)}) collective-permute-start(f32[128,1024]{1,0:T(8,128)S(1)} %add_parts.3.refs_0_), channel_id=1, source_target_pairs={{2,0},{3,1},{0,2},{1,3},{6,4},{7,5},{4,6},{5,7},{10,8},{11,9},{8,1... | collective-permute-start | bytes 1572872 | tf_op jit(solution)/shard_map/ppermute | solution.py:492
  101.8 25.9 %collective-permute-start.12 = (f32[128,1024]{1,0:T(8,128)S(1)}, f32[128,1024]{1,0:T(8,128)S(1)}, u32[]{:S(2)}, u32[]{:S(2)}) collective-permute-start(f32[128,1024]{1,0:T(8,128)S(1)} %add_parts.4), channel_id=1, source_target_pairs={{2,0},{3,1},{0,2},{1,3},{6,4},{7,5},{4,6},{5,7},{10,8},{11,9},{8,1... | collective-permute-start | bytes 1572872 | tf_op jit(solution)/shard_map/ppermute | solution.py:492
  110.8 18.9 %copy-start.11 = (f32[2,512,256]{2,1,0:T(8,128)S(1)}, f32[2,512,256]{2,1,0:T(8,128)}, u32[]{:S(2)}) copy-start(f32[2,512,256]{2,1,0:T(8,128)} %interp_ref.1) | copy-start | bytes 3145732
  116.5 13.2 %collective-permute-start.14 = (f32[128,1024]{1,0:T(8,128)S(1)}, f32[128,1024]{1,0:T(8,128)S(1)}, u32[]{:S(2)}, u32[]{:S(2)}) collective-permute-start(f32[128,1024]{1,0:T(8,128)S(1)} %get-tuple-element.49), channel_id=1, source_target_pairs={{1,0},{0,1},{3,2},{2,3},{5,4},{4,5},{7,6},{6,7},{9,8},{8,9},{11,10... | collective-permute-start | bytes 1572872 | tf_op jit(solution)/shard_map/ppermute | solution.py:489
  116.6 13.1 %collective-permute-start.15 = (f32[128,1024]{1,0:T(8,128)S(1)}, f32[128,1024]{1,0:T(8,128)S(1)}, u32[]{:S(2)}, u32[]{:S(2)}) collective-permute-start(f32[128,1024]{1,0:T(8,128)S(1)} %get-tuple-element.50), channel_id=1, source_target_pairs={{1,0},{0,1},{3,2},{2,3},{5,4},{4,5},{7,6},{6,7},{9,8},{8,9},{11,10... | collective-permute-start | bytes 1572872 | tf_op jit(solution)/shard_map/ppermute | solution.py:489
  117.1 10.7 %collective-permute-start.11 = (f32[64,256]{1,0:T(8,128)S(1)}, f32[64,256]{1,0:T(8,128)S(1)}, u32[]{:S(2)}, u32[]{:S(2)}) collective-permute-start(f32[64,256]{1,0:T(8,128)S(1)} %far.1.refs_6_.refs_0_), channel_id=1, source_target_pairs={{3,0},{2,1},{1,2},{0,3},{7,4},{6,5},{5,6},{4,7},{11,8},{10,9},{9,1... | collective-permute-start | bytes 196616 | tf_op jit(solution)/shard_map/ppermute | solution.py:489
  118.1 11.6 %collective-permute-start.10 = (f32[64,256]{1,0:T(8,128)S(1)}, f32[64,256]{1,0:T(8,128)S(1)}, u32[]{:S(2)}, u32[]{:S(2)}) collective-permute-start(f32[64,256]{1,0:T(8,128)S(1)} %far.1.refs_6_.refs_0_), channel_id=1, source_target_pairs={{2,0},{3,1},{0,2},{1,3},{6,4},{7,5},{4,6},{5,7},{10,8},{11,9},{8,1... | collective-permute-start | bytes 196616 | tf_op jit(solution)/shard_map/ppermute | solution.py:489
  127.7 2.0 %collective-permute-start.9 = (f32[64,256]{1,0:T(8,128)S(1)}, f32[64,256]{1,0:T(8,128)S(1)}, u32[]{:S(2)}, u32[]{:S(2)}) collective-permute-start(f32[64,256]{1,0:T(8,128)S(1)} %far.1.refs_6_.refs_0_), channel_id=1, source_target_pairs={{1,0},{0,1},{3,2},{2,3},{5,4},{4,5},{7,6},{6,7},{9,8},{8,9},{11,10... | collective-permute-start | bytes 196616 | tf_op jit(solution)/shard_map/ppermute | solution.py:489
  (17 other events, 38.0 us)

commit v6 on v5

--- a/solution.py
+++ b/solution.py
@@ -20,7 +20,7 @@
 LOG2E = 1.0 / math.log(2.0)
 SCALE = math.sqrt(0.5 * LOG2E)
 BIAS = 0.0625 * F * LOG2E
-VMEM_LIMIT = 24 * 1024 * 1024
+VMEM_LIMIT = 64 * 1024 * 1024
 
 
 def dot(a, b):
@@ -58,58 +58,53 @@
     return jnp.concatenate([hi, hi, lo, lo], axis=1), off
 
 
-def near_body(
-    xs, sets, leaves_at, rows, row, nacc, nout, pos_ref, got_ref, t_ref, tb_ref, *refs
-):
+def near_body(xs, sets, blocks_at, rows, row, nacc, nout, pos_ref, *refs):
     nset = len(sets)
-    if nacc:
-        s_scr, sb_scr, w_scr, o_scr, k_scr, times_scr, list_ref, times_ref, sem = refs[-9:]
-        outs = refs[-9 - nout : -9]
-    else:
-        o_scr, s_scr, sb_scr, w_scr, k_scr, times_scr, list_ref, times_ref, sem = refs[-9:]
-    copy = pltpu.make_async_copy(got_ref.at[:, F : F + EXTRA, :128], times_ref, sem)
-    copy.start()
+    first, last = blocks_at
+    nblk = last - first
+    msgs, refs = refs[:nblk], refs[nblk:]
+    tp_scr, sp_scr, wf_scr, t_scr, tb_scr, s_scr, sb_scr, w_scr, k_scr = refs[-13:-4]
+    times_ref, times_scr, list_ref, sems = refs[-4:]
+    outs = refs[-13 - (2 if nacc else 0) - nout : -13 - (2 if nacc else 0)]
+    o_scr, acc_scr = refs[-15:-13] if nacc else (outs[0], None)
+    copies = []
+
+    def fetch(source, target):
+        copies.append(pltpu.make_async_copy(source, target, sems.at[len(copies)]))
+        copies[-1].start()
+        return copies[-1]
+
+    counts = [fetch(msgs[b].at[F : F + EXTRA, :128], times_ref.at[b]) for b in range(nblk)]
     at = 0
-    for k, (_, ready, chunks) in enumerate(sets):
-        heads = refs[at : at + 1 + ready]
-        parts = refs[at + 1 + ready : at + 1 + ready + chunks]
-        at += 1 + ready + chunks
+    heads, parts = [], []
+    for k, (_, chunks) in enumerate(sets):
         each = rows // chunks
-        for leaf in range(2):
-            cols = slice(leaf * LEAF, (leaf + 1) * LEAF)
-            j = 2 * k + leaf
-            if ready:
-                s_scr[j] = heads[0][leaf]
-                sb_scr[j] = heads[1][leaf]
-            else:
-                side, off = source_side(heads[0][:F, cols] * SCALE)
-                s_scr[j] = side
-                sb_scr[j] = jnp.broadcast_to(off, (LEAF, 128))
-            for c in range(chunks):
-                hi, lo = halves(parts[c][:, cols])
-                w_scr[j, c * each : (c + 1) * each, :] = hi
-                w_scr[j, rows + c * each : rows + (c + 1) * each, :] = lo
-    start, stop = leaves_at
-    for t in range(start, stop):
-        if nacc:
-            o_scr[t - start] = sum(ref[t, row : row + rows, :] for ref in refs[at : at + nacc])
-        else:
-            o_scr[t - start] = jnp.zeros((rows, LEAF), F32)
+        heads.append(fetch(refs[at], sp_scr.at[k]))
+        parts.append((refs[at + 1 : at + 1 + chunks], each))
+        at += 1 + chunks
+    targets = [fetch(msgs[b].at[:F, :], tp_scr.at[b]) for b in range(nblk)]
+    weights = [
+        [fetch(ref, wf_scr.at[k, c * each : (c + 1) * each, :]) for c, ref in enumerate(chunks)]
+        for k, (chunks, each) in enumerate(parts)
+    ]
+    accs = [
+        fetch(refs[at + n].at[2 * first : 2 * last, row : row + rows, :], acc_scr.at[n])
+        for n in range(nacc)
+    ]
 
     x, core, group, leaves = pos_ref[0], pos_ref[1], pos_ref[2], pos_ref[3]
     odd = group % 2
     column = []
-    for kind, _, _ in sets:
+    for kind, _ in sets:
         relative = {"own": 1, "pair": 2 - 2 * odd, "next": 2 * odd}[kind]
         column.append(relative * leaves + 2 * (2 * x + core))
-
-    copy.wait()
+    for copy in counts:
+        copy.wait()
     count = jnp.int32(0)
     list_ref[0] = 0
-    for t in range(start, stop):
+    for t in range(2 * nblk):
         for j in range(2 * nset):
-            helper = 2 * lax.rem(x + t // 4, xs) + (core if t // 2 % 2 == 0 else 1 - core)
-            times = times_ref[helper, t % 2, column[j // 2] + j % 2]
+            times = times_ref[t // 2, t % 2, column[j // 2] + j % 2]
 
             @pl.when(times > 0)
             def _(count=count, t=t, j=j, times=times):
@@ -118,11 +113,34 @@
 
             count = count + (times > 0).astype(jnp.int32)
 
+    for k in range(nset):
+        heads[k].wait()
+        for leaf in range(2):
+            cols = slice(leaf * LEAF, (leaf + 1) * LEAF)
+            side, off = source_side(sp_scr[k, :, cols] * SCALE)
+            s_scr[2 * k + leaf] = side
+            sb_scr[2 * k + leaf] = jnp.broadcast_to(off, (LEAF, 128))
+    for b in range(nblk):
+        targets[b].wait()
+        for leaf in range(2):
+            side, off = target_side(tp_scr[b, :, leaf * LEAF : (leaf + 1) * LEAF] * SCALE)
+            t_scr[2 * b + leaf] = side
+            tb_scr[2 * b + leaf] = jnp.broadcast_to(off, (8, LEAF))
+    for t in range(2 * nblk):
+        o_scr[t] = jnp.zeros((rows, LEAF), F32)
+    for k in range(nset):
+        for copy in weights[k]:
+            copy.wait()
+        for leaf in range(2):
+            hi, lo = halves(wf_scr[k, :, leaf * LEAF : (leaf + 1) * LEAF])
+            w_scr[2 * k + leaf, :rows, :] = hi
+            w_scr[2 * k + leaf, rows:, :] = lo
+
     def block(index, slot):
         code = list_ref[jnp.minimum(index, jnp.maximum(count - 1, 0))]
         t, j = code // 8, code % 8
-        side = t_ref[t]
-        off = tb_ref[t][:1, :]
+        side = t_scr[t]
+        off = tb_scr[t][:1, :]
         for half in range(2):
             part = slice(half * 256, (half + 1) * 256)
             cross = dot(s_scr[j, part, :], side)
@@ -134,7 +152,7 @@
 
     def apply(index, slot):
         code = list_ref[index]
-        t, j = code // 8 - start, code % 8
+        t, j = code // 8, code % 8
         factor = times_scr[index]
         for half in range(2):
             cols = slice(half * 256, (half + 1) * 256)
@@ -158,76 +176,65 @@
         return carry
 
     lax.fori_loop(0, (count + 1) // 2, pair, jnp.int32(0))
+    for copy in accs:
+        copy.wait()
     if nacc:
         tall = outs[0].shape[0]
         for n, ref in enumerate(outs):
             t, top = 2 * (n // (rows // tall)), n % (rows // tall) * tall
+            part = slice(top, top + tall)
             for leaf in range(2):
                 cols = slice(leaf * LEAF, (leaf + 1) * LEAF)
-                ref[:, cols] = o_scr[t + leaf, top : top + tall, :]
-
-
-def near_call(name, where, targets, leaves_at, sources, rows, row=0, acc=(), after=()):
+                total = o_scr[t + leaf, part, :]
+                for m in range(nacc):
+                    total = total + acc_scr[m, t + leaf, part, :]
+                ref[:, cols] = total
+
+
+def near_call(name, pos, msgs, blocks_at, sources, rows, row=0, acc=(), after=()):
     nset = len(sources)
-    start, stop = leaves_at
+    first, last = blocks_at
+    nblk = last - first
+    nt = 2 * nblk
     tall = R // 2
     vmem = pl.BlockSpec(memory_space=pltpu.VMEM)
     smem = pl.BlockSpec(memory_space=pltpu.SMEM)
-    operands = [a for _, heads, chunks in sources for a in (*heads, *chunks)]
+    operands = list(msgs[first:last])
+    operands += [a for _, points, chunks in sources for a in (points, *chunks)]
+    operands += list(acc)
     scratch = [
+        pltpu.VMEM((nblk, F, 2 * LEAF), F32),
+        pltpu.VMEM((nset, F, 2 * LEAF), F32),
+        pltpu.VMEM((nset, rows, 2 * LEAF), F32),
+        pltpu.VMEM((nt, 4 * F, LEAF), BF),
+        pltpu.VMEM((nt, 8, LEAF), F32),
         pltpu.VMEM((2 * nset, LEAF, 4 * F), BF),
         pltpu.VMEM((2 * nset, LEAF, 128), F32),
         pltpu.VMEM((2 * nset, 2 * rows, LEAF), BF),
-        pltpu.VMEM((stop - start, rows, LEAF), F32),
         pltpu.VMEM((2, 2 * LEAF, LEAF), BF),
-        pltpu.SMEM((2 * nset * (stop - start),), F32),
-        pltpu.SMEM((2 * nset * (stop - start),), jnp.int32),
-        pltpu.SMEM((where[1].shape[0], EXTRA, 128), F32),
-        pltpu.SemaphoreType.DMA,
+        pltpu.SMEM((nblk, EXTRA, 128), F32),
+        pltpu.SMEM((2 * nset * nt,), F32),
+        pltpu.SMEM((2 * nset * nt,), jnp.int32),
+        pltpu.SemaphoreType.DMA((2 * nblk + len(operands),)),
     ]
-    if not acc:
-        out = [jax.ShapeDtypeStruct((stop - start, rows, LEAF), F32)]
-        scratch.pop(3)
+    if acc:
+        out = [jax.ShapeDtypeStruct((tall, 2 * LEAF), F32)] * (nblk * (rows // tall))
+        scratch = [
+            pltpu.VMEM((nt, rows, LEAF), F32),
+            pltpu.VMEM((len(acc), nt, rows, LEAF), F32),
+        ] + scratch
     else:
-        operands += list(acc)
-        out = [jax.ShapeDtypeStruct((tall, 2 * LEAF), F32)] * ((stop - start) // 2 * (rows // tall))
-    sets = tuple((kind, len(heads) - 1, len(chunks)) for kind, heads, chunks in sources)
+        out = [jax.ShapeDtypeStruct((nt, rows, LEAF), F32)]
+    sets = tuple((kind, len(chunks)) for kind, _, chunks in sources)
     return pl.pallas_call(
-        partial(
-            near_body, targets[0].shape[0] // 4, sets, leaves_at, rows, row, len(acc), len(out)
-        ),
+        partial(near_body, len(msgs) // 2, sets, blocks_at, rows, row, len(acc), len(out)),
         name=name,
         out_shape=out,
-        in_specs=[smem, pl.BlockSpec(memory_space=pl.ANY)]
-        + [vmem] * (2 + len(operands))
-        + [pl.BlockSpec(memory_space=pl.ANY)] * len(after),
+        in_specs=[smem] + [pl.BlockSpec(memory_space=pl.ANY)] * (len(operands) + len(after)),
         out_specs=[vmem] * len(out),
         scratch_shapes=scratch,
         compiler_params=pltpu.CompilerParams(vmem_limit_bytes=VMEM_LIMIT),
-    )(*where, *targets, *operands, *after)
-
-
-def source_body(pts_ref, side_ref, off_ref):
-    for leaf in range(2):
-        cols = slice(leaf * LEAF, (leaf + 1) * LEAF)
-        side, off = source_side(pts_ref[:, cols] * SCALE)
-        side_ref[leaf] = side
-        off_ref[leaf] = jnp.broadcast_to(off, (LEAF, 128))
-
-
-def source_call(pts):
-    vmem = pl.BlockSpec(memory_space=pltpu.VMEM)
-    return pl.pallas_call(
-        source_body,
-        name="source_side",
-        out_shape=[
-            jax.ShapeDtypeStruct((2, LEAF, 4 * F), BF),
-            jax.ShapeDtypeStruct((2, LEAF, 128), F32),
-        ],
-        in_specs=[vmem],
-        out_specs=[vmem, vmem],
-        compiler_params=pltpu.CompilerParams(vmem_limit_bytes=VMEM_LIMIT),
-    )(pts)
+    )(pos, *operands, *after)
 
 
 def share_rows(xs):
@@ -235,7 +242,8 @@
 
 
 def leaf_body(xs, pos_ref, count_ref, src_ref, pts_in, w_in, interp_in, *refs):
-    msg, pts_ref, w_ref, interp_ref, scr, sems = refs
+    msgs = refs[: 2 * xs]
+    pts_ref, w_ref, interp_ref, scr, sems = refs[2 * xs :]
     copies = [
         pltpu.make_async_copy(pts_in, pts_ref, sems.at[0]),
         pltpu.make_async_copy(w_in, w_ref, sems.at[1]),
@@ -243,7 +251,7 @@
     ]
     for copy in copies:
         copy.start()
-    group, leaves = pos_ref[2], pos_ref[3]
+    x, core, group, leaves = pos_ref[0], pos_ref[1], pos_ref[2], pos_ref[3]
     lane = lax.broadcasted_iota(jnp.int32, (1, 128), 1) + (group - 1) * leaves
     times = []
     for leaf in range(2):
@@ -261,26 +269,27 @@
     scr[...] = total
     rows = R // (2 * xs)
     tall = share_rows(xs)
-    for helper in range(2 * xs):
-        msg[helper, :F, :] = pts_ref[...]
-        msg[helper, F : F + EXTRA, :] = jnp.zeros((EXTRA, 2 * LEAF), F32)
-        msg[helper, F : F + EXTRA, :128] = times
+    for n, msg in enumerate(msgs):
+        helper = 2 * lax.rem(x + n // 2, xs) + (core if n % 2 == 0 else 1 - core)
+        msg[:F, :] = pts_ref[...]
+        msg[F : F + EXTRA, :] = jnp.zeros((EXTRA, 2 * LEAF), F32)
+        msg[F : F + EXTRA, :128] = times
         for i in range(rows // tall):
-            at = helper * rows + i * tall
-            msg[helper, F + EXTRA :, i * SK : (i + 1) * SK] = scr[at : at + tall, :]
+            at = pl.multiple_of(helper * rows + i * tall, tall)
+            msg[F + EXTRA :, i * SK : (i + 1) * SK] = scr[pl.ds(at, tall), :]
 
 
 def leaf_call(xs, pos, near_count, near_src, points, weights, interp):
     vmem = pl.BlockSpec(memory_space=pltpu.VMEM)
     smem = pl.BlockSpec(memory_space=pltpu.SMEM)
-    hbm = pl.BlockSpec(memory_space=pltpu.HBM)
+    anywhere = pl.BlockSpec(memory_space=pl.ANY)
     height = F + EXTRA + share_rows(xs)
     return pl.pallas_call(
         partial(leaf_body, xs),
         name="leaf_up",
-        out_shape=jax.ShapeDtypeStruct((2 * xs, height, 2 * LEAF), F32),
-        in_specs=[smem, smem, smem, hbm, hbm, hbm],
-        out_specs=vmem,
+        out_shape=[jax.ShapeDtypeStruct((height, 2 * LEAF), F32)] * (2 * xs),
+        in_specs=[smem, smem, smem, anywhere, anywhere, anywhere],
+        out_specs=[vmem] * (2 * xs),
         scratch_shapes=[
             pltpu.VMEM(points.shape, F32),
             pltpu.VMEM(weights.shape, F32),
@@ -292,24 +301,20 @@
     )(pos, near_count, near_src, points, weights, interp)
 
 
-def skel_body(xs, pos_ref, index_ref, msgs, out_ref, side_ref, off_ref):
-    nblk = 2 * xs
-    rows = R // nblk
+def skel_body(xs, pos_ref, index_ref, *refs):
+    msgs, out_ref = refs[:-1], refs[-1]
+    rows = R // (2 * xs)
     tall = share_rows(xs)
     total = jnp.zeros((2 * F, SK), F32)
     value = jnp.zeros((tall, 2 * LEAF), F32)
     spot = lax.broadcasted_iota(jnp.int32, (2 * LEAF, SK), 0)
     x, core = pos_ref[0], pos_ref[1]
-    for b in range(nblk):
+    for b, msg in enumerate(msgs):
         helper = 2 * lax.rem(x + b // 2, xs) + (core if b % 2 == 0 else 1 - core)
-        side, off = target_side(msgs[helper, :F, :] * SCALE)
-        for leaf in range(2):
-            part = slice(leaf * LEAF, (leaf + 1) * LEAF)
-            side_ref[2 * b + leaf] = side[:, part]
-            off_ref[2 * b + leaf] = jnp.broadcast_to(off[:, part], (8, LEAF))
+        hi, lo = halves(msg[:F, :] * SCALE)
         hot = spot + helper * (2 * LEAF) == index_ref[...]
-        total = total + dot(side[: 2 * F], hot.astype(F32).astype(BF))
-        value = value + msgs[helper, F + EXTRA :, :]
+        total = total + dot(jnp.concatenate([hi, lo], axis=0), hot.astype(F32).astype(BF))
+        value = value + msg[F + EXTRA :, :]
     for n in range(out_ref.shape[0]):
         out_ref[n, :F, :] = total[:F] + total[F:]
         for i in range(rows // tall):
@@ -319,20 +324,15 @@
 
 def skel_call(xs, copies, pos, index, msgs):
     rows = R // (2 * xs)
-    nblk = 2 * xs
     vmem = pl.BlockSpec(memory_space=pltpu.VMEM)
     return pl.pallas_call(
         partial(skel_body, xs),
         name="skeleton",
-        out_shape=[
-            jax.ShapeDtypeStruct((copies, F + rows, SK), F32),
-            jax.ShapeDtypeStruct((2 * nblk, 4 * F, LEAF), BF),
-            jax.ShapeDtypeStruct((2 * nblk, 8, LEAF), F32),
-        ],
-        in_specs=[pl.BlockSpec(memory_space=pltpu.SMEM)] + [vmem] * 2,
-        out_specs=[vmem] * 3,
+        out_shape=jax.ShapeDtypeStruct((copies, F + rows, SK), F32),
+        in_specs=[pl.BlockSpec(memory_space=pltpu.SMEM)] + [vmem] * (1 + len(msgs)),
+        out_specs=vmem,
         compiler_params=pltpu.CompilerParams(vmem_limit_bytes=VMEM_LIMIT),
-    )(pos, index, msgs)
+    )(pos, index, *msgs)
 
 
 def upper_start(level, groups):
@@ -501,32 +501,33 @@
 
     pts_y = lax.ppermute(points, "leaf", beside)
     w_y = [lax.ppermute(weights[c * rows : (c + 1) * rows], "leaf", beside) for c in range(2)]
-    msgs = leaf_call(xs, pos, near_count, near_src, points, weights, interp)
-    got = lax.all_to_all(msgs, "help", 0, 0)
+    sent = leaf_call(xs, pos, near_count, near_src, points, weights, interp)
+    got = [
+        lax.ppermute(sent[n], "help", help_pairs(xs, -dx, dc))
+        for n, (dx, dc) in enumerate(order)
+        if n
+    ]
     pts_z = lax.ppermute(pts_y, "leaf", across)
-
-    payload, *targets = skel_call(xs, groups // 2, pos, skel_group, got)
-    where = (pos, got)
+    got, pts_z = together(got, pts_z)
+    msgs = [sent[0]] + [got[order.index((-dx % xs, dc)) - 1] for dx, dc in order[1:]]
+
+    payload = skel_call(xs, groups // 2, pos, skel_group, msgs)
     parity = [[n for n in range(groups) if n % 2 == odd] for odd in range(2)]
     alike = lax.all_to_all(payload, "leaf", 0, 0, axis_index_groups=parity)
-    pts_z, w_y[0] = together(pts_z, w_y[0])
     w_z = [lax.ppermute(w_y[0], "leaf", across)]
     (own,) = near_call(
-        "near_own", where, targets, (0, 2 * helpers), [("own", (points,), [weights])], R
+        "near_own", pos, msgs, (0, helpers), [("own", points, [weights])], R, after=[payload]
     )
     own, w_y[1] = together(own, w_y[1])
     w_z.append(lax.ppermute(w_y[1], "leaf", across))
-    z_side = source_call(pts_z)
     alike, w_y[1] = together(alike, w_y[1])
     side = lax.ppermute(alike, "leaf", beside)
-    (pair,) = near_call(
-        "near_pair", where, targets, (0, 2 * helpers), [("pair", (pts_y,), w_y)], R
-    )
+    (pair,) = near_call("near_pair", pos, msgs, (0, helpers), [("pair", pts_y, w_y)], R)
 
     sums, part = [], []
     for c in range(2):
         part = near_call(
-            "near_next_away", where, targets, (4, 2 * helpers), [("next", z_side, w_z[c : c + 1])],
+            "near_next_away", pos, msgs, (2, helpers), [("next", pts_z, w_z[c : c + 1])],
             rows, c * rows, (own, pair), part[:1],
         )
         kept, given = part[::2], part[1::2]
@@ -541,7 +542,7 @@
     v_own = far_call(groups, pos, far_nodes, skel_node, transfer, alike, side, both[:1])
     values = [v_own] + [from_help(v_own, dx, dc) for dx, dc in order[1:]]
     home = near_call(
-        "near_next_home", where, targets, (0, 4), [("next", z_side, w_z)], R, 0, (own, pair), [v_own]
+        "near_next_home", pos, msgs, (0, 2), [("next", pts_z, w_z)], R, 0, (own, pair), [v_own]
     )
     mate = [from_help(value, 0, 1) for value in home[2:]]
     mine = add_call(*[[home[c], *parts[c]] for c in range(2)])

time: 132 us -> 122 us (0.924)
  the two profiles are of different devices: /device:TPU:6 before, /device:TPU:0 now
where the time goes in v6:
time: 122 us; the launch traced here: 120 us
  Pallas kernels  60.5 us (50%)
  starting transfers between devices  30.1 us (25%)
  waiting for transfers between devices  24.9 us (20%)
  local copies, waits for them, and re-layouts  3.59 us (3%)
    pallas_call x5, Pallas kernels, near_call(): pl.pallas_call(partial(near_body, len(msgs) // 2, sets, blocks_at, rows,...  35.5 us
    ppermute x1, waiting for transfers between devices, shards(): side = lax.ppermute(alike, 'leaf', beside)  10.3 us
    pallas_call x1, Pallas kernels, far_call(): pl.pallas_call(partial(far_body, groups, rows), name='far', out_shape=jax...  8.05 us
    ppermute x3, waiting for transfers between devices, shards(): lax.ppermute(sent[n], 'help', help_pairs(xs, -dx, dc))  7.79 us
    pallas_call x3, Pallas kernels, add_call(): pl.pallas_call(partial(add_body, len(sums[0])), name='add_parts', out_sha...  6.66 us
    ppermute x2, waiting for transfers between devices, to_help(): return lax.ppermute(value, 'help', help_pairs(xs, -dx, 0))  4.94 us
    all_to_all x1, starting transfers between devices, shards(): alike = lax.all_to_all(payload, 'leaf', 0, 0, axis_index_groups=parity)  4.87 us
    ppermute x1, starting transfers between devices, shards(): w_z = [lax.ppermute(w_y[0], 'leaf', across)]  4.72 us
  transfers between devices with their start and end apart: 20, of which 5 were waited for; matrix products, arithmetic and copies ran while one was open for 3% of the time, Pallas kernels for 48%

profile of v6, /device:TPU:0, one launch (start us, length us, event | category | flops | bytes accessed | tf_op | source)
XLA Modules:
  0.0 119.8 jit_solution(10660061755970059768)
XLA Ops:
  0.0 3.0 %collective-permute-start.3 = (f32[64,1024]{1,0:T(8,128)}, f32[64,1024]{1,0:T(8,128)}, u32[]{:S(2)}, u32[]{:S(2)}) collective-permute-start(f32[64,1024]{1,0:T(8,128)} %refs_4_.1), channel_id=1, source_target_pairs={{0,4},{4,0},{8,12},{12,8},{16,20},{20,16},{24,28},{28,24},{1,5},{5... | collective-permute-start | bytes 786440 | tf_op jit(solution)/shard_map/ppermute | solution.py:502
  3.6 4.0 %leaf_up.1 = (f32[88,1024]{1,0:T(8,128)}, f32[88,1024]{1,0:T(8,128)}, f32[88,1024]{1,0:T(8,128)}, f32[88,1024]{1,0:T(8,128)}) custom-call(s32[4]{0:T(128)} %pad_add_fusion.pos_ref, s32[1,2]{1,0:T(1,128)} %count_ref.1, s32[2,32]{1,0:T(2,128)} %src_ref.1, f32[64,1024]{1,0:T(8,128)} %refs_4_.1, f32[256,1024]{1,0:T(8,128)} %refs_5_.1, f32[2,512,256]{2,1,0:T(8,128)} %interp_ref.1), custom_call_target="tpu_custom_call" | custom-call | tf_op jit(solution)/shard_map/leaf_up/pallas_call | solution.py:287
  9.6 4.4 %collective-permute-start.4 = (f32[64,1024]{1,0:T(8,128)}, f32[64,1024]{1,0:T(8,128)}, u32[]{:S(2)}, u32[]{:S(2)}) collective-permute-start(f32[64,1024]{1,0:T(8,128)} %collective-permute-done.3.refs_4_), channel_id=1, source_target_pairs={{0,8},{8,16},{16,24},{12,4},{20,12},{28,20},{1,9},{9,17},{17,25},{... | collective-permute-start | bytes 786440 | tf_op jit(solution)/shard_map/ppermute | solution.py:510
  14.0 2.3 %fusion = (f32[128,1024]{1,0:T(8,128)}, f32[128,1024]{1,0:T(8,128)}) fusion(f32[256,1024]{1,0:T(8,128)} %refs_5_.1), kind=kLoop, calls=%fused_computation.1 | loop fusion | bytes 2097152 | tf_op jit(solution)/shard_map/slice | solution.py:503
  16.3 2.0 %collective-permute-start.5 = (f32[128,1024]{1,0:T(8,128)}, f32[128,1024]{1,0:T(8,128)}, u32[]{:S(2)}, u32[]{:S(2)}) collective-permute-start(f32[128,1024]{1,0:T(8,128)} %get-tuple-element.54), channel_id=1, source_target_pairs={{0,4},{4,0},{8,12},{12,8},{16,20},{20,16},{24,28},{28,24},{1,5},{5... | collective-permute-start | bytes 1572872 | tf_op jit(solution)/shard_map/ppermute | solution.py:503
  19.3 6.8 %collective-permute-done.2.refs_3_.refs_1_ = f32[88,1024]{1,0:T(8,128)} collective-permute-done((f32[88,1024]{1,0:T(8,128)}, f32[88,1024]{1,0:T(8,128)}, u32[]{:S(2)}, u32[]{:S(2)}) %collective-permute-start.2) | collective-permute-done | bytes 360480 | tf_op jit(solution)/shard_map/ppermute | solution.py:506
  26.1 2.7 %skeleton.1.refs_6_ = f32[4,128,256]{2,1,0:T(8,128)} custom-call(s32[4]{0:T(128)} %pad_add_fusion.pos_ref, s32[1,256]{1,0:T(1,128)} %index_ref.1, f32[88,1024]{1,0:T(8,128)} %get-tuple-element.29.refs_0_, f32[88,1024]{1,0:T(8,128)} %collective-permute-done.refs_1_, f32[88,1024]{1,0:T(8,128)} %collective-permute-done.1.refs_2_.refs_0_, ...), custom_call_target="tpu_custom_call" | custom-call | tf_op jit(solution)/shard_map/skeleton/pallas_call | solution.py:328
  28.8 4.9 %all-to-all-start = ((f32[4,128,256]{2,1,0:T(8,128)}), f32[4,128,256]{2,1,0:T(8,128)}, u32[]{:S(2)}, u32[]{:S(2)}) async-start(f32[4,128,256]{2,1,0:T(8,128)} %skeleton.1.refs_6_), calls=%async_computation | async-start | bytes 1048576 | tf_op jit(solution)/shard_map/all_to_all | solution.py:516
  33.7 4.7 %collective-permute-start.7 = (f32[128,1024]{1,0:T(8,128)}, f32[128,1024]{1,0:T(8,128)}, u32[]{:S(2)}, u32[]{:S(2)}) collective-permute-start(f32[128,1024]{1,0:T(8,128)} %collective-permute-done.6.refs_5_), channel_id=1, source_target_pairs={{0,8},{8,16},{16,24},{12,4},{20,12},{28,20},{1,9},{9,17},{17,25},{... | collective-permute-start | bytes 1572872 | tf_op jit(solution)/shard_map/ppermute | solution.py:517
  38.4 13.8 %near_own.1.refs_4_.refs_5_ = f32[8,256,512]{2,1,0:T(8,128)} custom-call(s32[4]{0:T(128)} %pad_add_fusion.pos_ref, f32[88,1024]{1,0:T(8,128)} %get-tuple-element.29.refs_0_, f32[88,1024]{1,0:T(8,128)} %collective-permute-done.refs_1_, f32[88,1024]{1,0:T(8,128)} %collective-permute-done.1.refs_2_.refs_0_, f32[88,1024]{1,0:T(8,128)} %collective-permute-done.2.refs_3_.refs_1_, ...), custom_call_target="tpu_custom_call" | custom-call | tf_op jit(solution)/shard_map/near_own/pallas_call | solution.py:229
  52.2 2.1 %collective-permute-start.10 = (f32[128,1024]{1,0:T(8,128)}, f32[128,1024]{1,0:T(8,128)}, u32[]{:S(2)}, u32[]{:S(2)}) collective-permute-start(f32[128,1024]{1,0:T(8,128)} %collective-permute-done.5.refs_6_), channel_id=1, source_target_pairs={{0,8},{8,16},{16,24},{12,4},{20,12},{28,20},{1,9},{9,17},{17,25},{... | collective-permute-start | bytes 1572872 | tf_op jit(solution)/shard_map/ppermute | solution.py:522
  54.3 9.3 %near_pair.1.refs_5_.refs_6_ = f32[8,256,512]{2,1,0:T(8,128)} custom-call(s32[4]{0:T(128)} %pad_add_fusion.pos_ref, f32[88,1024]{1,0:T(8,128)} %get-tuple-element.29.refs_0_, f32[88,1024]{1,0:T(8,128)} %collective-permute-done.refs_1_, f32[88,1024]{1,0:T(8,128)} %collective-permute-done.1.refs_2_.refs_0_, f32[88,1024]{1,0:T(8,128)} %collective-permute-done.2.refs_3_.refs_1_, ...), custom_call_target="tpu_custom_call" | custom-call | tf_op jit(solution)/shard_map/near_pair/pallas_call | solution.py:229
  63.6 3.8 %near_next_away.2 = (f32[128,1024]{1,0:T(8,128)}, f32[128,1024]{1,0:T(8,128)}) custom-call(s32[4]{0:T(128)} %pad_add_fusion.pos_ref, f32[88,1024]{1,0:T(8,128)} %collective-permute-done.1.refs_2_.refs_0_, f32[88,1024]{1,0:T(8,128)} %collective-permute-done.2.refs_3_.refs_1_, f32[64,1024]{1,0:T(8,128)} %collective-permute-done.4.refs_2_, ...), custom_call_target="tpu_custom_call" | custom-call | tf_op jit(solution)/shard_map/near_next_away/pallas_call | solution.py:229
  68.6 3.8 %near_next_away.3 = (f32[128,1024]{1,0:T(8,128)}, f32[128,1024]{1,0:T(8,128)}) custom-call(s32[4]{0:T(128)} %pad_add_fusion.pos_ref, f32[88,1024]{1,0:T(8,128)} %collective-permute-done.1.refs_2_.refs_0_, f32[88,1024]{1,0:T(8,128)} %collective-permute-done.2.refs_3_.refs_1_, f32[64,1024]{1,0:T(8,128)} %collective-permute-done.4.refs_2_, ...), custom_call_target="tpu_custom_call" | custom-call | tf_op jit(solution)/shard_map/near_next_away/pallas_call | solution.py:229
  72.6 10.3 %collective-permute-done.9.beside_ref = f32[4,128,256]{2,1,0:T(8,128)} collective-permute-done((f32[4,128,256]{2,1,0:T(8,128)}, f32[4,128,256]{2,1,0:T(8,128)}, u32[]{:S(2)}, u32[]{:S(2)}) %collective-permute-start.9) | collective-permute-done | bytes 524320 | tf_op jit(solution)/shard_map/ppermute | solution.py:524
  82.9 2.0 %add_parts.4 = f32[128,1024]{1,0:T(8,128)} custom-call(f32[128,1024]{1,0:T(8,128)} %get-tuple-element.43.refs_6_.refs_0_, f32[128,1024]{1,0:T(8,128)} %collective-permute-done.8.refs_1_), custom_call_target="tpu_custom_call" | custom-call | tf_op jit(solution)/shard_map/add_parts/pallas_call | solution.py:446
  84.9 3.0 %collective-permute-start.15 = (f32[128,1024]{1,0:T(8,128)}, f32[128,1024]{1,0:T(8,128)}, u32[]{:S(2)}, u32[]{:S(2)}) collective-permute-start(f32[128,1024]{1,0:T(8,128)} %add_parts.4), channel_id=1, source_target_pairs={{2,0},{3,1},{0,2},{1,3},{6,4},{7,5},{4,6},{5,7},{10,8},{11,9},{8,1... | collective-permute-start | bytes 1572872 | tf_op jit(solution)/shard_map/ppermute | solution.py:492
  87.9 2.0 %add_parts.3.refs_0_ = f32[128,1024]{1,0:T(8,128)} custom-call(f32[128,1024]{1,0:T(8,128)} %get-tuple-element.44.refs_0_, f32[128,1024]{1,0:T(8,128)} %collective-permute-done.11.refs_1_), custom_call_target="tpu_custom_call" | custom-call | tf_op jit(solution)/shard_map/add_parts/pallas_call | solution.py:446
  91.2 8.0 %far.1.refs_7_.refs_0_ = f32[64,256]{1,0:T(8,128)} custom-call(s32[4]{0:T(128)} %pad_add_fusion.pos_ref, s32[4,14]{1,0:T(4,128)} %bitcast.4, s32[6,1,256]{2,1,0:T(1,128)} %broadcast_in_dim.3.node_ref, f32[6,512,256]{2,1,0:T(8,128)} %transfer_ref.1, f32[4,128,256]{2,1,0:T(8,128)} %all-to-all-done.alike_ref, f32[4,128,256]{2,1,0:T(8,128)} %collective-permute-done.9.beside_ref, ...), custom_call_target="tpu_custom_call" | custom-call | tf_op jit(solution)/shard_map/far/pallas_call | solution.py:402
  99.3 5.0 %near_next_home.1 = (f32[128,1024]{1,0:T(8,128)}, f32[128,1024]{1,0:T(8,128)}, f32[128,1024]{1,0:T(8,128)}, f32[128,1024]{1,0:T(8,128)}) custom-call(s32[4]{0:T(128)} %pad_add_fusion.pos_ref, f32[88,1024]{1,0:T(8,128)} %get-tuple-element.29.refs_0_, f32[88,1024]{1,0:T(8,128)} %collective-permute-done.refs_1_, f32[64,1024]{1,0:T(8,128)} %collective-permute-done.4.refs_2_, ...), custom_call_target="tpu_custom_call" | custom-call | tf_op jit(solution)/shard_map/near_next_home/pallas_call | solution.py:229
  104.9 2.0 %collective-permute-start.13 = (f32[64,256]{1,0:T(8,128)}, f32[64,256]{1,0:T(8,128)}, u32[]{:S(2)}, u32[]{:S(2)}) collective-permute-start(f32[64,256]{1,0:T(8,128)} %far.1.refs_7_.refs_0_), channel_id=1, source_target_pairs={{2,0},{3,1},{0,2},{1,3},{6,4},{7,5},{4,6},{5,7},{10,8},{11,9},{8,1... | collective-permute-start | bytes 196616 | tf_op jit(solution)/shard_map/ppermute | solution.py:489
  106.9 4.9 %collective-permute-done.16.refs_3_ = f32[128,1024]{1,0:T(8,128)} collective-permute-done((f32[128,1024]{1,0:T(8,128)}, f32[128,1024]{1,0:T(8,128)}, u32[]{:S(2)}, u32[]{:S(2)}) %collective-permute-start.16) | collective-permute-done | bytes 524320 | tf_op jit(solution)/shard_map/ppermute | solution.py:492
  111.9 2.6 %add_parts.5 = (f32[128,1024]{1,0:T(8,128)}, f32[128,1024]{1,0:T(8,128)}) custom-call(f32[128,1024]{1,0:T(8,128)} %get-tuple-element.46.refs_0_, f32[128,1024]{1,0:T(8,128)} %collective-permute-done.15.refs_1_, f32[128,1024]{1,0:T(8,128)} %get-tuple-element.48.refs_2_, f32[128,1024]{1,0:T(8,128)} %collective-permute-done.16.refs_3_), custom_call_target="tpu_custom_call" | custom-call | tf_op jit(solution)/shard_map/add_parts/pallas_call | solution.py:446
  116.3 3.6 %join.1 = f32[256,1024]{1,0:T(8,128)} custom-call(s32[4]{0:T(128)} %pad_add_fusion.pos_ref, f32[2,512,256]{2,1,0:T(8,128)} %interp_ref.1, f32[64,256]{1,0:T(8,128)} %far.1.refs_7_.refs_0_, f32[64,256]{1,0:T(8,128)} %collective-permute-done.12.refs_1_, f32[64,256]{1,0:T(8,128)} %collective-permute-done.13.refs_2_, f32[64,256]{1,0:T(8,128)} %collective-permute-done.14.refs_3_, ...), custom_call_target="tpu_custom_call" | custom-call | tf_op jit(solution)/shard_map/join/pallas_call | solution.py:458
  (31 shorter events, 8.8 us)
Async XLA Ops:
  0.0 9.6 %collective-permute-start.3 = (f32[64,1024]{1,0:T(8,128)}, f32[64,1024]{1,0:T(8,128)}, u32[]{:S(2)}, u32[]{:S(2)}) collective-permute-start(f32[64,1024]{1,0:T(8,128)} %refs_4_.1), channel_id=1, source_target_pairs={{0,4},{4,0},{8,12},{12,8},{16,20},{20,16},{24,28},{28,24},{1,5},{5... | collective-permute-start | bytes 786440 | tf_op jit(solution)/shard_map/ppermute | solution.py:502
  7.6 8.7 %collective-permute-start = (f32[88,1024]{1,0:T(8,128)}, f32[88,1024]{1,0:T(8,128)}, u32[]{:S(2)}, u32[]{:S(2)}) collective-permute-start(f32[88,1024]{1,0:T(8,128)} %get-tuple-element.30), channel_id=1, source_target_pairs={{1,0},{0,1},{3,2},{2,3},{5,4},{4,5},{7,6},{6,7},{9,8},{8,9},{11,10... | collective-permute-start | bytes 1081352 | tf_op jit(solution)/shard_map/ppermute | solution.py:506
  7.7 11.6 %collective-permute-start.1 = (f32[88,1024]{1,0:T(8,128)}, f32[88,1024]{1,0:T(8,128)}, u32[]{:S(2)}, u32[]{:S(2)}) collective-permute-start(f32[88,1024]{1,0:T(8,128)} %get-tuple-element.31), channel_id=1, source_target_pairs={{2,0},{3,1},{0,2},{1,3},{6,4},{7,5},{4,6},{5,7},{10,8},{11,9},{8,1... | collective-permute-start | bytes 1081352 | tf_op jit(solution)/shard_map/ppermute | solution.py:506
  9.3 16.9 %collective-permute-start.2 = (f32[88,1024]{1,0:T(8,128)}, f32[88,1024]{1,0:T(8,128)}, u32[]{:S(2)}, u32[]{:S(2)}) collective-permute-start(f32[88,1024]{1,0:T(8,128)} %get-tuple-element.32), channel_id=1, source_target_pairs={{3,0},{2,1},{1,2},{0,3},{7,4},{6,5},{5,6},{4,7},{11,8},{10,9},{9,1... | collective-permute-start | bytes 1081352 | tf_op jit(solution)/shard_map/ppermute | solution.py:506
  9.6 16.5 %collective-permute-start.4 = (f32[64,1024]{1,0:T(8,128)}, f32[64,1024]{1,0:T(8,128)}, u32[]{:S(2)}, u32[]{:S(2)}) collective-permute-start(f32[64,1024]{1,0:T(8,128)} %collective-permute-done.3.refs_4_), channel_id=1, source_target_pairs={{0,8},{8,16},{16,24},{12,4},{20,12},{28,20},{1,9},{9,17},{17,25},{... | collective-permute-start | bytes 786440 | tf_op jit(solution)/shard_map/ppermute | solution.py:510
  16.3 17.4 %collective-permute-start.6 = (f32[128,1024]{1,0:T(8,128)}, f32[128,1024]{1,0:T(8,128)}, u32[]{:S(2)}, u32[]{:S(2)}) collective-permute-start(f32[128,1024]{1,0:T(8,128)} %get-tuple-element.53), channel_id=1, source_target_pairs={{0,4},{4,0},{8,12},{12,8},{16,20},{20,16},{24,28},{28,24},{1,5},{5... | collective-permute-start | bytes 1572872 | tf_op jit(solution)/shard_map/ppermute | solution.py:503
  16.3 35.9 %collective-permute-start.5 = (f32[128,1024]{1,0:T(8,128)}, f32[128,1024]{1,0:T(8,128)}, u32[]{:S(2)}, u32[]{:S(2)}) collective-permute-start(f32[128,1024]{1,0:T(8,128)} %get-tuple-element.54), channel_id=1, source_target_pairs={{0,4},{4,0},{8,12},{12,8},{16,20},{20,16},{24,28},{28,24},{1,5},{5... | collective-permute-start | bytes 1572872 | tf_op jit(solution)/shard_map/ppermute | solution.py:503
  28.8 25.5 %all-to-all-start = ((f32[4,128,256]{2,1,0:T(8,128)}), f32[4,128,256]{2,1,0:T(8,128)}, u32[]{:S(2)}, u32[]{:S(2)}) async-start(f32[4,128,256]{2,1,0:T(8,128)} %skeleton.1.refs_6_), calls=%async_computation | async-start | bytes 1048576 | tf_op jit(solution)/shard_map/all_to_all | solution.py:516
  33.7 29.9 %collective-permute-start.7 = (f32[128,1024]{1,0:T(8,128)}, f32[128,1024]{1,0:T(8,128)}, u32[]{:S(2)}, u32[]{:S(2)}) collective-permute-start(f32[128,1024]{1,0:T(8,128)} %collective-permute-done.6.refs_5_), channel_id=1, source_target_pairs={{0,8},{8,16},{16,24},{12,4},{20,12},{28,20},{1,9},{9,17},{17,25},{... | collective-permute-start | bytes 1572872 | tf_op jit(solution)/shard_map/ppermute | solution.py:517
  52.2 16.5 %collective-permute-start.10 = (f32[128,1024]{1,0:T(8,128)}, f32[128,1024]{1,0:T(8,128)}, u32[]{:S(2)}, u32[]{:S(2)}) collective-permute-start(f32[128,1024]{1,0:T(8,128)} %collective-permute-done.5.refs_6_), channel_id=1, source_target_pairs={{0,8},{8,16},{16,24},{12,4},{20,12},{28,20},{1,9},{9,17},{17,25},{... | collective-permute-start | bytes 1572872 | tf_op jit(solution)/shard_map/ppermute | solution.py:522
  67.3 5.3 %collective-permute-start.8 = (f32[128,1024]{1,0:T(8,128)}, f32[128,1024]{1,0:T(8,128)}, u32[]{:S(2)}, u32[]{:S(2)}) collective-permute-start(f32[128,1024]{1,0:T(8,128)} %get-tuple-element.41), channel_id=1, source_target_pairs={{1,0},{0,1},{3,2},{2,3},{5,4},{4,5},{7,6},{6,7},{9,8},{8,9},{11,10... | collective-permute-start | bytes 1572872 | tf_op jit(solution)/shard_map/ppermute | solution.py:489
  68.6 14.2 %collective-permute-start.9 = (f32[4,128,256]{2,1,0:T(8,128)}, f32[4,128,256]{2,1,0:T(8,128)}, u32[]{:S(2)}, u32[]{:S(2)}) collective-permute-start(f32[4,128,256]{2,1,0:T(8,128)} %all-to-all-done.alike_ref), channel_id=1, source_target_pairs={{0,4},{4,0},{8,12},{12,8},{16,20},{20,16},{24,28},{28,24},{1,5},{5... | collective-permute-start | bytes 1572872 | tf_op jit(solution)/shard_map/ppermute | solution.py:524
  72.4 15.4 %collective-permute-start.11 = (f32[128,1024]{1,0:T(8,128)}, f32[128,1024]{1,0:T(8,128)}, u32[]{:S(2)}, u32[]{:S(2)}) collective-permute-start(f32[128,1024]{1,0:T(8,128)} %get-tuple-element.45), channel_id=1, source_target_pairs={{1,0},{0,1},{3,2},{2,3},{5,4},{4,5},{7,6},{6,7},{9,8},{8,9},{11,10... | collective-permute-start | bytes 1572872 | tf_op jit(solution)/shard_map/ppermute | solution.py:489
  84.9 20.0 %collective-permute-start.15 = (f32[128,1024]{1,0:T(8,128)}, f32[128,1024]{1,0:T(8,128)}, u32[]{:S(2)}, u32[]{:S(2)}) collective-permute-start(f32[128,1024]{1,0:T(8,128)} %add_parts.4), channel_id=1, source_target_pairs={{2,0},{3,1},{0,2},{1,3},{6,4},{7,5},{4,6},{5,7},{10,8},{11,9},{8,1... | collective-permute-start | bytes 1572872 | tf_op jit(solution)/shard_map/ppermute | solution.py:492
  89.9 21.9 %collective-permute-start.16 = (f32[128,1024]{1,0:T(8,128)}, f32[128,1024]{1,0:T(8,128)}, u32[]{:S(2)}, u32[]{:S(2)}) collective-permute-start(f32[128,1024]{1,0:T(8,128)} %add_parts.3.refs_0_), channel_id=1, source_target_pairs={{2,0},{3,1},{0,2},{1,3},{6,4},{7,5},{4,6},{5,7},{10,8},{11,9},{8,1... | collective-permute-start | bytes 1572872 | tf_op jit(solution)/shard_map/ppermute | solution.py:492
  104.2 12.0 %collective-permute-start.17 = (f32[128,1024]{1,0:T(8,128)}, f32[128,1024]{1,0:T(8,128)}, u32[]{:S(2)}, u32[]{:S(2)}) collective-permute-start(f32[128,1024]{1,0:T(8,128)} %get-tuple-element.51), channel_id=1, source_target_pairs={{1,0},{0,1},{3,2},{2,3},{5,4},{4,5},{7,6},{6,7},{9,8},{8,9},{11,10... | collective-permute-start | bytes 1572872 | tf_op jit(solution)/shard_map/ppermute | solution.py:489
  104.3 12.0 %collective-permute-start.18 = (f32[128,1024]{1,0:T(8,128)}, f32[128,1024]{1,0:T(8,128)}, u32[]{:S(2)}, u32[]{:S(2)}) collective-permute-start(f32[128,1024]{1,0:T(8,128)} %get-tuple-element.52), channel_id=1, source_target_pairs={{1,0},{0,1},{3,2},{2,3},{5,4},{4,5},{7,6},{6,7},{9,8},{8,9},{11,10... | collective-permute-start | bytes 1572872 | tf_op jit(solution)/shard_map/ppermute | solution.py:489
  104.8 9.6 %collective-permute-start.12 = (f32[64,256]{1,0:T(8,128)}, f32[64,256]{1,0:T(8,128)}, u32[]{:S(2)}, u32[]{:S(2)}) collective-permute-start(f32[64,256]{1,0:T(8,128)} %far.1.refs_7_.refs_0_), channel_id=1, source_target_pairs={{1,0},{0,1},{3,2},{2,3},{5,4},{4,5},{7,6},{6,7},{9,8},{8,9},{11,10... | collective-permute-start | bytes 196616 | tf_op jit(solution)/shard_map/ppermute | solution.py:489
  104.9 9.5 %collective-permute-start.13 = (f32[64,256]{1,0:T(8,128)}, f32[64,256]{1,0:T(8,128)}, u32[]{:S(2)}, u32[]{:S(2)}) collective-permute-start(f32[64,256]{1,0:T(8,128)} %far.1.refs_7_.refs_0_), channel_id=1, source_target_pairs={{2,0},{3,1},{0,2},{1,3},{6,4},{7,5},{4,6},{5,7},{10,8},{11,9},{8,1... | collective-permute-start | bytes 196616 | tf_op jit(solution)/shard_map/ppermute | solution.py:489
  111.9 4.4 %collective-permute-start.14 = (f32[64,256]{1,0:T(8,128)}, f32[64,256]{1,0:T(8,128)}, u32[]{:S(2)}, u32[]{:S(2)}) collective-permute-start(f32[64,256]{1,0:T(8,128)} %far.1.refs_7_.refs_0_), channel_id=1, source_target_pairs={{3,0},{2,1},{1,2},{0,3},{7,4},{6,5},{5,6},{4,7},{11,8},{10,9},{9,1... | collective-permute-start | bytes 196616 | tf_op jit(solution)/shard_map/ppermute | solution.py:489

commit v7 on v5

--- a/solution.py
+++ b/solution.py
@@ -59,16 +59,22 @@
 
 
 def near_body(
-    xs, sets, leaves_at, rows, row, nacc, nout, pos_ref, got_ref, t_ref, tb_ref, *refs
+    xs, sets, leaves_at, rows, row, nacc, nout, pos_ref, *refs
 ):
     nset = len(sets)
+    start, stop = leaves_at
+    msgs, (t_ref, tb_ref), refs = refs[: 2 * xs], refs[2 * xs : 2 * xs + 2], refs[2 * xs + 2 :]
     if nacc:
-        s_scr, sb_scr, w_scr, o_scr, k_scr, times_scr, list_ref, times_ref, sem = refs[-9:]
+        s_scr, sb_scr, w_scr, o_scr, k_scr, times_scr, list_ref, times_ref, sems = refs[-9:]
         outs = refs[-9 - nout : -9]
     else:
-        o_scr, s_scr, sb_scr, w_scr, k_scr, times_scr, list_ref, times_ref, sem = refs[-9:]
-    copy = pltpu.make_async_copy(got_ref.at[:, F : F + EXTRA, :128], times_ref, sem)
-    copy.start()
+        o_scr, s_scr, sb_scr, w_scr, k_scr, times_scr, list_ref, times_ref, sems = refs[-9:]
+    copies = [
+        pltpu.make_async_copy(msgs[b].at[F : F + EXTRA, :128], times_ref.at[b], sems.at[b])
+        for b in range(start // 2, stop // 2)
+    ]
+    for copy in copies:
+        copy.start()
     at = 0
     for k, (_, ready, chunks) in enumerate(sets):
         heads = refs[at : at + 1 + ready]
@@ -89,7 +95,6 @@
                 hi, lo = halves(parts[c][:, cols])
                 w_scr[j, c * each : (c + 1) * each, :] = hi
                 w_scr[j, rows + c * each : rows + (c + 1) * each, :] = lo
-    start, stop = leaves_at
     for t in range(start, stop):
         if nacc:
             o_scr[t - start] = sum(ref[t, row : row + rows, :] for ref in refs[at : at + nacc])
@@ -103,13 +108,13 @@
         relative = {"own": 1, "pair": 2 - 2 * odd, "next": 2 * odd}[kind]
         column.append(relative * leaves + 2 * (2 * x + core))
 
-    copy.wait()
+    for copy in copies:
+        copy.wait()
     count = jnp.int32(0)
     list_ref[0] = 0
     for t in range(start, stop):
         for j in range(2 * nset):
-            helper = 2 * lax.rem(x + t // 4, xs) + (core if t // 2 % 2 == 0 else 1 - core)
-            times = times_ref[helper, t % 2, column[j // 2] + j % 2]
+            times = times_ref[t // 2, t % 2, column[j // 2] + j % 2]
 
             @pl.when(times > 0)
             def _(count=count, t=t, j=j, times=times):
@@ -167,7 +172,7 @@
                 ref[:, cols] = o_scr[t + leaf, top : top + tall, :]
 
 
-def near_call(name, where, targets, leaves_at, sources, rows, row=0, acc=(), after=()):
+def near_call(name, pos, msgs, targets, leaves_at, sources, rows, row=0, acc=(), after=()):
     nset = len(sources)
     start, stop = leaves_at
     tall = R // 2
@@ -182,8 +187,8 @@
         pltpu.VMEM((2, 2 * LEAF, LEAF), BF),
         pltpu.SMEM((2 * nset * (stop - start),), F32),
         pltpu.SMEM((2 * nset * (stop - start),), jnp.int32),
-        pltpu.SMEM((where[1].shape[0], EXTRA, 128), F32),
-        pltpu.SemaphoreType.DMA,
+        pltpu.SMEM((len(msgs), EXTRA, 128), F32),
+        pltpu.SemaphoreType.DMA((len(msgs),)),
     ]
     if not acc:
         out = [jax.ShapeDtypeStruct((stop - start, rows, LEAF), F32)]
@@ -194,17 +199,18 @@
     sets = tuple((kind, len(heads) - 1, len(chunks)) for kind, heads, chunks in sources)
     return pl.pallas_call(
         partial(
-            near_body, targets[0].shape[0] // 4, sets, leaves_at, rows, row, len(acc), len(out)
+            near_body, len(msgs) // 2, sets, leaves_at, rows, row, len(acc), len(out)
         ),
         name=name,
         out_shape=out,
-        in_specs=[smem, pl.BlockSpec(memory_space=pl.ANY)]
+        in_specs=[smem]
+        + [pl.BlockSpec(memory_space=pl.ANY)] * len(msgs)
         + [vmem] * (2 + len(operands))
         + [pl.BlockSpec(memory_space=pl.ANY)] * len(after),
         out_specs=[vmem] * len(out),
         scratch_shapes=scratch,
         compiler_params=pltpu.CompilerParams(vmem_limit_bytes=VMEM_LIMIT),
-    )(*where, *targets, *operands, *after)
+    )(pos, *msgs, *targets, *operands, *after)
 
 
 def source_body(pts_ref, side_ref, off_ref):
@@ -235,7 +241,8 @@
 
 
 def leaf_body(xs, pos_ref, count_ref, src_ref, pts_in, w_in, interp_in, *refs):
-    msg, pts_ref, w_ref, interp_ref, scr, sems = refs
+    msgs = refs[: 2 * xs]
+    pts_ref, w_ref, interp_ref, scr, sems = refs[2 * xs :]
     copies = [
         pltpu.make_async_copy(pts_in, pts_ref, sems.at[0]),
         pltpu.make_async_copy(w_in, w_ref, sems.at[1]),
@@ -243,7 +250,7 @@
     ]
     for copy in copies:
         copy.start()
-    group, leaves = pos_ref[2], pos_ref[3]
+    x, core, group, leaves = pos_ref[0], pos_ref[1], pos_ref[2], pos_ref[3]
     lane = lax.broadcasted_iota(jnp.int32, (1, 128), 1) + (group - 1) * leaves
     times = []
     for leaf in range(2):
@@ -261,26 +268,27 @@
     scr[...] = total
     rows = R // (2 * xs)
     tall = share_rows(xs)
-    for helper in range(2 * xs):
-        msg[helper, :F, :] = pts_ref[...]
-        msg[helper, F : F + EXTRA, :] = jnp.zeros((EXTRA, 2 * LEAF), F32)
-        msg[helper, F : F + EXTRA, :128] = times
+    for n, msg in enumerate(msgs):
+        helper = 2 * lax.rem(x + n // 2, xs) + (core if n % 2 == 0 else 1 - core)
+        msg[:F, :] = pts_ref[...]
+        msg[F : F + EXTRA, :] = jnp.zeros((EXTRA, 2 * LEAF), F32)
+        msg[F : F + EXTRA, :128] = times
         for i in range(rows // tall):
-            at = helper * rows + i * tall
-            msg[helper, F + EXTRA :, i * SK : (i + 1) * SK] = scr[at : at + tall, :]
+            at = pl.multiple_of(helper * rows + i * tall, tall)
+            msg[F + EXTRA :, i * SK : (i + 1) * SK] = scr[pl.ds(at, tall), :]
 
 
 def leaf_call(xs, pos, near_count, near_src, points, weights, interp):
     vmem = pl.BlockSpec(memory_space=pltpu.VMEM)
     smem = pl.BlockSpec(memory_space=pltpu.SMEM)
-    hbm = pl.BlockSpec(memory_space=pltpu.HBM)
+    anywhere = pl.BlockSpec(memory_space=pl.ANY)
     height = F + EXTRA + share_rows(xs)
     return pl.pallas_call(
         partial(leaf_body, xs),
         name="leaf_up",
-        out_shape=jax.ShapeDtypeStruct((2 * xs, height, 2 * LEAF), F32),
-        in_specs=[smem, smem, smem, hbm, hbm, hbm],
-        out_specs=vmem,
+        out_shape=[jax.ShapeDtypeStruct((height, 2 * LEAF), F32)] * (2 * xs),
+        in_specs=[smem, smem, smem, anywhere, anywhere, anywhere],
+        out_specs=[vmem] * (2 * xs),
         scratch_shapes=[
             pltpu.VMEM(points.shape, F32),
             pltpu.VMEM(weights.shape, F32),
@@ -292,47 +300,63 @@
     )(pos, near_count, near_src, points, weights, interp)
 
 
-def skel_body(xs, pos_ref, index_ref, msgs, out_ref, side_ref, off_ref):
-    nblk = 2 * xs
-    rows = R // nblk
+def skel_body(xs, pos_ref, index_ref, *refs):
+    msgs, (out_ref, side_ref, off_ref) = refs[:-3], refs[-3:]
+    rows = R // (2 * xs)
     tall = share_rows(xs)
     total = jnp.zeros((2 * F, SK), F32)
     value = jnp.zeros((tall, 2 * LEAF), F32)
     spot = lax.broadcasted_iota(jnp.int32, (2 * LEAF, SK), 0)
     x, core = pos_ref[0], pos_ref[1]
-    for b in range(nblk):
+    for b, msg in enumerate(msgs):
         helper = 2 * lax.rem(x + b // 2, xs) + (core if b % 2 == 0 else 1 - core)
-        side, off = target_side(msgs[helper, :F, :] * SCALE)
+        side, off = target_side(msg[:F, :] * SCALE)
         for leaf in range(2):
             part = slice(leaf * LEAF, (leaf + 1) * LEAF)
             side_ref[2 * b + leaf] = side[:, part]
             off_ref[2 * b + leaf] = jnp.broadcast_to(off[:, part], (8, LEAF))
         hot = spot + helper * (2 * LEAF) == index_ref[...]
         total = total + dot(side[: 2 * F], hot.astype(F32).astype(BF))
-        value = value + msgs[helper, F + EXTRA :, :]
-    for n in range(out_ref.shape[0]):
-        out_ref[n, :F, :] = total[:F] + total[F:]
-        for i in range(rows // tall):
-            part = slice(F + i * tall, F + (i + 1) * tall)
-            out_ref[n, part, :] = value[:, i * SK : (i + 1) * SK]
-
-
-def skel_call(xs, copies, pos, index, msgs):
+        value = value + msg[F + EXTRA :, :]
+    out_ref[:F, :] = total[:F] + total[F:]
+    for i in range(rows // tall):
+        out_ref[F + i * tall : F + (i + 1) * tall, :] = value[:, i * SK : (i + 1) * SK]
+
+
+def skel_call(xs, pos, index, msgs):
     rows = R // (2 * xs)
-    nblk = 2 * xs
-    vmem = pl.BlockSpec(memory_space=pltpu.VMEM)
-    return pl.pallas_call(
+    leaves = 2 * len(msgs)
+    vmem = pl.BlockSpec(memory_space=pltpu.VMEM)
+    payload, *targets = pl.pallas_call(
         partial(skel_body, xs),
         name="skeleton",
         out_shape=[
-            jax.ShapeDtypeStruct((copies, F + rows, SK), F32),
-            jax.ShapeDtypeStruct((2 * nblk, 4 * F, LEAF), BF),
-            jax.ShapeDtypeStruct((2 * nblk, 8, LEAF), F32),
+            jax.ShapeDtypeStruct((F + rows, SK), F32),
+            jax.ShapeDtypeStruct((leaves, 4 * F, LEAF), BF),
+            jax.ShapeDtypeStruct((leaves, 8, LEAF), F32),
         ],
-        in_specs=[pl.BlockSpec(memory_space=pltpu.SMEM)] + [vmem] * 2,
+        in_specs=[pl.BlockSpec(memory_space=pltpu.SMEM)] + [vmem] * (1 + len(msgs)),
         out_specs=[vmem] * 3,
         compiler_params=pltpu.CompilerParams(vmem_limit_bytes=VMEM_LIMIT),
-    )(pos, index, msgs)
+    )(pos, index, *msgs)
+    return payload, targets
+
+
+def stack_body(*refs):
+    for n, ref in enumerate(refs[:-1]):
+        refs[-1][n] = ref[...]
+
+
+def stack_call(pieces):
+    vmem = pl.BlockSpec(memory_space=pltpu.VMEM)
+    return pl.pallas_call(
+        stack_body,
+        name="stack",
+        out_shape=jax.ShapeDtypeStruct((len(pieces), *pieces[0].shape), F32),
+        in_specs=[vmem] * len(pieces),
+        out_specs=vmem,
+        compiler_params=pltpu.CompilerParams(vmem_limit_bytes=VMEM_LIMIT),
+    )(*pieces)
 
 
 def upper_start(level, groups):
@@ -347,19 +371,19 @@
     out_ref, p_scr, u_scr, f_scr = refs[-4:]
     levels = groups.bit_length() - 1
     group = pos_ref[2]
-    odd = group % 2
     start = [list_start(level, groups) for level in range(levels)]
     for n in range(groups // 2):
-        p_scr[2 * n + odd] = alike_ref[n, :F, :]
-        u_scr[2 * n + odd] = alike_ref[n, F:, :]
-        p_scr[2 * n + 1 - odd] = beside_ref[n, :F, :]
-        u_scr[2 * n + 1 - odd] = beside_ref[n, F:, :]
+        same, other = group ^ (2 * n), group ^ (2 * n + 1)
+        p_scr[same] = alike_ref[n, :F, :]
+        u_scr[same] = alike_ref[n, F:, :]
+        p_scr[other] = beside_ref[n, :F, :]
+        u_scr[other] = beside_ref[n, F:, :]
     spot = lax.broadcasted_iota(jnp.int32, (2 * SK, SK), 0)
     for level in range(1, levels):
         for n in range(groups >> level):
             row = upper_start(level, groups) + n
             left = start[level - 1] + 2 * n
-            hot = (spot == node_ref[row]).astype(F32).astype(BF)
+            hot = (spot == node_ref[row : row + 1, :]).astype(F32).astype(BF)
             hi, lo = halves(jnp.concatenate([p_scr[left], p_scr[left + 1]], axis=1))
             both = dot(jnp.concatenate([hi, lo], axis=0), hot)
             p_scr[start[level] + n] = both[:F] + both[F:]
@@ -412,7 +436,7 @@
             pltpu.VMEM((groups.bit_length(), rows, SK), F32),
         ],
         compiler_params=pltpu.CompilerParams(vmem_limit_bytes=VMEM_LIMIT),
-    )(pos, far_nodes.T, skel_node[:, None, :], transfer, alike, beside, *after)
+    )(pos, far_nodes.T, skel_node, transfer, alike, beside, *after)
 
 
 def final_body(xs, pos_ref, interp_ref, *refs):
@@ -500,48 +524,50 @@
     order = [(dx, dc) for dx in range(xs) for dc in range(2)]
 
     pts_y = lax.ppermute(points, "leaf", beside)
-    w_y = [lax.ppermute(weights[c * rows : (c + 1) * rows], "leaf", beside) for c in range(2)]
-    msgs = leaf_call(xs, pos, near_count, near_src, points, weights, interp)
-    got = lax.all_to_all(msgs, "help", 0, 0)
+    w_own = [weights[:rows], weights[rows:]]
+    w_y = [lax.ppermute(chunk, "leaf", beside) for chunk in w_own]
+    sent = leaf_call(xs, pos, near_count, near_src, points, weights, interp)
+    got = [
+        lax.ppermute(sent[n], "help", help_pairs(xs, -dx, dc))
+        for n, (dx, dc) in enumerate(order)
+        if n
+    ]
     pts_z = lax.ppermute(pts_y, "leaf", across)
-
-    payload, *targets = skel_call(xs, groups // 2, pos, skel_group, got)
-    where = (pos, got)
-    parity = [[n for n in range(groups) if n % 2 == odd] for odd in range(2)]
-    alike = lax.all_to_all(payload, "leaf", 0, 0, axis_index_groups=parity)
-    pts_z, w_y[0] = together(pts_z, w_y[0])
     w_z = [lax.ppermute(w_y[0], "leaf", across)]
-    (own,) = near_call(
-        "near_own", where, targets, (0, 2 * helpers), [("own", (points,), [weights])], R
-    )
-    own, w_y[1] = together(own, w_y[1])
+    w_y = list(together(*w_y))
     w_z.append(lax.ppermute(w_y[1], "leaf", across))
+
+    got, w_y = together(got, w_y)
+    msgs = [sent[0]] + [got[order.index((-dx % xs, dc)) - 1] for dx, dc in order[1:]]
+    payload, targets = skel_call(xs, pos, skel_group, msgs)
+    pieces = [payload]
+    for mask in range(2, groups, 2):
+        pieces.append(lax.ppermute(payload, "leaf", [(i, i ^ mask) for i in range(groups)]))
+
+    sources = [("own", (points,), [weights]), ("pair", (pts_y,), w_y)]
+    (near,) = near_call("near_own_pair", pos, msgs, targets, (0, 2 * helpers), sources, R)
     z_side = source_call(pts_z)
-    alike, w_y[1] = together(alike, w_y[1])
-    side = lax.ppermute(alike, "leaf", beside)
-    (pair,) = near_call(
-        "near_pair", where, targets, (0, 2 * helpers), [("pair", (pts_y,), w_y)], R
-    )
-
     sums, part = [], []
     for c in range(2):
+        if c == 1:
+            pieces, w_z[1], part = together(pieces, w_z[1], part)
+            alike = stack_call(pieces)
+            side = lax.ppermute(alike, "leaf", beside)
         part = near_call(
-            "near_next_away", where, targets, (4, 2 * helpers), [("next", z_side, w_z[c : c + 1])],
-            rows, c * rows, (own, pair), part[:1],
+            "near_next_away", pos, msgs, targets, (4, 2 * helpers),
+            [("next", z_side, w_z[c : c + 1])], rows, c * rows, [near], part[:1],
         )
         kept, given = part[::2], part[1::2]
         sums.append((kept, [from_help(value, 0, 1) for value in given]))
     parts = []
     for c in range(2):
         kept, mates = sums[c]
-        if c == 0:
-            mates, side = together(mates, side)
         both = add_call(*zip(kept, mates))
         parts.append([to_help(value, dx + 1) for dx, value in enumerate(both)])
     v_own = far_call(groups, pos, far_nodes, skel_node, transfer, alike, side, both[:1])
     values = [v_own] + [from_help(v_own, dx, dc) for dx, dc in order[1:]]
     home = near_call(
-        "near_next_home", where, targets, (0, 4), [("next", z_side, w_z)], R, 0, (own, pair), [v_own]
+        "near_next_home", pos, msgs, targets, (0, 4), [("next", z_side, w_z)], R, 0, [near], [v_own]
     )
     mate = [from_help(value, 0, 1) for value in home[2:]]
     mine = add_call(*[[home[c], *parts[c]] for c in range(2)])

time: 132 us -> 113 us (0.86)
  the two profiles are of different devices: /device:TPU:6 before, /device:TPU:12 now
where the time goes in v7:
time: 113 us; the launch traced here: 112 us
  waiting for transfers between devices  40.2 us (36%)
  Pallas kernels  38.5 us (34%)
  starting transfers between devices  25.6 us (23%)
  local copies, waits for them, and re-layouts  6.96 us (6%)
    pallas_call x4, Pallas kernels, near_call(): pl.pallas_call(partial(near_body, len(msgs) // 2, sets, leaves_at, rows,...  26.2 us
    ppermute x2, waiting for transfers between devices, shards(): w_y = [lax.ppermute(chunk, 'leaf', beside) for chunk in w_own]  15 us
    ppermute x1, waiting for transfers between devices, shards(): side = lax.ppermute(alike, 'leaf', beside)  10.7 us
    ppermute x3, waiting for transfers between devices, shards(): lax.ppermute(sent[n], 'help', help_pairs(xs, -dx, dc))  10.1 us
    ppermute x7, starting transfers between devices, from_help(): return lax.ppermute(value, 'help', help_pairs(xs, dx, dc))  7.15 us
    pallas_call x1, Pallas kernels, far_call(): pl.pallas_call(partial(far_body, groups, rows), name='far', out_shape=jax...  6.53 us
    unnamed x24, local copies, waits for them, and re-layouts  4.77 us
    ppermute x3, starting transfers between devices, shards(): lax.ppermute(payload, 'leaf', [(i, i ^ mask) for i in range(groups)])  4.15 us
  transfers between devices with their start and end apart: 22, of which 8 were waited for; matrix products, arithmetic and copies ran while one was open for 0% of the time, Pallas kernels for 33%

profile of v7, /device:TPU:12, one launch (start us, length us, event | category | flops | bytes accessed | tf_op | source)
XLA Modules:
  0.0 111.6 jit_solution(16570430671688747615)
XLA Ops:
  0.0 2.2 %fusion = (f32[128,1024]{1,0:T(8,128)S(1)}, f32[128,1024]{1,0:T(8,128)}) fusion(f32[256,1024]{1,0:T(8,128)} %refs_7_.1), kind=kLoop, calls=%fused_computation.1 | loop fusion | bytes 2097152 | tf_op jit(solution)/shard_map/slice | solution.py:527
  2.7 1.5 %collective-permute-start.4 = (f32[128,1024]{1,0:T(8,128)S(1)}, f32[128,1024]{1,0:T(8,128)S(1)}, u32[]{:S(2)}, u32[]{:S(2)}) collective-permute-start(f32[128,1024]{1,0:T(8,128)S(1)} %get-tuple-element.69), channel_id=1, source_target_pairs={{0,4},{4,0},{8,12},{12,8},{16,20},{20,16},{24,28},{28,24},{1,5},{5... | collective-permute-start | bytes 1572872 | tf_op jit(solution)/shard_map/ppermute | solution.py:528
  9.6 1.5 %leaf_up.1 = (f32[88,1024]{1,0:T(8,128)S(1)}, f32[88,1024]{1,0:T(8,128)S(1)}, f32[88,1024]{1,0:T(8,128)S(1)}, f32[88,1024]{1,0:T(8,128)S(1)}) custom-call(s32[4]{0:T(128)S(1)} %pad_add_fusion.pos_ref, s32[1,2]{1,0:T(1,128)S(1)} %copy-done.11, s32[2,32]{1,0:T(2,128)S(1)} %copy-done.9, f32[64,1024]{1,0:T(8,128)S(1)} %copy-done.5, f32[256,1024]{1,0:T(8,128)S(1)} %copy-done, ...), custom_call_target="tpu_custom_call" | custom-call | tf_op jit(solution)/shard_map/leaf_up/pallas_call | solution.py:286
  11.1 6.1 %collective-permute-done.3.refs_9_ = f32[128,1024]{1,0:T(8,128)S(1)} collective-permute-done((f32[128,1024]{1,0:T(8,128)}, f32[128,1024]{1,0:T(8,128)S(1)}, u32[]{:S(2)}, u32[]{:S(2)}) %collective-permute-start.3) | collective-permute-done | bytes 524320 | tf_op jit(solution)/shard_map/ppermute | solution.py:528
  17.2 2.3 %collective-permute-start.11 = (f32[128,1024]{1,0:T(8,128)S(1)}, f32[128,1024]{1,0:T(8,128)S(1)}, u32[]{:S(2)}, u32[]{:S(2)}) collective-permute-start(f32[128,1024]{1,0:T(8,128)S(1)} %collective-permute-done.3.refs_9_), channel_id=1, source_target_pairs={{0,8},{8,16},{16,24},{12,4},{20,12},{28,20},{1,9},{9,17},{17,25},{... | collective-permute-start | bytes 1572872 | tf_op jit(solution)/shard_map/ppermute | solution.py:536
  19.6 8.9 %collective-permute-done.4.refs_10_ = f32[128,1024]{1,0:T(8,128)S(1)} collective-permute-done((f32[128,1024]{1,0:T(8,128)S(1)}, f32[128,1024]{1,0:T(8,128)S(1)}, u32[]{:S(2)}, u32[]{:S(2)}) %collective-permute-start.4) | collective-permute-done | bytes 524320 | tf_op jit(solution)/shard_map/ppermute | solution.py:528
  28.5 2.3 %collective-permute-start.8 = (f32[128,1024]{1,0:T(8,128)S(1)}, f32[128,1024]{1,0:T(8,128)S(1)}, u32[]{:S(2)}, u32[]{:S(2)}) collective-permute-start(f32[128,1024]{1,0:T(8,128)S(1)} %collective-permute-done.4.refs_10_), channel_id=1, source_target_pairs={{0,8},{8,16},{16,24},{12,4},{20,12},{28,20},{1,9},{9,17},{17,25},{... | collective-permute-start | bytes 1572872 | tf_op jit(solution)/shard_map/ppermute | solution.py:538
  30.8 1.6 %collective-permute-start.1 = (f32[88,1024]{1,0:T(8,128)S(1)}, f32[88,1024]{1,0:T(8,128)S(1)}, u32[]{:S(2)}, u32[]{:S(2)}) collective-permute-start(f32[88,1024]{1,0:T(8,128)S(1)} %get-tuple-element.39), channel_id=1, source_target_pairs={{2,0},{3,1},{0,2},{1,3},{6,4},{7,5},{4,6},{5,7},{10,8},{11,9},{8,1... | collective-permute-start | bytes 1081352 | tf_op jit(solution)/shard_map/ppermute | solution.py:531
  33.0 2.3 %collective-permute-start.10 = (f32[64,1024]{1,0:T(8,128)S(1)}, f32[64,1024]{1,0:T(8,128)S(1)}, u32[]{:S(2)}, u32[]{:S(2)}) collective-permute-start(f32[64,1024]{1,0:T(8,128)S(1)} %collective-permute-done.9.refs_8_), channel_id=1, source_target_pairs={{0,8},{8,16},{16,24},{12,4},{20,12},{28,20},{1,9},{9,17},{17,25},{... | collective-permute-start | bytes 786440 | tf_op jit(solution)/shard_map/ppermute | solution.py:535
  35.3 6.1 %collective-permute-done.1.refs_2_ = f32[88,1024]{1,0:T(8,128)S(1)} collective-permute-done((f32[88,1024]{1,0:T(8,128)S(1)}, f32[88,1024]{1,0:T(8,128)S(1)}, u32[]{:S(2)}, u32[]{:S(2)}) %collective-permute-start.1) | collective-permute-done | bytes 360480 | tf_op jit(solution)/shard_map/ppermute | solution.py:531
  41.5 4.0 %collective-permute-done.2.refs_3_ = f32[88,1024]{1,0:T(8,128)S(1)} collective-permute-done((f32[88,1024]{1,0:T(8,128)S(1)}, f32[88,1024]{1,0:T(8,128)S(1)}, u32[]{:S(2)}, u32[]{:S(2)}) %collective-permute-start.2) | collective-permute-done | bytes 360480 | tf_op jit(solution)/shard_map/ppermute | solution.py:531
  46.8 1.6 %collective-permute-start.7 = (f32[128,256]{1,0:T(8,128)S(1)}, f32[128,256]{1,0:T(8,128)S(1)}, u32[]{:S(2)}, u32[]{:S(2)}) collective-permute-start(f32[128,256]{1,0:T(8,128)S(1)} %get-tuple-element.55.refs_0_), channel_id=1, source_target_pairs={{0,24},{4,28},{8,16},{12,20},{16,8},{20,12},{24,0},{28,4},{1,25},{... | collective-permute-start | bytes 393224 | tf_op jit(solution)/shard_map/ppermute | solution.py:545
  51.5 13.3 %near_own_pair.1.refs_9_.refs_10_ = f32[8,256,512]{2,1,0:T(8,128)S(1)} custom-call(s32[4]{0:T(128)S(1)} %pad_add_fusion.pos_ref, f32[88,1024]{1,0:T(8,128)S(1)} %get-tuple-element.37.refs_0_, f32[88,1024]{1,0:T(8,128)S(1)} %collective-permute-done.refs_1_, f32[88,1024]{1,0:T(8,128)S(1)} %collective-permute-done.1.refs_2_, ...), custom_call_target="tpu_custom_call" | custom-call | tf_op jit(solution)/shard_map/near_own_pair/pallas_call | solution.py:200
  64.8 3.9 %near_next_away.2 = (f32[128,1024]{1,0:T(8,128)S(1)}, f32[128,1024]{1,0:T(8,128)S(1)}) custom-call(s32[4]{0:T(128)S(1)} %pad_add_fusion.pos_ref, f32[88,1024]{1,0:T(8,128)S(1)} %get-tuple-element.37.refs_0_, f32[88,1024]{1,0:T(8,128)S(1)} %collective-permute-done.refs_1_, f32[88,1024]{1,0:T(8,128)S(1)} %collective-permute-done.1.refs_2_, ...), custom_call_target="tpu_custom_call" | custom-call | tf_op jit(solution)/shard_map/near_next_away/pallas_call | solution.py:200
  68.8 3.1 %collective-permute-start.17 = (f32[128,1024]{1,0:T(8,128)S(1)}, f32[128,1024]{1,0:T(8,128)S(1)}, u32[]{:S(2)}, u32[]{:S(2)}) collective-permute-start(f32[128,1024]{1,0:T(8,128)S(1)} %get-tuple-element.54), channel_id=1, source_target_pairs={{1,0},{0,1},{3,2},{2,3},{5,4},{4,5},{7,6},{6,7},{9,8},{8,9},{11,10... | collective-permute-start | bytes 1572872 | tf_op jit(solution)/shard_map/ppermute | solution.py:513
  71.9 4.1 %near_next_away.3 = (f32[128,1024]{1,0:T(8,128)S(1)}, f32[128,1024]{1,0:T(8,128)S(1)}) custom-call(s32[4]{0:T(128)S(1)} %pad_add_fusion.pos_ref, f32[88,1024]{1,0:T(8,128)S(1)} %get-tuple-element.37.refs_0_, f32[88,1024]{1,0:T(8,128)S(1)} %collective-permute-done.refs_1_, f32[88,1024]{1,0:T(8,128)S(1)} %collective-permute-done.1.refs_2_, ...), custom_call_target="tpu_custom_call" | custom-call | tf_op jit(solution)/shard_map/near_next_away/pallas_call | solution.py:200
  76.9 2.9 %collective-permute-start.18 = (f32[128,1024]{1,0:T(8,128)S(1)}, f32[128,1024]{1,0:T(8,128)S(1)}, u32[]{:S(2)}, u32[]{:S(2)}) collective-permute-start(f32[128,1024]{1,0:T(8,128)S(1)} %add_parts.4), channel_id=1, source_target_pairs={{2,0},{3,1},{0,2},{1,3},{6,4},{7,5},{4,6},{5,7},{10,8},{11,9},{8,1... | collective-permute-start | bytes 1572872 | tf_op jit(solution)/shard_map/ppermute | solution.py:516
  80.0 10.7 %collective-permute-done.12.beside_ref = f32[4,128,256]{2,1,0:T(8,128)S(1)} collective-permute-done((f32[4,128,256]{2,1,0:T(8,128)S(1)}, f32[4,128,256]{2,1,0:T(8,128)S(1)}, u32[]{:S(2)}, u32[]{:S(2)}) %collective-permute-start.12) | collective-permute-done | bytes 524320 | tf_op jit(solution)/shard_map/ppermute | solution.py:555
  90.7 6.5 %far.1.refs_11_.refs_0_ = f32[64,256]{1,0:T(8,128)S(1)} custom-call(s32[4]{0:T(128)S(1)} %pad_add_fusion.pos_ref, s32[4,14]{1,0:T(4,128)S(1)} %bitcast.4, s32[6,256]{1,0:T(8,128)S(1)} %copy-done.7, f32[6,512,256]{2,1,0:T(8,128)S(1)} %copy-done.4, f32[4,128,256]{2,1,0:T(8,128)S(1)} %stack.17.alike_ref, f32[4,128,256]{2,1,0:T(8,128)S(1)} %collective-permute-done.12.beside_ref, ...), custom_call_target="tpu_custom_call" | custom-call | tf_op jit(solution)/shard_map/far/pallas_call | solution.py:426
  97.2 4.8 %near_next_home.1 = (f32[128,1024]{1,0:T(8,128)S(1)}, f32[128,1024]{1,0:T(8,128)S(1)}, f32[128,1024]{1,0:T(8,128)S(1)}, f32[128,1024]{1,0:T(8,128)S(1)}) custom-call(s32[4]{0:T(128)S(1)} %pad_add_fusion.pos_ref, f32[88,1024]{1,0:T(8,128)S(1)} %get-tuple-element.37.refs_0_, f32[88,1024]{1,0:T(8,128)S(1)} %collective-permute-done.refs_1_, ...), custom_call_target="tpu_custom_call" | custom-call | tf_op jit(solution)/shard_map/near_next_home/pallas_call | solution.py:200
  102.6 2.3 %collective-permute-start.16 = (f32[64,256]{1,0:T(8,128)S(1)}, f32[64,256]{1,0:T(8,128)S(1)}, u32[]{:S(2)}, u32[]{:S(2)}) collective-permute-start(f32[64,256]{1,0:T(8,128)S(1)} %far.1.refs_11_.refs_0_), channel_id=1, source_target_pairs={{3,0},{2,1},{1,2},{0,3},{7,4},{6,5},{5,6},{4,7},{11,8},{10,9},{9,1... | collective-permute-start | bytes 196616 | tf_op jit(solution)/shard_map/ppermute | solution.py:513
  105.6 1.8 %collective-permute-done.16.refs_3_ = f32[64,256]{1,0:T(8,128)S(1)} collective-permute-done((f32[64,256]{1,0:T(8,128)S(1)}, f32[64,256]{1,0:T(8,128)S(1)}, u32[]{:S(2)}, u32[]{:S(2)}) %collective-permute-start.16) | collective-permute-done | bytes 65568 | tf_op jit(solution)/shard_map/ppermute | solution.py:513
  107.4 2.0 %collective-permute-done.15.refs_2_ = f32[64,256]{1,0:T(8,128)S(1)} collective-permute-done((f32[64,256]{1,0:T(8,128)S(1)}, f32[64,256]{1,0:T(8,128)S(1)}, u32[]{:S(2)}, u32[]{:S(2)}) %collective-permute-start.15) | collective-permute-done | bytes 65568 | tf_op jit(solution)/shard_map/ppermute | solution.py:513
  109.4 2.2 %join.1 = f32[256,1024]{1,0:T(8,128)} custom-call(s32[4]{0:T(128)S(1)} %pad_add_fusion.pos_ref, f32[2,512,256]{2,1,0:T(8,128)S(1)} %copy-done.3, f32[64,256]{1,0:T(8,128)S(1)} %far.1.refs_11_.refs_0_, f32[64,256]{1,0:T(8,128)S(1)} %collective-permute-done.14.refs_1_, f32[64,256]{1,0:T(8,128)S(1)} %collective-permute-done.15.refs_2_, ...), custom_call_target="tpu_custom_call" | custom-call | tf_op jit(solution)/shard_map/join/pallas_call | solution.py:482
  (59 shorter events, 13.1 us)
Async XLA Ops:
  0.0 51.5 %copy-start.1 = (f32[256,1024]{1,0:T(8,128)S(1)}, f32[256,1024]{1,0:T(8,128)}, u32[]{:S(2)}) copy-start(f32[256,1024]{1,0:T(8,128)} %refs_7_.1) | copy-start | bytes 3145732
  0.0 51.5 %copy-start.6 = (f32[64,1024]{1,0:T(8,128)S(1)}, f32[64,1024]{1,0:T(8,128)}, u32[]{:S(2)}) copy-start(f32[64,1024]{1,0:T(8,128)} %refs_6_.1) | copy-start | bytes 786436
  2.2 15.0 %collective-permute-start.3 = (f32[128,1024]{1,0:T(8,128)}, f32[128,1024]{1,0:T(8,128)S(1)}, u32[]{:S(2)}, u32[]{:S(2)}) collective-permute-start(f32[128,1024]{1,0:T(8,128)} %get-tuple-element.70), channel_id=1, source_target_pairs={{0,4},{4,0},{8,12},{12,8},{16,20},{20,16},{24,28},{28,24},{1,5},{5... | collective-permute-start | bytes 1572872 | tf_op jit(solution)/shard_map/ppermute | solution.py:528
  2.7 25.7 %collective-permute-start.4 = (f32[128,1024]{1,0:T(8,128)S(1)}, f32[128,1024]{1,0:T(8,128)S(1)}, u32[]{:S(2)}, u32[]{:S(2)}) collective-permute-start(f32[128,1024]{1,0:T(8,128)S(1)} %get-tuple-element.69), channel_id=1, source_target_pairs={{0,4},{4,0},{8,12},{12,8},{16,20},{20,16},{24,28},{28,24},{1,5},{5... | collective-permute-start | bytes 1572872 | tf_op jit(solution)/shard_map/ppermute | solution.py:528
  4.2 28.7 %collective-permute-start.9 = (f32[64,1024]{1,0:T(8,128)}, f32[64,1024]{1,0:T(8,128)S(1)}, u32[]{:S(2)}, u32[]{:S(2)}) collective-permute-start(f32[64,1024]{1,0:T(8,128)} %refs_6_.1), channel_id=1, source_target_pairs={{0,4},{4,0},{8,12},{12,8},{16,20},{20,16},{24,28},{28,24},{1,5},{5... | collective-permute-start | bytes 786440 | tf_op jit(solution)/shard_map/ppermute | solution.py:526
  11.1 21.9 %collective-permute-start = (f32[88,1024]{1,0:T(8,128)S(1)}, f32[88,1024]{1,0:T(8,128)S(1)}, u32[]{:S(2)}, u32[]{:S(2)}) collective-permute-start(f32[88,1024]{1,0:T(8,128)S(1)} %get-tuple-element.38), channel_id=1, source_target_pairs={{1,0},{0,1},{3,2},{2,3},{5,4},{4,5},{7,6},{6,7},{9,8},{8,9},{11,10... | collective-permute-start | bytes 1081352 | tf_op jit(solution)/shard_map/ppermute | solution.py:531
  17.2 47.6 %collective-permute-start.11 = (f32[128,1024]{1,0:T(8,128)S(1)}, f32[128,1024]{1,0:T(8,128)S(1)}, u32[]{:S(2)}, u32[]{:S(2)}) collective-permute-start(f32[128,1024]{1,0:T(8,128)S(1)} %collective-permute-done.3.refs_9_), channel_id=1, source_target_pairs={{0,8},{8,16},{16,24},{12,4},{20,12},{28,20},{1,9},{9,17},{17,25},{... | collective-permute-start | bytes 1572872 | tf_op jit(solution)/shard_map/ppermute | solution.py:536
  28.5 43.4 %collective-permute-start.8 = (f32[128,1024]{1,0:T(8,128)S(1)}, f32[128,1024]{1,0:T(8,128)S(1)}, u32[]{:S(2)}, u32[]{:S(2)}) collective-permute-start(f32[128,1024]{1,0:T(8,128)S(1)} %collective-permute-done.4.refs_10_), channel_id=1, source_target_pairs={{0,8},{8,16},{16,24},{12,4},{20,12},{28,20},{1,9},{9,17},{17,25},{... | collective-permute-start | bytes 1572872 | tf_op jit(solution)/shard_map/ppermute | solution.py:538
  30.8 10.7 %collective-permute-start.1 = (f32[88,1024]{1,0:T(8,128)S(1)}, f32[88,1024]{1,0:T(8,128)S(1)}, u32[]{:S(2)}, u32[]{:S(2)}) collective-permute-start(f32[88,1024]{1,0:T(8,128)S(1)} %get-tuple-element.39), channel_id=1, source_target_pairs={{2,0},{3,1},{0,2},{1,3},{6,4},{7,5},{4,6},{5,7},{10,8},{11,9},{8,1... | collective-permute-start | bytes 1081352 | tf_op jit(solution)/shard_map/ppermute | solution.py:531
  32.9 12.5 %collective-permute-start.2 = (f32[88,1024]{1,0:T(8,128)S(1)}, f32[88,1024]{1,0:T(8,128)S(1)}, u32[]{:S(2)}, u32[]{:S(2)}) collective-permute-start(f32[88,1024]{1,0:T(8,128)S(1)} %get-tuple-element.40), channel_id=1, source_target_pairs={{3,0},{2,1},{1,2},{0,3},{7,4},{6,5},{5,6},{4,7},{11,8},{10,9},{9,1... | collective-permute-start | bytes 1081352 | tf_op jit(solution)/shard_map/ppermute | solution.py:531
  33.0 16.6 %collective-permute-start.10 = (f32[64,1024]{1,0:T(8,128)S(1)}, f32[64,1024]{1,0:T(8,128)S(1)}, u32[]{:S(2)}, u32[]{:S(2)}) collective-permute-start(f32[64,1024]{1,0:T(8,128)S(1)} %collective-permute-done.9.refs_8_), channel_id=1, source_target_pairs={{0,8},{8,16},{16,24},{12,4},{20,12},{28,20},{1,9},{9,17},{17,25},{... | collective-permute-start | bytes 786440 | tf_op jit(solution)/shard_map/ppermute | solution.py:535
  46.8 25.1 %collective-permute-start.7 = (f32[128,256]{1,0:T(8,128)S(1)}, f32[128,256]{1,0:T(8,128)S(1)}, u32[]{:S(2)}, u32[]{:S(2)}) collective-permute-start(f32[128,256]{1,0:T(8,128)S(1)} %get-tuple-element.55.refs_0_), channel_id=1, source_target_pairs={{0,24},{4,28},{8,16},{12,20},{16,8},{20,12},{24,0},{28,4},{1,25},{... | collective-permute-start | bytes 393224 | tf_op jit(solution)/shard_map/ppermute | solution.py:545
  48.4 23.5 %collective-permute-start.6 = (f32[128,256]{1,0:T(8,128)S(1)}, f32[128,256]{1,0:T(8,128)S(1)}, u32[]{:S(2)}, u32[]{:S(2)}) collective-permute-start(f32[128,256]{1,0:T(8,128)S(1)} %get-tuple-element.55.refs_0_), channel_id=1, source_target_pairs={{0,16},{4,20},{8,24},{12,28},{16,0},{20,4},{24,8},{28,12},{1,17},{... | collective-permute-start | bytes 393224 | tf_op jit(solution)/shard_map/ppermute | solution.py:545
  49.5 22.4 %collective-permute-start.5 = (f32[128,256]{1,0:T(8,128)S(1)}, f32[128,256]{1,0:T(8,128)S(1)}, u32[]{:S(2)}, u32[]{:S(2)}) collective-permute-start(f32[128,256]{1,0:T(8,128)S(1)} %get-tuple-element.55.refs_0_), channel_id=1, source_target_pairs={{0,8},{4,12},{8,0},{12,4},{16,24},{20,28},{24,16},{28,20},{1,9},{5... | collective-permute-start | bytes 393224 | tf_op jit(solution)/shard_map/ppermute | solution.py:545
  68.8 8.1 %collective-permute-start.17 = (f32[128,1024]{1,0:T(8,128)S(1)}, f32[128,1024]{1,0:T(8,128)S(1)}, u32[]{:S(2)}, u32[]{:S(2)}) collective-permute-start(f32[128,1024]{1,0:T(8,128)S(1)} %get-tuple-element.54), channel_id=1, source_target_pairs={{1,0},{0,1},{3,2},{2,3},{5,4},{4,5},{7,6},{6,7},{9,8},{8,9},{11,10... | collective-permute-start | bytes 1572872 | tf_op jit(solution)/shard_map/ppermute | solution.py:513
  76.1 3.7 %collective-permute-start.13 = (f32[128,1024]{1,0:T(8,128)S(1)}, f32[128,1024]{1,0:T(8,128)S(1)}, u32[]{:S(2)}, u32[]{:S(2)}) collective-permute-start(f32[128,1024]{1,0:T(8,128)S(1)} %get-tuple-element.62), channel_id=1, source_target_pairs={{1,0},{0,1},{3,2},{2,3},{5,4},{4,5},{7,6},{6,7},{9,8},{8,9},{11,10... | collective-permute-start | bytes 1572872 | tf_op jit(solution)/shard_map/ppermute | solution.py:513
  76.7 13.9 %collective-permute-start.12 = (f32[4,128,256]{2,1,0:T(8,128)S(1)}, f32[4,128,256]{2,1,0:T(8,128)S(1)}, u32[]{:S(2)}, u32[]{:S(2)}) collective-permute-start(f32[4,128,256]{2,1,0:T(8,128)S(1)} %stack.17.alike_ref), channel_id=1, source_target_pairs={{0,4},{4,0},{8,12},{12,8},{16,20},{20,16},{24,28},{28,24},{1,5},{5... | collective-permute-start | bytes 1572872 | tf_op jit(solution)/shard_map/ppermute | solution.py:555
  76.9 28.0 %collective-permute-start.18 = (f32[128,1024]{1,0:T(8,128)S(1)}, f32[128,1024]{1,0:T(8,128)S(1)}, u32[]{:S(2)}, u32[]{:S(2)}) collective-permute-start(f32[128,1024]{1,0:T(8,128)S(1)} %add_parts.4), channel_id=1, source_target_pairs={{2,0},{3,1},{0,2},{1,3},{6,4},{7,5},{4,6},{5,7},{10,8},{11,9},{8,1... | collective-permute-start | bytes 1572872 | tf_op jit(solution)/shard_map/ppermute | solution.py:516
  79.9 25.4 %collective-permute-start.19 = (f32[128,1024]{1,0:T(8,128)S(1)}, f32[128,1024]{1,0:T(8,128)S(1)}, u32[]{:S(2)}, u32[]{:S(2)}) collective-permute-start(f32[128,1024]{1,0:T(8,128)S(1)} %add_parts.3.refs_0_), channel_id=1, source_target_pairs={{2,0},{3,1},{0,2},{1,3},{6,4},{7,5},{4,6},{5,7},{10,8},{11,9},{8,1... | collective-permute-start | bytes 1572872 | tf_op jit(solution)/shard_map/ppermute | solution.py:516
  102.0 7.3 %collective-permute-start.20 = (f32[128,1024]{1,0:T(8,128)S(1)}, f32[128,1024]{1,0:T(8,128)S(1)}, u32[]{:S(2)}, u32[]{:S(2)}) collective-permute-start(f32[128,1024]{1,0:T(8,128)S(1)} %get-tuple-element.67), channel_id=1, source_target_pairs={{1,0},{0,1},{3,2},{2,3},{5,4},{4,5},{7,6},{6,7},{9,8},{8,9},{11,10... | collective-permute-start | bytes 1572872 | tf_op jit(solution)/shard_map/ppermute | solution.py:513
  102.1 7.3 %collective-permute-start.21 = (f32[128,1024]{1,0:T(8,128)S(1)}, f32[128,1024]{1,0:T(8,128)S(1)}, u32[]{:S(2)}, u32[]{:S(2)}) collective-permute-start(f32[128,1024]{1,0:T(8,128)S(1)} %get-tuple-element.68), channel_id=1, source_target_pairs={{1,0},{0,1},{3,2},{2,3},{5,4},{4,5},{7,6},{6,7},{9,8},{8,9},{11,10... | collective-permute-start | bytes 1572872 | tf_op jit(solution)/shard_map/ppermute | solution.py:513
  102.6 4.8 %collective-permute-start.16 = (f32[64,256]{1,0:T(8,128)S(1)}, f32[64,256]{1,0:T(8,128)S(1)}, u32[]{:S(2)}, u32[]{:S(2)}) collective-permute-start(f32[64,256]{1,0:T(8,128)S(1)} %far.1.refs_11_.refs_0_), channel_id=1, source_target_pairs={{3,0},{2,1},{1,2},{0,3},{7,4},{6,5},{5,6},{4,7},{11,8},{10,9},{9,1... | collective-permute-start | bytes 196616 | tf_op jit(solution)/shard_map/ppermute | solution.py:513
  104.9 4.4 %collective-permute-start.15 = (f32[64,256]{1,0:T(8,128)S(1)}, f32[64,256]{1,0:T(8,128)S(1)}, u32[]{:S(2)}, u32[]{:S(2)}) collective-permute-start(f32[64,256]{1,0:T(8,128)S(1)} %far.1.refs_11_.refs_0_), channel_id=1, source_target_pairs={{2,0},{3,1},{0,2},{1,3},{6,4},{7,5},{4,6},{5,7},{10,8},{11,9},{8,1... | collective-permute-start | bytes 196616 | tf_op jit(solution)/shard_map/ppermute | solution.py:513
  105.3 4.1 %collective-permute-start.14 = (f32[64,256]{1,0:T(8,128)S(1)}, f32[64,256]{1,0:T(8,128)S(1)}, u32[]{:S(2)}, u32[]{:S(2)}) collective-permute-start(f32[64,256]{1,0:T(8,128)S(1)} %far.1.refs_11_.refs_0_), channel_id=1, source_target_pairs={{1,0},{0,1},{3,2},{2,3},{5,4},{4,5},{7,6},{6,7},{9,8},{8,9},{11,10... | collective-permute-start | bytes 196616 | tf_op jit(solution)/shard_map/ppermute | solution.py:513
  (10 other events, 106.3 us)

commit v8 on v7

--- a/solution.py
+++ b/solution.py
@@ -21,6 +21,7 @@
 SCALE = math.sqrt(0.5 * LOG2E)
 BIAS = 0.0625 * F * LOG2E
 VMEM_LIMIT = 24 * 1024 * 1024
+VMEM_WHOLE = 64 * 1024 * 1024
 
 
 def dot(a, b):
@@ -296,7 +297,7 @@
             pltpu.VMEM((R, SK), F32),
             pltpu.SemaphoreType.DMA((3,)),
         ],
-        compiler_params=pltpu.CompilerParams(vmem_limit_bytes=VMEM_LIMIT),
+        compiler_params=pltpu.CompilerParams(vmem_limit_bytes=VMEM_WHOLE),
     )(pos, near_count, near_src, points, weights, interp)
 
 
@@ -338,6 +339,9 @@
         in_specs=[pl.BlockSpec(memory_space=pltpu.SMEM)] + [vmem] * (1 + len(msgs)),
         out_specs=[vmem] * 3,
         compiler_params=pltpu.CompilerParams(vmem_limit_bytes=VMEM_LIMIT),
+        cost_estimate=pl.CostEstimate(
+            flops=5_000_000_000, bytes_accessed=8_000_000, transcendentals=0
+        ),
     )(pos, index, *msgs)
     return payload, targets
 
@@ -534,28 +538,29 @@
     ]
     pts_z = lax.ppermute(pts_y, "leaf", across)
     w_z = [lax.ppermute(w_y[0], "leaf", across)]
-    w_y = list(together(*w_y))
-    w_z.append(lax.ppermute(w_y[1], "leaf", across))
-
-    got, w_y = together(got, w_y)
+
+    got, pts_z = together(got, pts_z)
     msgs = [sent[0]] + [got[order.index((-dx % xs, dc)) - 1] for dx, dc in order[1:]]
     payload, targets = skel_call(xs, pos, skel_group, msgs)
+    every = (0, 2 * helpers)
+    (own,) = near_call("near_own", pos, msgs, targets, every, [("own", (points,), [weights])], R)
+    own, w_y[1], payload, w_z[0] = together(own, w_y[1], payload, w_z[0])
+    w_z.append(lax.ppermute(w_y[1], "leaf", across))
     pieces = [payload]
     for mask in range(2, groups, 2):
         pieces.append(lax.ppermute(payload, "leaf", [(i, i ^ mask) for i in range(groups)]))
 
-    sources = [("own", (points,), [weights]), ("pair", (pts_y,), w_y)]
-    (near,) = near_call("near_own_pair", pos, msgs, targets, (0, 2 * helpers), sources, R)
+    (pair,) = near_call("near_pair", pos, msgs, targets, every, [("pair", (pts_y,), w_y)], R)
+    pieces, pair = together(pieces, pair)
+    alike = stack_call(pieces)
+    side = lax.ppermute(alike, "leaf", beside)
     z_side = source_call(pts_z)
-    sums, part = [], []
+    near = [own, pair]
+    sums, part = [], [alike]
     for c in range(2):
-        if c == 1:
-            pieces, w_z[1], part = together(pieces, w_z[1], part)
-            alike = stack_call(pieces)
-            side = lax.ppermute(alike, "leaf", beside)
         part = near_call(
             "near_next_away", pos, msgs, targets, (4, 2 * helpers),
-            [("next", z_side, w_z[c : c + 1])], rows, c * rows, [near], part[:1],
+            [("next", z_side, w_z[c : c + 1])], rows, c * rows, near, part[:1],
         )
         kept, given = part[::2], part[1::2]
         sums.append((kept, [from_help(value, 0, 1) for value in given]))
@@ -567,7 +572,7 @@
     v_own = far_call(groups, pos, far_nodes, skel_node, transfer, alike, side, both[:1])
     values = [v_own] + [from_help(v_own, dx, dc) for dx, dc in order[1:]]
     home = near_call(
-        "near_next_home", pos, msgs, targets, (0, 4), [("next", z_side, w_z)], R, 0, [near], [v_own]
+        "near_next_home", pos, msgs, targets, (0, 4), [("next", z_side, w_z)], R, 0, near, [v_own]
     )
     mate = [from_help(value, 0, 1) for value in home[2:]]
     mine = add_call(*[[home[c], *parts[c]] for c in range(2)])

time: 113 us -> 114 us (level)
  the two profiles are of different devices: /device:TPU:12 before, /device:TPU:4 now
where the time goes in v8:
time: 114 us; the launch traced here: 112 us
  waiting for transfers between devices  43.1 us (38%)
  Pallas kernels  40.9 us (36%)
  starting transfers between devices  22.8 us (20%)
  local copies, waits for them, and re-layouts  4.69 us (4%)
    pallas_call x5, Pallas kernels, near_call(): pl.pallas_call(partial(near_body, len(msgs) // 2, sets, leaves_at, rows,...  26.1 us
    ppermute x1, waiting for transfers between devices, shards(): side = lax.ppermute(alike, 'leaf', beside)  11 us
    ppermute x1, waiting for transfers between devices, shards(): pts_y = lax.ppermute(points, 'leaf', beside)  10.9 us
    ppermute x3, waiting for transfers between devices, shards(): lax.ppermute(payload, 'leaf', [(i, i ^ mask) for i in range(groups)])  10.9 us
    ppermute x3, starting transfers between devices, shards(): lax.ppermute(payload, 'leaf', [(i, i ^ mask) for i in range(groups)])  6.91 us
    pallas_call x1, Pallas kernels, far_call(): pl.pallas_call(partial(far_body, groups, rows), name='far', out_shape=jax...  6.51 us
    ppermute x1, waiting for transfers between devices, shards(): pts_z = lax.ppermute(pts_y, 'leaf', across)  5.78 us
    ppermute x7, waiting for transfers between devices, from_help(): return lax.ppermute(value, 'help', help_pairs(xs, dx, dc))  4.28 us
  transfers between devices with their start and end apart: 22, of which 9 were waited for; matrix products, arithmetic and copies ran while one was open for 1% of the time, Pallas kernels for 34%

profile of v8, /device:TPU:4, one launch (start us, length us, event | category | flops | bytes accessed | tf_op | source)
XLA Modules:
  0.0 112.4 jit_solution(16438307623484547641)
XLA Ops:
  0.0 2.3 %fusion = (f32[128,1024]{1,0:T(8,128)}, f32[128,1024]{1,0:T(8,128)}) fusion(f32[256,1024]{1,0:T(8,128)} %refs_7_.1), kind=kLoop, calls=%fused_computation.1 | loop fusion | bytes 2097152 | tf_op jit(solution)/shard_map/slice | solution.py:531
  2.3 2.0 %collective-permute-start.3 = (f32[64,1024]{1,0:T(8,128)}, f32[64,1024]{1,0:T(8,128)}, u32[]{:S(2)}, u32[]{:S(2)}) collective-permute-start(f32[64,1024]{1,0:T(8,128)} %refs_6_.1), channel_id=1, source_target_pairs={{0,4},{4,0},{8,12},{12,8},{16,20},{20,16},{24,28},{28,24},{1,5},{5... | collective-permute-start | bytes 786440 | tf_op jit(solution)/shard_map/ppermute | solution.py:530
  5.0 4.1 %leaf_up.1 = (f32[88,1024]{1,0:T(8,128)}, f32[88,1024]{1,0:T(8,128)}, f32[88,1024]{1,0:T(8,128)}, f32[88,1024]{1,0:T(8,128)}) custom-call(s32[4]{0:T(128)} %pad_add_fusion.pos_ref, s32[1,2]{1,0:T(1,128)} %count_ref.1, s32[2,32]{1,0:T(2,128)} %src_ref.1, f32[64,1024]{1,0:T(8,128)} %refs_6_.1, f32[256,1024]{1,0:T(8,128)} %refs_7_.1, f32[2,512,256]{2,1,0:T(8,128)} %interp_ref.1), custom_call_target="tpu_custom_call" | custom-call | tf_op jit(solution)/shard_map/leaf_up/pallas_call | solution.py:287
  9.1 1.6 %collective-permute-start.1 = (f32[88,1024]{1,0:T(8,128)}, f32[88,1024]{1,0:T(8,128)S(1)}, u32[]{:S(2)}, u32[]{:S(2)}) collective-permute-start(f32[88,1024]{1,0:T(8,128)} %get-tuple-element.39), channel_id=1, source_target_pairs={{2,0},{3,1},{0,2},{1,3},{6,4},{7,5},{4,6},{5,7},{10,8},{11,9},{8,1... | collective-permute-start | bytes 1081352 | tf_op jit(solution)/shard_map/ppermute | solution.py:535
  11.0 10.9 %collective-permute-done.3.refs_6_ = f32[64,1024]{1,0:T(8,128)} collective-permute-done((f32[64,1024]{1,0:T(8,128)}, f32[64,1024]{1,0:T(8,128)}, u32[]{:S(2)}, u32[]{:S(2)}) %collective-permute-start.3) | collective-permute-done | bytes 262176 | tf_op jit(solution)/shard_map/ppermute | solution.py:530
  23.2 2.8 %collective-permute-start.5 = (f32[128,1024]{1,0:T(8,128)}, f32[128,1024]{1,0:T(8,128)S(1)}, u32[]{:S(2)}, u32[]{:S(2)}) collective-permute-start(f32[128,1024]{1,0:T(8,128)} %get-tuple-element.70), channel_id=1, source_target_pairs={{0,4},{4,0},{8,12},{12,8},{16,20},{20,16},{24,28},{28,24},{1,5},{5... | collective-permute-start | bytes 1572872 | tf_op jit(solution)/shard_map/ppermute | solution.py:532
  26.0 1.3 %collective-permute-start.7 = (f32[128,1024]{1,0:T(8,128)}, f32[128,1024]{1,0:T(8,128)S(1)}, u32[]{:S(2)}, u32[]{:S(2)}) collective-permute-start(f32[128,1024]{1,0:T(8,128)} %collective-permute-done.6.refs_7_), channel_id=1, source_target_pairs={{0,8},{8,16},{16,24},{12,4},{20,12},{28,20},{1,9},{9,17},{17,25},{... | collective-permute-start | bytes 1572872 | tf_op jit(solution)/shard_map/ppermute | solution.py:540
  27.4 5.8 %collective-permute-done.4.pts_ref = f32[64,1024]{1,0:T(8,128)S(1)} collective-permute-done((f32[64,1024]{1,0:T(8,128)}, f32[64,1024]{1,0:T(8,128)S(1)}, u32[]{:S(2)}, u32[]{:S(2)}) %collective-permute-start.4) | collective-permute-done | bytes 262176 | tf_op jit(solution)/shard_map/ppermute | solution.py:539
  35.6 1.3 %skeleton.1 = (f32[128,256]{1,0:T(8,128)S(1)}, bf16[8,256,512]{2,1,0:T(8,128)(2,1)S(1)}, f32[8,8,512]{2,1,0:T(8,128)S(1)}) custom-call(s32[4]{0:T(128)S(1)} %copy-done.6, s32[1,256]{1,0:T(1,128)S(1)} %copy-done.10, f32[88,1024]{1,0:T(8,128)S(1)} %copy-done.1, f32[88,1024]{1,0:T(8,128)S(1)} %collective-permute-done.refs_1_, ...), custom_call_target="tpu_custom_call" | custom-call | flops 5000000000 | bytes 8000000 | tf_op jit(solution)/shard_map/skeleton/pallas_call | solution.py:331
  36.9 6.8 %near_own.1.refs_9_.refs_10_ = f32[8,256,512]{2,1,0:T(8,128)S(1)} custom-call(s32[4]{0:T(128)S(1)} %copy-done.6, f32[88,1024]{1,0:T(8,128)S(1)} %copy-done.2, f32[88,1024]{1,0:T(8,128)S(1)} %collective-permute-done.refs_1_, f32[88,1024]{1,0:T(8,128)S(1)} %collective-permute-done.1.refs_2_, f32[88,1024]{1,0:T(8,128)S(1)} %collective-permute-done.2.refs_3_, ...), custom_call_target="tpu_custom_call" | custom-call | tf_op jit(solution)/shard_map/near_own/pallas_call | solution.py:201
  43.8 1.3 %collective-permute-start.12 = (f32[128,1024]{1,0:T(8,128)S(1)}, f32[128,1024]{1,0:T(8,128)S(1)}, u32[]{:S(2)}, u32[]{:S(2)}) collective-permute-start(f32[128,1024]{1,0:T(8,128)S(1)} %collective-permute-done.5.refs_8_), channel_id=1, source_target_pairs={{0,8},{8,16},{16,24},{12,4},{20,12},{28,20},{1,9},{9,17},{17,25},{... | collective-permute-start | bytes 1572872 | tf_op jit(solution)/shard_map/ppermute | solution.py:548
  45.1 6.3 %collective-permute-start.10 = (f32[128,256]{1,0:T(8,128)S(1)}, f32[128,256]{1,0:T(8,128)S(1)}, u32[]{:S(2)}, u32[]{:S(2)}) collective-permute-start(f32[128,256]{1,0:T(8,128)S(1)} %get-tuple-element.49.refs_0_), channel_id=1, source_target_pairs={{0,24},{4,28},{8,16},{12,20},{16,8},{20,12},{24,0},{28,4},{1,25},{... | collective-permute-start | bytes 393224 | tf_op jit(solution)/shard_map/ppermute | solution.py:551
  52.5 6.4 %near_pair.1.refs_10_.refs_11_ = f32[8,256,512]{2,1,0:T(8,128)S(1)} custom-call(s32[4]{0:T(128)S(1)} %copy-done.6, f32[88,1024]{1,0:T(8,128)S(1)} %copy-done.2, f32[88,1024]{1,0:T(8,128)S(1)} %collective-permute-done.refs_1_, f32[88,1024]{1,0:T(8,128)S(1)} %collective-permute-done.1.refs_2_, f32[88,1024]{1,0:T(8,128)S(1)} %collective-permute-done.2.refs_3_, ...), custom_call_target="tpu_custom_call" | custom-call | tf_op jit(solution)/shard_map/near_pair/pallas_call | solution.py:201
  58.9 6.5 %collective-permute-done.10.refs_3_ = f32[128,256]{1,0:T(8,128)S(1)} collective-permute-done((f32[128,256]{1,0:T(8,128)S(1)}, f32[128,256]{1,0:T(8,128)S(1)}, u32[]{:S(2)}, u32[]{:S(2)}) %collective-permute-start.10) | collective-permute-done | bytes 131104 | tf_op jit(solution)/shard_map/ppermute | solution.py:551
  65.5 4.3 %collective-permute-done.9.refs_2_ = f32[128,256]{1,0:T(8,128)S(1)} collective-permute-done((f32[128,256]{1,0:T(8,128)S(1)}, f32[128,256]{1,0:T(8,128)S(1)}, u32[]{:S(2)}, u32[]{:S(2)}) %collective-permute-start.9) | collective-permute-done | bytes 131104 | tf_op jit(solution)/shard_map/ppermute | solution.py:551
  69.8 3.9 %near_next_away.2 = (f32[128,1024]{1,0:T(8,128)S(1)}, f32[128,1024]{1,0:T(8,128)S(1)}) custom-call(s32[4]{0:T(128)S(1)} %copy-done.6, f32[88,1024]{1,0:T(8,128)S(1)} %copy-done.2, f32[88,1024]{1,0:T(8,128)S(1)} %collective-permute-done.refs_1_, f32[88,1024]{1,0:T(8,128)S(1)} %collective-permute-done.1.refs_2_, ...), custom_call_target="tpu_custom_call" | custom-call | tf_op jit(solution)/shard_map/near_next_away/pallas_call | solution.py:201
  73.9 4.1 %near_next_away.3 = (f32[128,1024]{1,0:T(8,128)S(1)}, f32[128,1024]{1,0:T(8,128)S(1)}) custom-call(s32[4]{0:T(128)S(1)} %copy-done.6, f32[88,1024]{1,0:T(8,128)S(1)} %copy-done.2, f32[88,1024]{1,0:T(8,128)S(1)} %collective-permute-done.refs_1_, f32[88,1024]{1,0:T(8,128)S(1)} %collective-permute-done.1.refs_2_, ...), custom_call_target="tpu_custom_call" | custom-call | tf_op jit(solution)/shard_map/near_next_away/pallas_call | solution.py:201
  81.4 11.0 %collective-permute-done.11.beside_ref = f32[4,128,256]{2,1,0:T(8,128)S(1)} collective-permute-done((f32[4,128,256]{2,1,0:T(8,128)S(1)}, f32[4,128,256]{2,1,0:T(8,128)S(1)}, u32[]{:S(2)}, u32[]{:S(2)}) %collective-permute-start.11) | collective-permute-done | bytes 524320 | tf_op jit(solution)/shard_map/ppermute | solution.py:556
  92.5 6.5 %far.1.refs_12_.refs_0_ = f32[64,256]{1,0:T(8,128)S(1)} custom-call(s32[4]{0:T(128)S(1)} %copy-done.7, s32[4,14]{1,0:T(4,128)S(1)} %bitcast.4, s32[6,256]{1,0:T(8,128)S(1)} %copy-done.8, f32[6,512,256]{2,1,0:T(8,128)S(1)} %copy-done.4, f32[4,128,256]{2,1,0:T(8,128)S(1)} %stack.17.refs_11_.alike_ref, f32[4,128,256]{2,1,0:T(8,128)S(1)} %collective-permute-done.11.beside_ref, ...), custom_call_target="tpu_custom_call" | custom-call | tf_op jit(solution)/shard_map/far/pallas_call | solution.py:430
  99.0 4.8 %near_next_home.1 = (f32[128,1024]{1,0:T(8,128)S(1)}, f32[128,1024]{1,0:T(8,128)S(1)}, f32[128,1024]{1,0:T(8,128)S(1)}, f32[128,1024]{1,0:T(8,128)S(1)}) custom-call(s32[4]{0:T(128)S(1)} %copy-done.7, f32[88,1024]{1,0:T(8,128)S(1)} %copy-done.2, f32[88,1024]{1,0:T(8,128)S(1)} %collective-permute-done.refs_1_, f32[88,1024]{1,0:T(8,128)S(1)} %collective-permute-done.1.refs_2_, ...), custom_call_target="tpu_custom_call" | custom-call | tf_op jit(solution)/shard_map/near_next_home/pallas_call | solution.py:201
  104.4 1.3 %collective-permute-start.16 = (f32[64,256]{1,0:T(8,128)S(1)}, f32[64,256]{1,0:T(8,128)S(1)}, u32[]{:S(2)}, u32[]{:S(2)}) collective-permute-start(f32[64,256]{1,0:T(8,128)S(1)} %far.1.refs_12_.refs_0_), channel_id=1, source_target_pairs={{3,0},{2,1},{1,2},{0,3},{7,4},{6,5},{5,6},{4,7},{11,8},{10,9},{9,1... | collective-permute-start | bytes 196616 | tf_op jit(solution)/shard_map/ppermute | solution.py:517
  106.4 2.1 %collective-permute-done.16.refs_3_ = f32[64,256]{1,0:T(8,128)S(1)} collective-permute-done((f32[64,256]{1,0:T(8,128)S(1)}, f32[64,256]{1,0:T(8,128)S(1)}, u32[]{:S(2)}, u32[]{:S(2)}) %collective-permute-start.16) | collective-permute-done | bytes 65568 | tf_op jit(solution)/shard_map/ppermute | solution.py:517
  108.6 1.7 %collective-permute-done.15.refs_2_ = f32[64,256]{1,0:T(8,128)S(1)} collective-permute-done((f32[64,256]{1,0:T(8,128)S(1)}, f32[64,256]{1,0:T(8,128)S(1)}, u32[]{:S(2)}, u32[]{:S(2)}) %collective-permute-start.15) | collective-permute-done | bytes 65568 | tf_op jit(solution)/shard_map/ppermute | solution.py:517
  110.3 2.2 %join.1 = f32[256,1024]{1,0:T(8,128)} custom-call(s32[4]{0:T(128)S(1)} %copy-done.7, f32[2,512,256]{2,1,0:T(8,128)S(1)} %copy-done.3, f32[64,256]{1,0:T(8,128)S(1)} %far.1.refs_12_.refs_0_, f32[64,256]{1,0:T(8,128)S(1)} %collective-permute-done.14.refs_1_, f32[64,256]{1,0:T(8,128)S(1)} %collective-permute-done.15.refs_2_, ...), custom_call_target="tpu_custom_call" | custom-call | tf_op jit(solution)/shard_map/join/pallas_call | solution.py:486
  (58 shorter events, 10.8 us)
Async XLA Ops:
  2.3 23.7 %collective-permute-start.6 = (f32[128,1024]{1,0:T(8,128)}, f32[128,1024]{1,0:T(8,128)}, u32[]{:S(2)}, u32[]{:S(2)}) collective-permute-start(f32[128,1024]{1,0:T(8,128)} %get-tuple-element.69), channel_id=1, source_target_pairs={{0,4},{4,0},{8,12},{12,8},{16,20},{20,16},{24,28},{28,24},{1,5},{5... | collective-permute-start | bytes 1572872 | tf_op jit(solution)/shard_map/ppermute | solution.py:532
  2.3 19.6 %collective-permute-start.3 = (f32[64,1024]{1,0:T(8,128)}, f32[64,1024]{1,0:T(8,128)}, u32[]{:S(2)}, u32[]{:S(2)}) collective-permute-start(f32[64,1024]{1,0:T(8,128)} %refs_6_.1), channel_id=1, source_target_pairs={{0,4},{4,0},{8,12},{12,8},{16,20},{20,16},{24,28},{28,24},{1,5},{5... | collective-permute-start | bytes 786440 | tf_op jit(solution)/shard_map/ppermute | solution.py:530
  9.1 14.1 %collective-permute-start = (f32[88,1024]{1,0:T(8,128)}, f32[88,1024]{1,0:T(8,128)S(1)}, u32[]{:S(2)}, u32[]{:S(2)}) collective-permute-start(f32[88,1024]{1,0:T(8,128)} %get-tuple-element.38), channel_id=1, source_target_pairs={{1,0},{0,1},{3,2},{2,3},{5,4},{4,5},{7,6},{6,7},{9,8},{8,9},{11,10... | collective-permute-start | bytes 1081352 | tf_op jit(solution)/shard_map/ppermute | solution.py:535
  9.1 18.1 %collective-permute-start.1 = (f32[88,1024]{1,0:T(8,128)}, f32[88,1024]{1,0:T(8,128)S(1)}, u32[]{:S(2)}, u32[]{:S(2)}) collective-permute-start(f32[88,1024]{1,0:T(8,128)} %get-tuple-element.39), channel_id=1, source_target_pairs={{2,0},{3,1},{0,2},{1,3},{6,4},{7,5},{4,6},{5,7},{10,8},{11,9},{8,1... | collective-permute-start | bytes 1081352 | tf_op jit(solution)/shard_map/ppermute | solution.py:535
  10.7 16.8 %collective-permute-start.2 = (f32[88,1024]{1,0:T(8,128)}, f32[88,1024]{1,0:T(8,128)S(1)}, u32[]{:S(2)}, u32[]{:S(2)}) collective-permute-start(f32[88,1024]{1,0:T(8,128)} %get-tuple-element.40), channel_id=1, source_target_pairs={{3,0},{2,1},{1,2},{0,3},{7,4},{6,5},{5,6},{4,7},{11,8},{10,9},{9,1... | collective-permute-start | bytes 1081352 | tf_op jit(solution)/shard_map/ppermute | solution.py:535
  21.9 11.3 %collective-permute-start.4 = (f32[64,1024]{1,0:T(8,128)}, f32[64,1024]{1,0:T(8,128)S(1)}, u32[]{:S(2)}, u32[]{:S(2)}) collective-permute-start(f32[64,1024]{1,0:T(8,128)} %collective-permute-done.3.refs_6_), channel_id=1, source_target_pairs={{0,8},{8,16},{16,24},{12,4},{20,12},{28,20},{1,9},{9,17},{17,25},{... | collective-permute-start | bytes 786440 | tf_op jit(solution)/shard_map/ppermute | solution.py:539
  23.2 20.6 %collective-permute-start.5 = (f32[128,1024]{1,0:T(8,128)}, f32[128,1024]{1,0:T(8,128)S(1)}, u32[]{:S(2)}, u32[]{:S(2)}) collective-permute-start(f32[128,1024]{1,0:T(8,128)} %get-tuple-element.70), channel_id=1, source_target_pairs={{0,4},{4,0},{8,12},{12,8},{16,20},{20,16},{24,28},{28,24},{1,5},{5... | collective-permute-start | bytes 1572872 | tf_op jit(solution)/shard_map/ppermute | solution.py:532
  26.0 17.8 %collective-permute-start.7 = (f32[128,1024]{1,0:T(8,128)}, f32[128,1024]{1,0:T(8,128)S(1)}, u32[]{:S(2)}, u32[]{:S(2)}) collective-permute-start(f32[128,1024]{1,0:T(8,128)} %collective-permute-done.6.refs_7_), channel_id=1, source_target_pairs={{0,8},{8,16},{16,24},{12,4},{20,12},{28,20},{1,9},{9,17},{17,25},{... | collective-permute-start | bytes 1572872 | tf_op jit(solution)/shard_map/ppermute | solution.py:540
  43.8 30.1 %collective-permute-start.12 = (f32[128,1024]{1,0:T(8,128)S(1)}, f32[128,1024]{1,0:T(8,128)S(1)}, u32[]{:S(2)}, u32[]{:S(2)}) collective-permute-start(f32[128,1024]{1,0:T(8,128)S(1)} %collective-permute-done.5.refs_8_), channel_id=1, source_target_pairs={{0,8},{8,16},{16,24},{12,4},{20,12},{28,20},{1,9},{9,17},{17,25},{... | collective-permute-start | bytes 1572872 | tf_op jit(solution)/shard_map/ppermute | solution.py:548
  45.1 20.4 %collective-permute-start.10 = (f32[128,256]{1,0:T(8,128)S(1)}, f32[128,256]{1,0:T(8,128)S(1)}, u32[]{:S(2)}, u32[]{:S(2)}) collective-permute-start(f32[128,256]{1,0:T(8,128)S(1)} %get-tuple-element.49.refs_0_), channel_id=1, source_target_pairs={{0,24},{4,28},{8,16},{12,20},{16,8},{20,12},{24,0},{28,4},{1,25},{... | collective-permute-start | bytes 393224 | tf_op jit(solution)/shard_map/ppermute | solution.py:551
  51.3 18.5 %collective-permute-start.9 = (f32[128,256]{1,0:T(8,128)S(1)}, f32[128,256]{1,0:T(8,128)S(1)}, u32[]{:S(2)}, u32[]{:S(2)}) collective-permute-start(f32[128,256]{1,0:T(8,128)S(1)} %get-tuple-element.49.refs_0_), channel_id=1, source_target_pairs={{0,16},{4,20},{8,24},{12,28},{16,0},{20,4},{24,8},{28,12},{1,17},{... | collective-permute-start | bytes 393224 | tf_op jit(solution)/shard_map/ppermute | solution.py:551
  51.3 18.5 %collective-permute-start.8 = (f32[128,256]{1,0:T(8,128)S(1)}, f32[128,256]{1,0:T(8,128)S(1)}, u32[]{:S(2)}, u32[]{:S(2)}) collective-permute-start(f32[128,256]{1,0:T(8,128)S(1)} %get-tuple-element.49.refs_0_), channel_id=1, source_target_pairs={{0,8},{4,12},{8,0},{12,4},{16,24},{20,28},{24,16},{28,20},{1,9},{5... | collective-permute-start | bytes 393224 | tf_op jit(solution)/shard_map/ppermute | solution.py:551
  73.8 4.8 %collective-permute-start.17 = (f32[128,1024]{1,0:T(8,128)S(1)}, f32[128,1024]{1,0:T(8,128)S(1)}, u32[]{:S(2)}, u32[]{:S(2)}) collective-permute-start(f32[128,1024]{1,0:T(8,128)S(1)} %get-tuple-element.63), channel_id=1, source_target_pairs={{1,0},{0,1},{3,2},{2,3},{5,4},{4,5},{7,6},{6,7},{9,8},{8,9},{11,10... | collective-permute-start | bytes 1572872 | tf_op jit(solution)/shard_map/ppermute | solution.py:517
  73.9 18.6 %copy-start.7 = (s32[4]{0:T(128)S(1)}, s32[4]{0:T(128)}, u32[]{:S(2)}) copy-start(s32[4]{0:T(128)} %pad_add_fusion.pos_ref) | copy-start | bytes 52
  73.9 18.6 %copy-start.8 = (s32[6,256]{1,0:T(8,128)S(1)}, s32[6,256]{1,0:T(8,128)}, u32[]{:S(2)}) copy-start(s32[6,256]{1,0:T(8,128)} %node_ref.1) | copy-start | bytes 18436
  78.0 2.1 %collective-permute-start.13 = (f32[128,1024]{1,0:T(8,128)S(1)}, f32[128,1024]{1,0:T(8,128)S(1)}, u32[]{:S(2)}, u32[]{:S(2)}) collective-permute-start(f32[128,1024]{1,0:T(8,128)S(1)} %get-tuple-element.61), channel_id=1, source_target_pairs={{1,0},{0,1},{3,2},{2,3},{5,4},{4,5},{7,6},{6,7},{9,8},{8,9},{11,10... | collective-permute-start | bytes 1572872 | tf_op jit(solution)/shard_map/ppermute | solution.py:517
  78.6 13.9 %collective-permute-start.11 = (f32[4,128,256]{2,1,0:T(8,128)S(1)}, f32[4,128,256]{2,1,0:T(8,128)S(1)}, u32[]{:S(2)}, u32[]{:S(2)}) collective-permute-start(f32[4,128,256]{2,1,0:T(8,128)S(1)} %stack.17.refs_11_.alike_ref), channel_id=1, source_target_pairs={{0,4},{4,0},{8,12},{12,8},{16,20},{20,16},{24,28},{28,24},{1,5},{5... | collective-permute-start | bytes 1572872 | tf_op jit(solution)/shard_map/ppermute | solution.py:556
  78.6 27.1 %collective-permute-start.18 = (f32[128,1024]{1,0:T(8,128)S(1)}, f32[128,1024]{1,0:T(8,128)S(1)}, u32[]{:S(2)}, u32[]{:S(2)}) collective-permute-start(f32[128,1024]{1,0:T(8,128)S(1)} %add_parts.4), channel_id=1, source_target_pairs={{2,0},{3,1},{0,2},{1,3},{6,4},{7,5},{4,6},{5,7},{10,8},{11,9},{8,1... | collective-permute-start | bytes 1572872 | tf_op jit(solution)/shard_map/ppermute | solution.py:520
  80.2 26.0 %collective-permute-start.19 = (f32[128,1024]{1,0:T(8,128)S(1)}, f32[128,1024]{1,0:T(8,128)S(1)}, u32[]{:S(2)}, u32[]{:S(2)}) collective-permute-start(f32[128,1024]{1,0:T(8,128)S(1)} %add_parts.3.refs_0_), channel_id=1, source_target_pairs={{2,0},{3,1},{0,2},{1,3},{6,4},{7,5},{4,6},{5,7},{10,8},{11,9},{8,1... | collective-permute-start | bytes 1572872 | tf_op jit(solution)/shard_map/ppermute | solution.py:520
  103.9 6.4 %collective-permute-start.20 = (f32[128,1024]{1,0:T(8,128)S(1)}, f32[128,1024]{1,0:T(8,128)S(1)}, u32[]{:S(2)}, u32[]{:S(2)}) collective-permute-start(f32[128,1024]{1,0:T(8,128)S(1)} %get-tuple-element.67), channel_id=1, source_target_pairs={{1,0},{0,1},{3,2},{2,3},{5,4},{4,5},{7,6},{6,7},{9,8},{8,9},{11,10... | collective-permute-start | bytes 1572872 | tf_op jit(solution)/shard_map/ppermute | solution.py:517
  103.9 6.3 %collective-permute-start.21 = (f32[128,1024]{1,0:T(8,128)S(1)}, f32[128,1024]{1,0:T(8,128)S(1)}, u32[]{:S(2)}, u32[]{:S(2)}) collective-permute-start(f32[128,1024]{1,0:T(8,128)S(1)} %get-tuple-element.68), channel_id=1, source_target_pairs={{1,0},{0,1},{3,2},{2,3},{5,4},{4,5},{7,6},{6,7},{9,8},{8,9},{11,10... | collective-permute-start | bytes 1572872 | tf_op jit(solution)/shard_map/ppermute | solution.py:517
  104.4 4.1 %collective-permute-start.16 = (f32[64,256]{1,0:T(8,128)S(1)}, f32[64,256]{1,0:T(8,128)S(1)}, u32[]{:S(2)}, u32[]{:S(2)}) collective-permute-start(f32[64,256]{1,0:T(8,128)S(1)} %far.1.refs_12_.refs_0_), channel_id=1, source_target_pairs={{3,0},{2,1},{1,2},{0,3},{7,4},{6,5},{5,6},{4,7},{11,8},{10,9},{9,1... | collective-permute-start | bytes 196616 | tf_op jit(solution)/shard_map/ppermute | solution.py:517
  105.8 4.5 %collective-permute-start.15 = (f32[64,256]{1,0:T(8,128)S(1)}, f32[64,256]{1,0:T(8,128)S(1)}, u32[]{:S(2)}, u32[]{:S(2)}) collective-permute-start(f32[64,256]{1,0:T(8,128)S(1)} %far.1.refs_12_.refs_0_), channel_id=1, source_target_pairs={{2,0},{3,1},{0,2},{1,3},{6,4},{7,5},{4,6},{5,7},{10,8},{11,9},{8,1... | collective-permute-start | bytes 196616 | tf_op jit(solution)/shard_map/ppermute | solution.py:517
  106.2 4.1 %collective-permute-start.14 = (f32[64,256]{1,0:T(8,128)S(1)}, f32[64,256]{1,0:T(8,128)S(1)}, u32[]{:S(2)}, u32[]{:S(2)}) collective-permute-start(f32[64,256]{1,0:T(8,128)S(1)} %far.1.refs_12_.refs_0_), channel_id=1, source_target_pairs={{1,0},{0,1},{3,2},{2,3},{5,4},{4,5},{7,6},{6,7},{9,8},{8,9},{11,10... | collective-permute-start | bytes 196616 | tf_op jit(solution)/shard_map/ppermute | solution.py:517
  (9 other events, 50.6 us)
